TPU v7x, 32 devices: a whole 2x2x4 slice. The times are simulated.
32 devices in a mesh: leaf: 32 (over z, y, x, core).
Axes of the slice: x: 2, y: 2, z: 4, core: 2. Of those that a mesh axis runs over, the one named last changes fastest.
Arguments:
- weights: float32 [131072, 128], P('leaf'), may hold values from -6 to 6
- labels: int32 [131072], P('leaf'), may hold values from 0 to 127
- basis: bfloat16 [512, 64, 256], P('leaf'), may hold values from -0.375 to 0.375
- near_tiles: bfloat16 [512, 3, 256, 256], P('leaf'), may hold values from -0.21875 to 0.21875
- near_ids: int32 [512, 2], P('leaf'), may hold values from 0 to 511, as said below
- transfer: bfloat16 [992, 64, 64], P('leaf'), may hold values from -0.5 to 0.5
- couplings: bfloat16 [992, 64, 256], P('leaf'), may hold values from -0.375 to 0.375
- sources: int32 [992, 4], P('leaf'), may hold values from 0 to 511, as said below
- coarse_transfer: bfloat16 [28, 64, 64], replicated, may hold values from -0.5 to 0.5
- coarse_couplings: bfloat16 [30, 64, 256], replicated, may hold values from -0.375 to 0.375
- coarse_sources: int32 [30, 4], replicated, may hold values from 0 to 15, as said below
Outputs:
- updated: float32 [131072, 128], P('leaf')
- second_scores: float32 [131072, 128], P('leaf')
Inputs may be any that keep to these rules, and one draw needn't show every extreme that they name: `sources`: rows of device q's block name nodes of their row's level, numbered over all devices; the rows of one device name at most 4 nodes held by any single device (counted over all its rows), and some pair of devices reaches 4. `coarse_sources`: entries of a row name a node of that row's coarse level. `near_ids`: each entry lies within 2 leaves of its own leaf and differs from it; distance 2 occurs.
All inputs are finite; a program needn't handle non-finite values.
Results may differ from a plain program's by a relative error of at most 0.025.
Values may be sent and summed in bfloat16 or wider, within the bound.
No kernel may reach another device: no remote copies, remote signals or barrier semaphores. Data moves between devices by JAX's collectives and lax.ppermute only.
A program may use at most 128 MiB of HBM per device.

v0:
```python
import jax
import jax.numpy as jnp
import numpy as np
from jax import lax
from jax.sharding import PartitionSpec as P

REACH = 2


step_size = 0.5


def with_halo(value, sides, width):
    for axis, dim in sides:
        size, length = (lax.axis_size(axis), value.shape[dim])
        up = [(i, (i + 1) % size) for i in range(size - 1)]
        down = [(j, i) for i, j in up]
        last = lax.slice_in_dim(value, length - width, length, axis=dim)
        first = lax.slice_in_dim(value, 0, width, axis=dim)
        before = lax.ppermute(last, axis, up)
        after = lax.ppermute(first, axis, down)
        value = jnp.concatenate([before, value, after], axis=dim)
    return value


def plan_blocks(
    all_lists, own_lists, lo_row, hi_row, row_height, counts, starts, me_index, capacity
):
    link_count = own_lists.shape[1]
    width = (hi_row - lo_row) * link_count
    heights_here = np.repeat(row_height[lo_row:hi_row], link_count)
    count_here = jnp.asarray(np.array([counts[value] for value in heights_here]), dtype=jnp.int32)
    start_here = jnp.asarray(np.array([starts[value] for value in heights_here]), dtype=jnp.int32)
    wanted = all_lists.reshape(all_lists.shape[0], width)
    owner_dev = wanted // count_here
    local_row = start_here + wanted % count_here
    is_mine = owner_dev == me_index
    rank_in = jnp.cumsum(is_mine.astype(jnp.int32), axis=1) - 1
    picked = is_mine[:, None, :] & (
        rank_in[:, None, :] == jnp.arange(capacity, dtype=jnp.int32)[None, :, None]
    )
    chosen = jnp.sum(jnp.where(picked, local_row[:, None, :], 0), axis=2)
    own_list = own_lists.reshape(width)
    own_owner = own_list // count_here
    earlier = jnp.asarray(np.tril(np.ones((width, width), dtype=bool), -1))
    before = jnp.sum(
        ((own_owner[:, None] == own_owner[None, :]) & earlier).astype(jnp.int32), axis=1
    )
    landing = own_owner * capacity + before
    return (chosen, landing)


def apply_blocks(incoming, landing, couplings, lo_row, hi_row):
    rank_dim = incoming.shape[2]
    classes = incoming.shape[3]
    blocks = incoming.reshape(-1, rank_dim, classes)[landing]
    row_count = hi_row - lo_row
    blocks = blocks.reshape(row_count, -1, classes)
    return jnp.einsum("tab,tbn->tan", couplings, blocks, preferred_element_type=jnp.float32)


def upward(children, mats):
    half = children.shape[0] // 2
    joined = mats.reshape(half, 2, mats.shape[1], mats.shape[2])
    kids = children.reshape(half, 2, children.shape[1], children.shape[2])
    return jnp.einsum("jkcp,jkcn->jpn", joined, kids, preferred_element_type=jnp.float32).astype(
        jnp.bfloat16
    )


def downward(coupled, mats, parent_field):
    half = parent_field.shape[0]
    joined = mats.reshape(half, 2, mats.shape[1], mats.shape[2])
    pushed = jnp.einsum("jkcp,jpn->jkcn", joined, parent_field, preferred_element_type=jnp.float32)
    return (coupled + pushed.reshape(coupled.shape)).astype(jnp.bfloat16)


def local(
    weights,
    labels,
    basis,
    near_tiles,
    near_ids,
    transfer,
    couplings,
    sources,
    coarse_transfer,
    coarse_couplings,
    coarse_sources,
):
    devices = lax.axis_size("leaf")
    me_index = lax.axis_index("leaf")
    per_dev = basis.shape[0]
    rank_dim = basis.shape[1]
    leaf_size = basis.shape[2]
    classes = weights.shape[1]
    node_count = transfer.shape[0]
    link_count = sources.shape[1]
    levels_dev = per_dev.bit_length()
    counts = [per_dev >> height for height in range(levels_dev)]
    starts = [sum(counts[:height]) for height in range(levels_dev)]
    row_height = np.concatenate([np.full(counts[height], height) for height in range(levels_dev)])
    capacity = node_count * link_count // devices + 1
    coarse_levels = devices.bit_length() - 2
    all_lists = lax.all_gather(sources, "leaf", axis=0, tiled=True).reshape(
        devices, node_count, link_count
    )
    layout_all = plan_blocks(
        all_lists, sources, 0, node_count, row_height, counts, starts, me_index, capacity
    )

    def operate(point_vals):
        point_rows = point_vals.reshape(per_dev, leaf_size, classes)
        padded = with_halo(point_vals, (("leaf", 0),), REACH * leaf_size)
        padded = padded.reshape(per_dev + 2 * REACH, leaf_size, classes)
        offset_ids = near_ids - (me_index * per_dev - REACH)
        neighbours = [point_rows, padded[offset_ids[:, 0]], padded[offset_ids[:, 1]]]
        leaf_coef = jnp.einsum(
            "trp,tpn->trn", basis, point_rows, preferred_element_type=jnp.float32
        ).astype(jnp.bfloat16)
        coefs = [leaf_coef]
        for height in range(levels_dev - 1):
            coefs.append(
                upward(coefs[-1], transfer[starts[height] : starts[height] + counts[height]])
            )
        stacked = jnp.concatenate(coefs, axis=0)
        top_coef, top_map = (
            lax.all_gather(coefs[-1], "leaf", axis=0, tiled=True),
            lax.all_gather(transfer[node_count - 1 : node_count], "leaf", axis=0, tiled=True),
        )
        chosen, landing = layout_all
        incoming = lax.all_to_all(stacked[chosen], "leaf", split_axis=0, concat_axis=0, tiled=True)
        coupled = apply_blocks(incoming, landing, couplings, 0, node_count)
        coarse = [top_coef, upward(top_coef, top_map)]
        for height in range(1, coarse_levels):
            offset = devices - (devices >> height - 1)
            level_count = devices >> height
            coarse.append(upward(coarse[-1], coarse_transfer[offset : offset + level_count]))
        parent_field = None
        for height in range(coarse_levels, 0, -1):
            offset = devices - (devices >> height - 1)
            ancestor = offset + (me_index >> height)
            blocks = coarse[height][coarse_sources[ancestor]].reshape(
                link_count * rank_dim, classes
            )
            term = jnp.dot(coarse_couplings[ancestor], blocks, preferred_element_type=jnp.float32)
            if height == coarse_levels:
                parent_field = term.astype(jnp.bfloat16)
            else:
                pushed = jnp.dot(
                    coarse_transfer[ancestor], parent_field, preferred_element_type=jnp.float32
                )
                parent_field = (term + pushed).astype(jnp.bfloat16)
        top_push = jnp.dot(
            transfer[node_count - 1], parent_field, preferred_element_type=jnp.float32
        )
        node_field = (coupled[node_count - 1 :] + top_push[None]).astype(jnp.bfloat16)
        for height in range(levels_dev - 2, -1, -1):
            lo_row = starts[height]
            node_field = downward(
                coupled[lo_row : lo_row + counts[height]],
                transfer[lo_row : lo_row + counts[height]],
                node_field,
            )
        near_term = jnp.einsum(
            "trp,trn->tpn", basis, node_field, preferred_element_type=jnp.float32
        )
        for member in range(3):
            near_term = near_term + jnp.einsum(
                "tpq,tqn->tpn",
                near_tiles[:, member],
                neighbours[member],
                preferred_element_type=jnp.float32,
            )
        return near_term.reshape(per_dev * leaf_size, classes)

    onehot = (labels[:, None] == jnp.arange(classes, dtype=jnp.int32)[None, :]).astype(jnp.float32)
    first_scores = operate(weights.astype(jnp.bfloat16))
    middle = weights - step_size * (jax.nn.sigmoid(first_scores) - onehot)
    second_scores = operate(middle.astype(jnp.bfloat16))
    updated = middle - step_size * (jax.nn.sigmoid(second_scores) - onehot)
    return (updated, second_scores)


def solution(mesh):
    in_specs = (
        P("leaf", None),
        P("leaf"),
        P("leaf", None, None),
        P("leaf", None, None, None),
        P("leaf", None),
        P("leaf", None, None),
        P("leaf", None, None),
        P("leaf", None),
        P(),
        P(),
        P(),
    )
    out_specs = (P("leaf", None), P("leaf", None))
    return jax.shard_map(local, mesh=mesh, in_specs=in_specs, out_specs=out_specs, check_vma=False)
```

profile of v0, /device:TPU:16, one launch (start us, length us, event | category | flops | bytes accessed | tf_op | source)
XLA Modules:
  0.0 349.9 jit_solution(18122558438947607743)
XLA Ops:
  4.3 1.7 convert_element_type.184
  6.0 31.6 %all-gather.2 = s32[32,31,4]{1,2,0:T(4,128)S(1)} all-gather(s32[1,31,4]{1,2,0:T(4,128)S(1)} %bitcast.551), channel_id=1, replica_groups=mesh['leaf'=32] {'leaf'}, dimensions={0}, use_global_device_ids=true | all-gather | bytes 16368 | tf_op jit(solution)/shard_map/all_gather | solution.py:105
  41.7 2.2 gather_fusion
  43.9 14.0 %all-to-all-start = ((bf16[32,4,64,128]{3,2,1,0:T(8,128)(2,1)}), bf16[32,4,64,128]{3,2,1,0:T(8,128)(2,1)}, u32[]{:S(2)}, u32[]{:S(2)}) async-start(bf16[32,4,64,128]{3,2,1,0:T(8,128)(2,1)} %bitcast.496), calls=%async_computation | async-start | bytes 4194304 | tf_op jit(solution)/shard_map/all_to_all | solution.py:132
  58.6 2.0 collective-permute-start
  60.7 5.3 %collective-permute-start.1 = (bf16[512,128]{1,0:T(8,128)(2,1)}, bf16[512,128]{1,0:T(8,128)(2,1)}, u32[]{:S(2)}, u32[]{:S(2)}) collective-permute-start(bf16[512,128]{1,0:T(8,128)(2,1)} %get-tuple-element.11), channel_id=1, source_target_pairs={{1,0},{2,1},{3,2},{4,3},{5,4},{6,5},{7,6},{8,7},{9,8},{10,9},{11,1... | collective-permute-start | bytes 393224 | tf_op jit(solution)/shard_map/ppermute | solution.py:21
  69.4 64.7 %all-gather = bf16[2048,128]{1,0:T(8,128)(2,1)S(1)} all-gather(bf16[64,128]{1,0:T(8,128)(2,1)S(1)} %bitcast.549), channel_id=2, replica_groups=mesh['leaf'=32] {'leaf'}, dimensions={0}, use_global_device_ids=true | all-gather | bytes 540672 | tf_op jit(solution)/shard_map/all_gather | solution.py:128
  134.1 31.0 %all_gather.15 = bf16[32,64,64]{2,1,0:T(8,128)(2,1)S(1)} all-gather(bf16[1,64,64]{2,1,0:T(8,128)(2,1)S(1)} %slice-done), channel_id=1, replica_groups=mesh['leaf'=32] {'leaf'}, dimensions={0}, use_global_device_ids=true | all-gather | bytes 270336 | tf_op jit(solution)/shard_map/all_gather | solution.py:129
  170.6 1.5 gather_fusion.2
  176.9 1.5 fusion.102
  178.4 3.7 %fusion.14 = f32[16,256,128]{1,2,0:T(8,128)} fusion(bf16[16,256,128]{2,1,0:T(8,128)(2,1)S(1)} %bitcast.489, bf16[16,3,256,256]{3,2,1,0:T(8,128)(2,1)} %param.17), kind=kOutput, calls=%fused_computation.32 | convolution fusion | flops 268435456 | bytes 5242880 | tf_op jit(solution)/shard_map/tpq,tqn->tpn/dot_general | solution.py:169
  184.0 1.7 gather_fusion.7
  185.7 3.7 %fusion.10 = f32[16,128,256]{2,1,0:T(8,128)} fusion(bf16[16,256,128]{2,1,0:T(8,128)(2,1)S(1)} %gather_fusion.6, bf16[16,3,256,256]{3,2,1,0:T(8,128)(2,1)} %param.17), kind=kOutput, calls=%fused_computation.28 | convolution fusion | flops 268435456 | bytes 5242880 | tf_op jit(solution)/shard_map/tpq,tqn->tpn/dot_general | solution.py:169
  189.4 3.7 %gather_fusion.1 = bf16[124,64,128]{2,1,0:T(8,128)(2,1)} fusion(bf16[128,64,128]{2,1,0:T(8,128)(2,1)} %bitcast.22, s32[1024]{0:T(1024)S(1)} %pad_clamp_fusion.6), kind=kCustom, calls=%fused_computation.1 | custom fusion | bytes 4063728 | tf_op jit(solution)/shard_map/gather | solution.py:56
  193.2 2.1 convolution_bitcast_fusion.1
  200.2 3.8 %fusion.19 = f32[16,256,128]{1,2,0:T(8,128)} fusion(f32[16,128,256]{2,1,0:T(8,128)S(1)} %copy-done.15, f32[16,256,128]{1,2,0:T(8,128)S(1)} %copy-done.14, f32[16,128,256]{2,1,0:T(8,128)S(1)} %fusion.172, bf16[16,256,128]{2,1,0:T(8,128)(2,1)S(1)} %copy-done.22, bf16[16,3,256,256]{3,2,1,0:T(8,128)(2,1)} %param.17), kind=kOutput, calls=%fused_computation.38 | convolution fusion | flops 271581184 | bytes 11534336 | tf_op jit(solution)/shard_map/tpq,tqn->tpn/dot_general | solution.py:169
  204.0 2.9 copy.130
  206.9 2.5 fusion.87
  210.7 2.1 gather_fusion.8
  212.9 9.5 %all-to-all-start.1 = ((bf16[32,4,64,128]{3,2,1,0:T(8,128)(2,1)}), bf16[32,4,64,128]{3,2,1,0:T(8,128)(2,1)}, u32[]{:S(2)}, u32[]{:S(2)}) async-start(bf16[32,4,64,128]{3,2,1,0:T(8,128)(2,1)} %bitcast.497), calls=%async_computation.1 | async-start | bytes 4194304 | tf_op jit(solution)/shard_map/all_to_all | solution.py:132
  222.4 74.7 %all-gather.1 = bf16[2048,128]{1,0:T(8,128)(2,1)S(1)} all-gather(bf16[64,128]{1,0:T(8,128)(2,1)S(1)} %bitcast.550), channel_id=3, replica_groups=mesh['leaf'=32] {'leaf'}, dimensions={0}, use_global_device_ids=true | all-gather | bytes 540672 | tf_op jit(solution)/shard_map/all_gather | solution.py:128
  300.6 1.6 gather_fusion.10
  302.3 2.3 collective-permute-start.2
  304.6 5.1 %collective-permute-start.3 = (bf16[512,128]{1,0:T(8,128)(2,1)S(1)}, bf16[512,128]{1,0:T(8,128)(2,1)}, u32[]{:S(2)}, u32[]{:S(2)}) collective-permute-start(bf16[512,128]{1,0:T(8,128)(2,1)S(1)} %get-tuple-element.9), channel_id=1, source_target_pairs={{1,0},{2,1},{3,2},{4,3},{5,4},{6,5},{7,6},{8,7},{9,8},{10,9},{11,1... | collective-permute-start | bytes 393224 | tf_op jit(solution)/shard_map/ppermute | solution.py:21
  313.4 3.8 %fusion.12 = f32[16,128,256]{2,1,0:T(8,128)} fusion(bf16[16,256,128]{2,1,0:T(8,128)(2,1)S(1)} %bitcast.491, bf16[16,3,256,256]{3,2,1,0:T(8,128)(2,1)} %param.17), kind=kOutput, calls=%fused_computation.30 | convolution fusion | flops 268435456 | bytes 5242880 | tf_op jit(solution)/shard_map/tpq,tqn->tpn/dot_general | solution.py:169
  321.2 1.8 gather_fusion.15
  323.0 3.7 %fusion.8 = f32[16,128,256]{2,1,0:T(8,128)} fusion(bf16[16,256,128]{2,1,0:T(8,128)(2,1)S(1)} %gather_fusion.14, bf16[16,3,256,256]{3,2,1,0:T(8,128)(2,1)} %param.17), kind=kOutput, calls=%fused_computation.26 | convolution fusion | flops 268435456 | bytes 5242880 | tf_op jit(solution)/shard_map/tpq,tqn->tpn/dot_general | solution.py:169
  326.8 3.8 %gather_fusion.9 = bf16[124,64,128]{2,1,0:T(8,128)(2,1)} fusion(bf16[128,64,128]{2,1,0:T(8,128)(2,1)} %bitcast.109, s32[1024]{0:T(1024)} %copy-done.35), kind=kCustom, calls=%fused_computation.9 | custom fusion | bytes 4063728 | tf_op jit(solution)/shard_map/gather | solution.py:56
  330.6 2.1 convolution_bitcast_fusion
  337.6 3.8 %add_bitcast_fusion = f32[16,256,128]{1,2,0:T(8,128)} fusion(f32[16,128,256]{2,1,0:T(8,128)S(1)} %copy-done.2, f32[16,128,256]{2,1,0:T(8,128)S(1)} %fusion.173, f32[16,128,256]{2,1,0:T(8,128)S(1)} %copy-done.1, bf16[16,256,128]{2,1,0:T(8,128)(2,1)S(1)} %copy-done.11, bf16[16,3,256,256]{3,2,1,0:T(8,128)(2,1)} %param.17), kind=kOutput, calls=%fused_computation.41 | convolution fusion | flops 270008320 | bytes 11534336 | tf_op jit(solution)/shard_map/tpq,tqn->tpn/dot_general | solution.py:169
  341.4 2.9 copy.138
  344.2 5.6 %fusion.3 = f32[4096,128]{1,0:T(8,128)} fusion(s32[4096]{0:T(1024)S(1)} %copy-done.29, f32[4096,128]{1,0:T(8,128)} %param.14, f32[16,256,128]{2,1,0:T(8,128)} %copy.130, f32[16,256,128]{2,1,0:T(8,128)} %copy.138), kind=kLoop, calls=%fused_computation.21 | loop fusion | flops 5767168 | bytes 8404992 | tf_op jit(solution)/shard_map/sub | solution.py:181
  (190 shorter events, 45.7 us)
Async XLA Ops:
  0.6 192.5 %copy-start = (bf16[31,64,256]{2,1,0:T(8,128)(2,1)S(1)}, bf16[31,64,256]{2,1,0:T(8,128)(2,1)}, u32[]{:S(2)}) copy-start(bf16[31,64,256]{2,1,0:T(8,128)(2,1)} %param.20) | copy-start | bytes 3047428
  0.6 5.3 %copy-start.32 = (s32[31,4]{0,1:T(4,128)S(1)}, s32[31,4]{0,1:T(4,128)}, u32[]{:S(2)}) copy-start(s32[31,4]{0,1:T(4,128)} %param.21) | copy-start | bytes 1492
  1.7 37.5 %copy-start.6 = (bf16[16,64,64]{2,1,0:T(8,128)(2,1)}, bf16[16,64,64]{2,1,0:T(8,128)(2,1)S(1)}, u32[]{:S(2)}) copy-start(bf16[16,64,64]{2,1,0:T(8,128)(2,1)S(1)} %slice.104) | copy-start | bytes 393220
  1.7 36.1 %copy-start.41 = (s32[124]{0:T(128)S(1)}, s32[124]{0:T(128)}, u32[]{:S(2)}) copy-start(s32[124]{0:T(128)} %constant.82.clone) | copy-start | bytes 1492
  1.7 36.6 %copy-start.44 = (s32[124]{0:T(128)S(1)}, s32[124]{0:T(128)}, u32[]{:S(2)}) copy-start(s32[124]{0:T(128)} %constant.83.clone) | copy-start | bytes 1492
  1.8 37.2 %copy-start.3 = (bf16[16,64,256]{2,1,0:T(8,128)(2,1)S(1)}, bf16[16,64,256]{2,1,0:T(8,128)(2,1)}, u32[]{:S(2)}) copy-start(bf16[16,64,256]{2,1,0:T(8,128)(2,1)} %param.16) | copy-start | bytes 1572868
  43.9 22.1 %copy-start.24 = (bf16[28,64,64]{2,1,0:T(8,128)(2,1)S(1)}, bf16[28,64,64]{2,1,0:T(8,128)(2,1)}, u32[]{:S(2)}) copy-start(bf16[28,64,64]{2,1,0:T(8,128)(2,1)} %param.22) | copy-start | bytes 688132
  43.9 23.5 %copy-start.33 = (s32[31,4]{0,1:T(4,128)S(1)}, s32[31,4]{0,1:T(4,128)}, u32[]{:S(2)}) copy-start(s32[31,4]{0,1:T(4,128)} %constant.97) | copy-start | bytes 1492
  43.9 23.7 %copy-start.31 = (s32[30,4]{0,1:T(4,128)S(1)}, s32[30,4]{0,1:T(4,128)}, u32[]{:S(2)}) copy-start(s32[30,4]{0,1:T(4,128)} %param.24) | copy-start | bytes 1444
  43.9 90.2 %slice-start = ((bf16[31,64,64]{2,1,0:T(8,128)(2,1)}), bf16[1,64,64]{2,1,0:T(8,128)(2,1)S(1)}, s32[]{:S(2)}) async-start(bf16[31,64,64]{2,1,0:T(8,128)(2,1)} %param.19), calls=%async_computation.2 | async-start | bytes 32768 | tf_op jit(solution)/shard_map/slice | solution.py:155
  43.9 145.5 %all-to-all-start = ((bf16[32,4,64,128]{3,2,1,0:T(8,128)(2,1)}), bf16[32,4,64,128]{3,2,1,0:T(8,128)(2,1)}, u32[]{:S(2)}, u32[]{:S(2)}) async-start(bf16[32,4,64,128]{3,2,1,0:T(8,128)(2,1)} %bitcast.496), calls=%async_computation | async-start | bytes 4194304 | tf_op jit(solution)/shard_map/all_to_all | solution.py:132
  58.6 123.5 %collective-permute-start = (bf16[512,128]{1,0:T(8,128)(2,1)}, bf16[512,128]{1,0:T(8,128)(2,1)}, u32[]{:S(2)}, u32[]{:S(2)}) collective-permute-start(bf16[512,128]{1,0:T(8,128)(2,1)} %get-tuple-element.10), channel_id=1, source_target_pairs={{0,1},{1,2},{2,3},{3,4},{4,5},{5,6},{6,7},{7,8},{8,9},{9,10},{10,1... | collective-permute-start | bytes 393224 | tf_op jit(solution)/shard_map/ppermute | solution.py:20
  60.7 121.5 %collective-permute-start.1 = (bf16[512,128]{1,0:T(8,128)(2,1)}, bf16[512,128]{1,0:T(8,128)(2,1)}, u32[]{:S(2)}, u32[]{:S(2)}) collective-permute-start(bf16[512,128]{1,0:T(8,128)(2,1)} %get-tuple-element.11), channel_id=1, source_target_pairs={{1,0},{2,1},{3,2},{4,3},{5,4},{6,5},{7,6},{8,7},{9,8},{10,9},{11,1... | collective-permute-start | bytes 393224 | tf_op jit(solution)/shard_map/ppermute | solution.py:21
  66.0 103.4 %copy-start.12 = (bf16[16,64,64]{2,1,0:T(8,128)(2,1)}, bf16[16,64,64]{2,1,0:T(8,128)(2,1)S(1)}, u32[]{:S(2)}) copy-start(bf16[16,64,64]{2,1,0:T(8,128)(2,1)S(1)} %slice.114) | copy-start | bytes 393220
  134.1 35.3 %copy-start.42 = (s32[4]{0:T(128)S(1)}, s32[4]{0:T(128)}, u32[]{:S(2)}) copy-start(s32[4]{0:T(128)} %get-tuple-element.5) | copy-start | bytes 52
  134.1 39.0 %copy-start.43 = (s32[16,2]{0,1:T(2,128)S(1)}, s32[16,2]{0,1:T(2,128)}, u32[]{:S(2)}) copy-start(s32[16,2]{0,1:T(2,128)} %param.18) | copy-start | bytes 388
  165.1 17.0 %copy-start.9 = (bf16[32,64,64]{2,1,0:T(8,128)(2,1)}, bf16[32,64,64]{2,1,0:T(8,128)(2,1)S(1)}, u32[]{:S(2)}) copy-start(bf16[32,64,64]{2,1,0:T(8,128)(2,1)S(1)} %all_gather.15) | copy-start | bytes 786436
  166.3 8.6 %copy-start.34 = (s32[1024]{0:T(1024)}, s32[1024]{0:T(1024)S(1)}, u32[]{:S(2)}) copy-start(s32[1024]{0:T(1024)S(1)} %get-tuple-element.39) | copy-start | bytes 12292
  166.3 8.7 %copy-start.36 = (s32[1024]{0:T(1024)}, s32[1024]{0:T(1024)S(1)}, u32[]{:S(2)}) copy-start(s32[1024]{0:T(1024)S(1)} %get-tuple-element.38) | copy-start | bytes 12292
  169.5 5.5 %copy-start.38 = (s32[1024]{0:T(1024)}, s32[1024]{0:T(1024)S(1)}, u32[]{:S(2)}) copy-start(s32[1024]{0:T(1024)S(1)} %pad_clamp_fusion.3) | copy-start | bytes 12292
  170.1 4.9 %copy-start.40 = (s32[1024]{0:T(1024)}, s32[1024]{0:T(1024)S(1)}, u32[]{:S(2)}) copy-start(s32[1024]{0:T(1024)S(1)} %pad_clamp_fusion.4) | copy-start | bytes 12292
  182.1 7.3 %copy-start.35 = (s32[1024]{0:T(1024)}, s32[1024]{0:T(1024)S(1)}, u32[]{:S(2)}) copy-start(s32[1024]{0:T(1024)S(1)} %pad_clamp_fusion.6) | copy-start | bytes 12292
  193.1 3.2 copy-start.16
  193.1 4.5 %copy-start.7 = (bf16[16,64,64]{2,1,0:T(8,128)(2,1)S(1)}, bf16[16,64,64]{2,1,0:T(8,128)(2,1)}, u32[]{:S(2)}) copy-start(bf16[16,64,64]{2,1,0:T(8,128)(2,1)} %copy-done.6) | copy-start | bytes 393220
  212.9 84.3 %copy-start.10 = (bf16[32,64,64]{2,1,0:T(8,128)(2,1)S(1)}, bf16[32,64,64]{2,1,0:T(8,128)(2,1)}, u32[]{:S(2)}) copy-start(bf16[32,64,64]{2,1,0:T(8,128)(2,1)} %copy-done.9) | copy-start | bytes 786436
  212.9 84.6 %copy-start.13 = (bf16[16,64,64]{2,1,0:T(8,128)(2,1)S(1)}, bf16[16,64,64]{2,1,0:T(8,128)(2,1)}, u32[]{:S(2)}) copy-start(bf16[16,64,64]{2,1,0:T(8,128)(2,1)} %copy-done.12) | copy-start | bytes 393220
  212.9 113.9 %all-to-all-start.1 = ((bf16[32,4,64,128]{3,2,1,0:T(8,128)(2,1)}), bf16[32,4,64,128]{3,2,1,0:T(8,128)(2,1)}, u32[]{:S(2)}, u32[]{:S(2)}) async-start(bf16[32,4,64,128]{3,2,1,0:T(8,128)(2,1)} %bitcast.497), calls=%async_computation.1 | async-start | bytes 4194304 | tf_op jit(solution)/shard_map/all_to_all | solution.py:132
  222.4 75.8 %copy-start.21 = (bf16[8,64,64]{2,1,0:T(8,128)(2,1)S(1)}, bf16[8,64,64]{2,1,0:T(8,128)(2,1)}, u32[]{:S(2)}) copy-start(bf16[8,64,64]{2,1,0:T(8,128)(2,1)} %slice.115) | copy-start | bytes 196612
  222.4 76.0 %copy-start.26 = (bf16[4,64,64]{2,1,0:T(8,128)(2,1)S(1)}, bf16[4,64,64]{2,1,0:T(8,128)(2,1)}, u32[]{:S(2)}) copy-start(bf16[4,64,64]{2,1,0:T(8,128)(2,1)} %slice.116) | copy-start | bytes 98308
  302.3 16.3 %collective-permute-start.2 = (bf16[512,128]{1,0:T(8,128)(2,1)S(1)}, bf16[512,128]{1,0:T(8,128)(2,1)S(1)}, u32[]{:S(2)}, u32[]{:S(2)}) collective-permute-start(bf16[512,128]{1,0:T(8,128)(2,1)S(1)} %get-tuple-element.8), channel_id=1, source_target_pairs={{0,1},{1,2},{2,3},{3,4},{4,5},{5,6},{6,7},{7,8},{8,9},{9,10},{10,1... | collective-permute-start | bytes 393224 | tf_op jit(solution)/shard_map/ppermute | solution.py:20
  304.6 14.7 %collective-permute-start.3 = (bf16[512,128]{1,0:T(8,128)(2,1)S(1)}, bf16[512,128]{1,0:T(8,128)(2,1)}, u32[]{:S(2)}, u32[]{:S(2)}) collective-permute-start(bf16[512,128]{1,0:T(8,128)(2,1)S(1)} %get-tuple-element.9), channel_id=1, source_target_pairs={{1,0},{2,1},{3,2},{4,3},{5,4},{6,5},{7,6},{8,7},{9,8},{10,9},{11,1... | collective-permute-start | bytes 393224 | tf_op jit(solution)/shard_map/ppermute | solution.py:21
  330.6 4.5 %copy-start.8 = (bf16[16,64,64]{2,1,0:T(8,128)(2,1)S(1)}, bf16[16,64,64]{2,1,0:T(8,128)(2,1)}, u32[]{:S(2)}) copy-start(bf16[16,64,64]{2,1,0:T(8,128)(2,1)} %copy-done.6) | copy-start | bytes 393220
  (20 other events, 37.1 us)
where the time goes:
time: 352 us; the launch traced here: 350 us
  blocking collectives  202 us (57%)
  matrix products  49.8 us (14%)
  local copies, waits for them, and re-layouts  42.2 us (12%)
  starting transfers between devices  38.2 us (11%)
  other arithmetic  16.1 us (5%)
    all_gather x2, blocking collectives, operate(): lax.all_gather(coefs[-1], 'leaf', axis=0, tiled=True)  139 us
    all_gather x1, blocking collectives, local(): lax.all_gather(sources, 'leaf', axis=0, tiled=True)  31.6 us
    all_gather x1, blocking collectives, operate(): lax.all_gather(transfer[node_count - 1:node_count], 'leaf', axis=0, tiled...  31 us
    all_to_all x2, starting transfers between devices, operate(): lax.all_to_all(stacked[chosen], 'leaf', split_axis=0, concat_axis=0, tile...  23.5 us
    dot_general x6, matrix products, operate(): jnp.einsum('tpq,tqn->tpn', near_tiles[:, member], neighbours[member], pre...  22.6 us
    ppermute x2, starting transfers between devices, with_halo(): after = lax.ppermute(first, axis, down)  10.4 us
    gather x2, local copies, waits for them, and re-layouts, apply_blocks(): blocks = incoming.reshape(-1, rank_dim, classes)[landing]  7.54 us
  transfers between devices with their start and end apart: 6, of which 0 were waited for; matrix products, arithmetic and copies ran while one was open for 14% of the time, Pallas kernels for 0%

commit v1 on v0

v1 whole, which is shorter than its diff:
```python
import functools

import jax
import jax.numpy as jnp
import numpy as np
from jax import lax
from jax.experimental import pallas as pl
from jax.experimental.pallas import tpu as pltpu
from jax.sharding import PartitionSpec as P

REACH = 2
STEP_SIZE = 0.5
MIB = 1 << 20
F32 = jnp.float32
BF16 = jnp.bfloat16


def rows_dot(left, right):
    return lax.dot_general(left, right, (((0,), (0,)), ((), ())), preferred_element_type=F32)


def dot(left, right):
    return jnp.dot(left, right, preferred_element_type=F32)


def pair_rows(ref, first):
    both = ref[pl.ds(first, 2)]
    return both.reshape(2 * both.shape[1], both.shape[2])


def tree_rows(per_dev):
    counts = [per_dev >> height for height in range(per_dev.bit_length())]
    starts = [sum(counts[:height]) for height in range(len(counts))]
    return counts, starts


def go_up(coef, transfer, per_dev):
    counts, starts = tree_rows(per_dev)
    for height in range(1, len(counts)):
        for node in range(counts[height]):
            kids = starts[height - 1] + 2 * node
            coef[starts[height] + node] = rows_dot(
                pair_rows(transfer, kids), pair_rows(coef, kids)
            ).astype(BF16)


def go_down(field, coupled, transfer, parent, per_dev):
    counts, starts = tree_rows(per_dev)
    top = starts[-1]
    field[top] = (coupled[top] + dot(transfer[top], parent)).astype(BF16)
    for height in range(len(counts) - 2, -1, -1):
        for node in range(counts[height + 1]):
            kids = starts[height] + 2 * node
            pushed = dot(pair_rows(transfer, kids), field[starts[height + 1] + node])
            both = pair_rows(coupled, kids) + pushed
            field[pl.ds(kids, 2)] = both.reshape(2, -1, both.shape[1]).astype(BF16)


def first_kernel(per_dev, weights, basis, transfer, values, coef, top_part):
    step = pl.program_id(0)
    block = basis.shape[0]
    for leaf in range(block):
        rounded = weights[leaf].astype(BF16)
        values[leaf] = rounded
        coef[step * block + leaf] = dot(basis[leaf], rounded).astype(BF16)

    @pl.when(step == pl.num_programs(0) - 1)
    def _():
        go_up(coef, transfer, per_dev)
        top = coef.shape[0] - 1
        top_part[...] = rows_dot(transfer[top], coef[top])


def pick_kernel(chosen, coef, payload):
    for slot in range(payload.shape[0]):
        payload[slot] = coef[chosen[slot]]


def near_kernel(ids, before, own, after, tiles, out, padded):
    step = pl.program_id(0)
    block = tiles.shape[0]
    reach = before.shape[0]
    inner = own.shape[0]

    @pl.when(step == 0)
    def _():
        padded[pl.ds(0, reach)] = before[...]
        padded[pl.ds(reach, inner)] = own[...]
        padded[pl.ds(reach + inner, reach)] = after[...]

    for leaf in range(block):
        row = step * block + leaf
        out[leaf] = (
            dot(tiles[leaf, 0], padded[row + reach])
            + dot(tiles[leaf, 1], padded[ids[2 * row]])
            + dot(tiles[leaf, 2], padded[ids[2 * row + 1]])
        )


def coarse_kernel(devices, me, listed, gathered, transfer, couplings, out, coef):
    levels = devices.bit_length() - 2
    links = couplings.shape[2] // couplings.shape[1]
    offsets = [devices - (devices >> level - 1) for level in range(1, levels + 1)]
    mine = me[0]
    for node in range(devices // 2):
        coef[node] = gathered[jnp.bitwise_xor(mine >> 1, node)]
    for level in range(1, levels):
        for node in range(devices >> level + 1):
            kids = offsets[level - 1] + 2 * node
            coef[offsets[level] + node] = rows_dot(
                pair_rows(transfer, kids), pair_rows(coef, kids)
            ).astype(BF16)
    field = None
    for level in range(levels, 0, -1):
        offset = offsets[level - 1]
        node = offset + (mine >> level)
        blocks = jnp.concatenate(
            [coef[offset + listed[node * links + link]] for link in range(links)], axis=0
        )
        term = dot(couplings[node], blocks)
        if level < levels:
            term = term + dot(transfer[node], field)
        field = term.astype(BF16)
    out[...] = field


def finish_kernel(
    per_dev, last, landing, chosen, incoming, couplings, transfer, parent, near, base, basis, *rest
):
    if last:
        scores_out, new_out, field, coupled = rest
    else:
        new_out, values, payload, top_part, field, coupled, coef = rest
    step = pl.program_id(0)
    block = basis.shape[0]
    links = couplings.shape[2] // couplings.shape[1]

    @pl.when(step == 0)
    def _():
        for node in range(couplings.shape[0]):
            blocks = jnp.concatenate(
                [incoming[landing[node * links + link]] for link in range(links)], axis=0
            )
            coupled[node] = dot(couplings[node], blocks)
        go_down(field, coupled, transfer, parent[...], per_dev)

    for leaf in range(block):
        row = step * block + leaf
        scores = near[leaf] + rows_dot(basis[leaf], field[row])
        new = base[leaf] - (0.5 * STEP_SIZE) * (1.0 + jnp.tanh(0.5 * scores))
        new_out[leaf] = new
        if last:
            scores_out[leaf] = scores
        else:
            rounded = new.astype(BF16)
            values[leaf] = rounded
            coef[row] = dot(basis[leaf], rounded).astype(BF16)

    if not last:

        @pl.when(step == pl.num_programs(0) - 1)
        def _():
            go_up(coef, transfer, per_dev)
            top = coef.shape[0] - 1
            top_part[...] = rows_dot(transfer[top], coef[top])
            for slot in range(payload.shape[0]):
                payload[slot] = coef[chosen[slot]]


def whole(shape):
    return pl.BlockSpec(shape, lambda i, *_: (0,) * len(shape), pipeline_mode=pl.Buffered(1))


def whole_out(shape):
    return pl.BlockSpec(shape, lambda i, *_: (0,) * len(shape))


def per_step(block, shape):
    return pl.BlockSpec((block,) + tuple(shape[1:]), lambda i, *_: (i,) + (0,) * (len(shape) - 1))


def params(limit):
    return pltpu.CompilerParams(
        dimension_semantics=("arbitrary",), vmem_limit_bytes=limit * MIB
    )


def cost(flops, moved):
    return pl.CostEstimate(flops=int(flops), bytes_accessed=int(moved), transcendentals=0)


def plan(sources, devices, per_dev, capacity):
    counts, starts = tree_rows(per_dev)
    links = sources.shape[1]
    heights = np.repeat(np.arange(len(counts)), np.array(counts) * links)
    shift = jnp.asarray((len(counts) - 1 - heights).astype(np.int32))
    start = jnp.asarray(np.array(starts)[heights].astype(np.int32))
    mask = jnp.asarray((np.array(counts)[heights] - 1).astype(np.int32))
    flat = sources.reshape(-1)
    owner = flat >> shift
    row = start + (flat & mask)
    width = flat.shape[0]
    earlier = jnp.asarray(np.tril(np.ones((width, width), dtype=bool), -1))
    rank = jnp.sum(((owner[:, None] == owner[None, :]) & earlier).astype(jnp.int32), axis=1)
    landing = owner * capacity + rank
    slots = jnp.arange(devices * capacity, dtype=jnp.int32)
    wanted = jnp.sum(jnp.where(landing[None, :] == slots[:, None], row[None, :], 0), axis=1)
    chosen = lax.all_to_all(
        wanted.reshape(devices, capacity), "leaf", split_axis=0, concat_axis=0, tiled=True
    )
    return landing, chosen.reshape(-1)


def local(
    weights,
    labels,
    basis,
    near_tiles,
    near_ids,
    transfer,
    couplings,
    sources,
    coarse_transfer,
    coarse_couplings,
    coarse_sources,
):
    devices = lax.axis_size("leaf")
    me = lax.axis_index("leaf")
    per_dev, rank_dim, leaf_size = basis.shape
    classes = weights.shape[1]
    nodes = transfer.shape[0]
    links = sources.shape[1]
    capacity = nodes * links // devices + 1
    slots = devices * capacity
    block = next(size for size in (4, 2, 1) if per_dev % size == 0)
    steps = per_dev // block
    node_shape = (rank_dim, classes)
    leaf_shape = (per_dev, leaf_size, classes)
    weights3 = weights.reshape(leaf_shape)
    offset_ids = (near_ids - (me * per_dev - REACH)).reshape(-1)

    landing, chosen = plan(sources, devices, per_dev, capacity)

    values, coef, top_part = pl.pallas_call(
        functools.partial(first_kernel, per_dev),
        grid=(steps,),
        in_specs=[
            per_step(block, leaf_shape),
            per_step(block, basis.shape),
            whole(transfer.shape),
        ],
        out_specs=[
            per_step(block, leaf_shape),
            whole_out((nodes,) + node_shape),
            whole_out(node_shape),
        ],
        out_shape=[
            jax.ShapeDtypeStruct(leaf_shape, BF16),
            jax.ShapeDtypeStruct((nodes,) + node_shape, BF16),
            jax.ShapeDtypeStruct(node_shape, F32),
        ],
        compiler_params=params(16),
        cost_estimate=cost(2 * basis.size * classes, 4 * weights.size),
        name="leaf_coefs",
    )(weights3, basis, transfer)

    payload = pl.pallas_call(
        pick_kernel,
        grid=(1,),
        in_specs=[
            pl.BlockSpec(memory_space=pltpu.SMEM),
            whole((nodes,) + node_shape),
        ],
        out_specs=whole_out((slots,) + node_shape),
        out_shape=jax.ShapeDtypeStruct((slots,) + node_shape, BF16),
        compiler_params=params(16),
        cost_estimate=cost(0, 4 * slots * rank_dim * classes),
        name="pick_rows",
    )(chosen, coef)

    def exchange(payload):
        return lax.all_to_all(payload, "leaf", split_axis=0, concat_axis=0, tiled=True)

    def near_field(values):
        up = [(i, i + 1) for i in range(devices - 1)]
        down = [(j, i) for i, j in up]
        before = lax.ppermute(values[per_dev - REACH :], "leaf", up)
        after = lax.ppermute(values[:REACH], "leaf", down)
        halo = (REACH, leaf_size, classes)
        return pl.pallas_call(
            near_kernel,
            grid=(steps,),
            in_specs=[
                pl.BlockSpec(memory_space=pltpu.SMEM),
                whole(halo),
                whole(leaf_shape),
                whole(halo),
                per_step(block, near_tiles.shape),
            ],
            out_specs=per_step(block, leaf_shape),
            out_shape=jax.ShapeDtypeStruct(leaf_shape, F32),
            scratch_shapes=[pltpu.VMEM((per_dev + 2 * REACH, leaf_size, classes), BF16)],
            compiler_params=params(24),
            cost_estimate=cost(2 * near_tiles.size * classes, 2 * near_tiles.size),
            name="near_field",
        )(offset_ids, before, values, after, near_tiles)

    def coarse_field(top_part):
        other = lax.ppermute(top_part, "leaf", [(i, i ^ 1) for i in range(devices)])
        gathered = (top_part + other).astype(BF16)[None]
        hop = 2
        while hop < devices:
            arrived = lax.ppermute(gathered, "leaf", [(i, i ^ hop) for i in range(devices)])
            gathered = jnp.concatenate([gathered, arrived], axis=0)
            hop *= 2
        smem = pl.BlockSpec(memory_space=pltpu.SMEM)
        return pl.pallas_call(
            functools.partial(coarse_kernel, devices),
            grid=(1,),
            in_specs=[
                smem,
                smem,
                whole(gathered.shape),
                whole(coarse_transfer.shape),
                whole(coarse_couplings.shape),
            ],
            out_specs=whole_out(node_shape),
            out_shape=jax.ShapeDtypeStruct(node_shape, BF16),
            scratch_shapes=[pltpu.VMEM((coarse_couplings.shape[0],) + node_shape, BF16)],
            compiler_params=params(16),
            cost_estimate=cost(2 * coarse_couplings.size * classes, 2 * coarse_couplings.size),
            name="coarse_field",
        )(
            me.reshape(1),
            coarse_sources.reshape(-1),
            gathered,
            coarse_transfer,
            coarse_couplings,
        )

    def finish(incoming, parent, near, base, last):
        leaf_out = jax.ShapeDtypeStruct(leaf_shape, F32)
        scratch = [
            pltpu.VMEM((nodes,) + node_shape, BF16),
            pltpu.VMEM((nodes,) + node_shape, F32),
        ]
        if last:
            out_shape = [leaf_out, leaf_out]
            out_specs = [per_step(block, leaf_shape)] * 2
        else:
            out_shape = [
                leaf_out,
                jax.ShapeDtypeStruct(leaf_shape, BF16),
                jax.ShapeDtypeStruct((slots,) + node_shape, BF16),
                jax.ShapeDtypeStruct(node_shape, F32),
            ]
            out_specs = [
                per_step(block, leaf_shape),
                per_step(block, leaf_shape),
                whole_out((slots,) + node_shape),
                whole_out(node_shape),
            ]
            scratch.append(pltpu.VMEM((nodes,) + node_shape, BF16))
        return pl.pallas_call(
            functools.partial(finish_kernel, per_dev, last),
            grid_spec=pltpu.PrefetchScalarGridSpec(
                num_scalar_prefetch=2,
                grid=(steps,),
                in_specs=[
                    whole(incoming.shape),
                    whole(couplings.shape),
                    whole(transfer.shape),
                    whole(node_shape),
                    per_step(block, leaf_shape),
                    per_step(block, leaf_shape),
                    per_step(block, basis.shape),
                ],
                out_specs=out_specs,
                scratch_shapes=scratch,
            ),
            out_shape=out_shape,
            compiler_params=params(32),
            cost_estimate=cost(2 * couplings.size * classes, 12 * weights.size),
            name="last_scores" if last else "first_scores",
        )(landing, chosen, incoming, couplings, transfer, parent, near, base, basis)

    shift_up = STEP_SIZE * (
        labels[:, None] == jnp.arange(classes, dtype=jnp.int32)[None, :]
    ).astype(F32).reshape(leaf_shape)

    incoming = exchange(payload)
    near = near_field(values)
    parent = coarse_field(top_part)
    middle, values, payload, top_part = finish(
        incoming, parent, near, weights3 + shift_up, False
    )
    incoming = exchange(payload)
    near = near_field(values)
    parent = coarse_field(top_part)
    second_scores, updated = finish(incoming, parent, near, middle + shift_up, True)
    return updated.reshape(weights.shape), second_scores.reshape(weights.shape)


def solution(mesh):
    in_specs = (
        P("leaf", None),
        P("leaf"),
        P("leaf", None, None),
        P("leaf", None, None, None),
        P("leaf", None),
        P("leaf", None, None),
        P("leaf", None, None),
        P("leaf", None),
        P(),
        P(),
        P(),
    )
    out_specs = (P("leaf", None), P("leaf", None))
    return jax.shard_map(local, mesh=mesh, in_specs=in_specs, out_specs=out_specs, check_vma=False)
```

time: 352 us -> 176 us (0.50)
  blocking collectives: 202 us -> 0 us
  waiting for transfers between devices: 0.02 us -> 81.1 us
  matrix products: 49.8 us -> 0 us
  Pallas kernels: 0 us -> 25.2 us
  local copies, waits for them, and re-layouts: 42.2 us -> 25 us
  other arithmetic: 16.1 us -> 5.88 us
    all_gather x4 -> x0, blocking collectives: 202 us -> none  [the longest x2 139 us: operate(): lax.all_gather(coefs[-1], 'leaf', axis=0, tiled=True)]
    ppermute x4 -> x14, waiting for transfers between devices: 0.01 us -> 81.1 us  [the longest x8 51 us: coarse_field(): lax.ppermute(gathered, 'leaf', [(i, i ^ hop) for i in range(devices)])]
    dot_general x46 -> x0, matrix products: 49.8 us -> none  [the longest x6 22.6 us: operate(): jnp.einsum('tpq,tqn->tpn', near_tiles[:, member], neighbours[member], pre...]
    pallas_call x0 -> x8, Pallas kernels: none -> 25.2 us  [the longest x2 14 us: finish(): pl.pallas_call(functools.partial(finish_kernel, per_dev, last), grid_spec...]
    gather x16 -> x0, local copies, waits for them, and re-layouts: 23.8 us -> none  [the longest x2 7.54 us: apply_blocks(): blocks = incoming.reshape(-1, rank_dim, classes)[landing]]
    unnamed x90 -> x61, local copies, waits for them, and re-layouts: 5.45 us -> 21.2 us
    all_to_all x2 -> x3, starting transfers between devices: 23.5 us -> 15.2 us  [the longest x2 9.25 us: exchange(): lax.all_to_all(payload, 'leaf', split_axis=0, concat_axis=0, tiled=True)]
    ppermute x4 -> x14, starting transfers between devices: 14.7 us -> 21.8 us  [the longest x8 9.34 us: coarse_field(): lax.ppermute(gathered, 'leaf', [(i, i ^ hop) for i in range(devices)])]
  transfers between devices with their start and end apart: 6 -> 17, of which waited for: 0 -> 10; matrix products, arithmetic and copies ran while one was open for 14% -> 3% of each run, Pallas kernels for 0% -> 6%
where the time goes in v1:
time: 176 us; the launch traced here: 175 us
  waiting for transfers between devices  81.1 us (46%)
  starting transfers between devices  37 us (21%)
  Pallas kernels  25.2 us (14%)
  local copies, waits for them, and re-layouts  25 us (14%)
  other arithmetic  5.88 us (3%)
    ppermute x8, waiting for transfers between devices, coarse_field(): lax.ppermute(gathered, 'leaf', [(i, i ^ hop) for i in range(devices)])  51 us
    ppermute x2, waiting for transfers between devices, near_field(): after = lax.ppermute(values[:REACH], 'leaf', down)  24 us
    unnamed x61, local copies, waits for them, and re-layouts  21.2 us
    pallas_call x2, Pallas kernels, finish(): pl.pallas_call(functools.partial(finish_kernel, per_dev, last), grid_spec...  14 us
    ppermute x8, starting transfers between devices, coarse_field(): lax.ppermute(gathered, 'leaf', [(i, i ^ hop) for i in range(devices)])  9.34 us
    all_to_all x2, starting transfers between devices, exchange(): lax.all_to_all(payload, 'leaf', split_axis=0, concat_axis=0, tiled=True)  9.25 us
    ppermute x2, starting transfers between devices, near_field(): after = lax.ppermute(values[:REACH], 'leaf', down)  8.32 us
    ppermute x2, waiting for transfers between devices, near_field(): before = lax.ppermute(values[per_dev - REACH:], 'leaf', up)  6.13 us
  transfers between devices with their start and end apart: 17, of which 10 were waited for; matrix products, arithmetic and copies ran while one was open for 3% of the time, Pallas kernels for 6%

profile of v1, /device:TPU:16, one launch (start us, length us, event | category | flops | bytes accessed | tf_op | source)
XLA Modules:
  0.0 175.3 jit_solution(12228347578385398625)
XLA Ops:
  3.5 5.9 %all-to-all-start = ((s32[32,1,4]{2,1,0:T(1,128)}), s32[32,1,4]{2,1,0:T(1,128)S(1)}, u32[]{:S(2)}, u32[]{:S(2)}) async-start(s32[32,1,4]{2,1,0:T(1,128)} %bitcast), calls=%async_computation | async-start | bytes 32768 | tf_op jit(solution)/shard_map/all_to_all | solution.py:208
  9.5 1.6 copy-done.4
  18.0 5.9 %all-to-all-start.1 = ((bf16[128,64,128]{2,1,0:T(8,128)(2,1)}), bf16[128,64,128]{2,1,0:T(8,128)(2,1)}, u32[]{:S(2)}, u32[]{:S(2)}) async-start(bf16[128,64,128]{2,1,0:T(8,128)(2,1)} %copy-done.6), calls=%async_computation.1 | async-start | bytes 4194304 | tf_op jit(solution)/shard_map/all_to_all | solution.py:282
  24.9 4.2 %collective-permute-start.6 = (bf16[2,256,128]{2,1,0:T(8,128)(2,1)}, bf16[2,256,128]{2,1,0:T(8,128)(2,1)S(1)}, u32[]{:S(2)}, u32[]{:S(2)}) collective-permute-start(bf16[2,256,128]{2,1,0:T(8,128)(2,1)} %get-tuple-element.26), channel_id=1, source_target_pairs={{1,0},{2,1},{3,2},{4,3},{5,4},{6,5},{7,6},{8,7},{9,8},{10,9},{11,1... | collective-permute-start | bytes 393224 | tf_op jit(solution)/shard_map/ppermute | solution.py:288
  29.1 1.9 %collective-permute-start.5 = (bf16[2,256,128]{2,1,0:T(8,128)(2,1)}, bf16[2,256,128]{2,1,0:T(8,128)(2,1)S(1)}, u32[]{:S(2)}, u32[]{:S(2)}) collective-permute-start(bf16[2,256,128]{2,1,0:T(8,128)(2,1)} %get-tuple-element.27), channel_id=1, source_target_pairs={{0,1},{1,2},{2,3},{3,4},{4,5},{5,6},{6,7},{7,8},{8,9},{9,10},{10,1... | collective-permute-start | bytes 393224 | tf_op jit(solution)/shard_map/ppermute | solution.py:287
  31.1 1.7 select_add_fusion.1.base
  33.3 10.2 %collective-permute-done.1 = bf16[1,64,128]{2,1,0:T(8,128)(2,1)S(1)} collective-permute-done((bf16[1,64,128]{2,1,0:T(8,128)(2,1)S(1)}, bf16[1,64,128]{2,1,0:T(8,128)(2,1)S(1)}, u32[]{:S(2)}, u32[]{:S(2)}) %collective-permute-start.1) | collective-permute-done | bytes 16416 | tf_op jit(solution)/shard_map/ppermute | solution.py:313
  43.6 4.2 %collective-permute-done.2 = bf16[2,64,128]{2,1,0:T(8,128)(2,1)S(1)} collective-permute-done((bf16[2,64,128]{2,1,0:T(8,128)(2,1)S(1)}, bf16[2,64,128]{2,1,0:T(8,128)(2,1)S(1)}, u32[]{:S(2)}, u32[]{:S(2)}) %collective-permute-start.2) | collective-permute-done | bytes 32800 | tf_op jit(solution)/shard_map/ppermute | solution.py:313
  47.8 4.5 %collective-permute-start.3 = (bf16[4,64,128]{2,1,0:T(8,128)(2,1)S(1)}, bf16[4,64,128]{2,1,0:T(8,128)(2,1)S(1)}, u32[]{:S(2)}, u32[]{:S(2)}) collective-permute-start(bf16[4,64,128]{2,1,0:T(8,128)(2,1)S(1)} %pad_maximum_fusion.2), channel_id=1, source_target_pairs={{0,8},{1,9},{2,10},{3,11},{4,12},{5,13},{6,14},{7,15},{8,0},{9,1},... | collective-permute-start | bytes 196616 | tf_op jit(solution)/shard_map/ppermute | solution.py:313
  52.4 10.9 %collective-permute-done.3 = bf16[4,64,128]{2,1,0:T(8,128)(2,1)S(1)} collective-permute-done((bf16[4,64,128]{2,1,0:T(8,128)(2,1)S(1)}, bf16[4,64,128]{2,1,0:T(8,128)(2,1)S(1)}, u32[]{:S(2)}, u32[]{:S(2)}) %collective-permute-start.3) | collective-permute-done | bytes 65568 | tf_op jit(solution)/shard_map/ppermute | solution.py:313
  63.4 12.0 %collective-permute-done.6.after = bf16[2,256,128]{2,1,0:T(8,128)(2,1)S(1)} collective-permute-done((bf16[2,256,128]{2,1,0:T(8,128)(2,1)}, bf16[2,256,128]{2,1,0:T(8,128)(2,1)S(1)}, u32[]{:S(2)}, u32[]{:S(2)}) %collective-permute-start.6) | collective-permute-done | bytes 131104 | tf_op jit(solution)/shard_map/ppermute | solution.py:288
  75.4 3.0 %collective-permute-done.5.before = bf16[2,256,128]{2,1,0:T(8,128)(2,1)S(1)} collective-permute-done((bf16[2,256,128]{2,1,0:T(8,128)(2,1)}, bf16[2,256,128]{2,1,0:T(8,128)(2,1)S(1)}, u32[]{:S(2)}, u32[]{:S(2)}) %collective-permute-start.5) | collective-permute-done | bytes 131104 | tf_op jit(solution)/shard_map/ppermute | solution.py:287
  78.4 2.8 %copy-done = bf16[16,3,256,256]{3,2,1,0:T(8,128)(2,1)S(1)} copy-done((bf16[16,3,256,256]{3,2,1,0:T(8,128)(2,1)S(1)}, bf16[16,3,256,256]{3,2,1,0:T(8,128)(2,1)}, u32[]{:S(2)}) %copy-start) | copy-done | bytes 6291480
  82.4 2.9 %near_field.2.near = f32[16,256,128]{2,1,0:T(8,128)S(1)} custom-call(s32[32]{0:T(128)S(1)} %reshape.54.ids, bf16[2,256,128]{2,1,0:T(8,128)(2,1)S(1)} %collective-permute-done.5.before, bf16[16,256,128]{2,1,0:T(8,128)(2,1)S(1)} %copy-done.21, bf16[2,256,128]{2,1,0:T(8,128)(2,1)S(1)} %collective-permute-done.6.after, bf16[16,3,256,256]{3,2,1,0:T(8,128)(2,1)S(1)} %copy-done), custom_call_target="tpu_custom_call" | custom-call | flops 805306368 | bytes 6291456 | tf_op jit(solution)/shard_map/near_field/pallas_call | solution.py:290
  85.5 1.6 coarse_field.2.parent
  87.1 1.6 copy-done.2
  89.9 7.8 %first_scores.1 = (f32[16,256,128]{2,1,0:T(8,128)S(1)}, bf16[16,256,128]{2,1,0:T(8,128)(2,1)S(1)}, bf16[128,64,128]{2,1,0:T(8,128)(2,1)S(1)}, f32[64,128]{1,0:T(8,128)S(1)}) custom-call(s32[124]{0:T(128)S(1)} %multiply_add_fusion.landing, s32[128]{0:T(128)S(1)} %reshape.50.chosen, bf16[128,64,128]{2,1,0:T(8,128)(2,1)} %all-to-all-done.1.incoming, ...), custom_call_target="tpu_custom_call" | custom-call | flops 130023424 | bytes 6291456 | tf_op jit(solution)/shard_map/first_scores/pallas_call | solution.py:364
  101.3 3.4 %all-to-all-start.2 = ((bf16[128,64,128]{2,1,0:T(8,128)(2,1)}), bf16[128,64,128]{2,1,0:T(8,128)(2,1)}, u32[]{:S(2)}, u32[]{:S(2)}) async-start(bf16[128,64,128]{2,1,0:T(8,128)(2,1)} %copy-done.15), calls=%async_computation.2 | async-start | bytes 4194304 | tf_op jit(solution)/shard_map/all_to_all | solution.py:282
  105.8 4.1 %collective-permute-start.13 = (bf16[2,256,128]{2,1,0:T(8,128)(2,1)S(1)}, bf16[2,256,128]{2,1,0:T(8,128)(2,1)S(1)}, u32[]{:S(2)}, u32[]{:S(2)}) collective-permute-start(bf16[2,256,128]{2,1,0:T(8,128)(2,1)S(1)} %get-tuple-element.24), channel_id=1, source_target_pairs={{1,0},{2,1},{3,2},{4,3},{5,4},{6,5},{7,6},{8,7},{9,8},{10,9},{11,1... | collective-permute-start | bytes 393224 | tf_op jit(solution)/shard_map/ppermute | solution.py:288
  109.9 1.9 %collective-permute-start.12 = (bf16[2,256,128]{2,1,0:T(8,128)(2,1)S(1)}, bf16[2,256,128]{2,1,0:T(8,128)(2,1)S(1)}, u32[]{:S(2)}, u32[]{:S(2)}) collective-permute-start(bf16[2,256,128]{2,1,0:T(8,128)(2,1)S(1)} %get-tuple-element.25), channel_id=1, source_target_pairs={{0,1},{1,2},{2,3},{3,4},{4,5},{5,6},{6,7},{7,8},{8,9},{9,10},{10,1... | collective-permute-start | bytes 393224 | tf_op jit(solution)/shard_map/ppermute | solution.py:287
  111.9 1.7 select_add_fusion.base
  113.6 10.4 %collective-permute-done.8 = bf16[1,64,128]{2,1,0:T(8,128)(2,1)S(1)} collective-permute-done((bf16[1,64,128]{2,1,0:T(8,128)(2,1)S(1)}, bf16[1,64,128]{2,1,0:T(8,128)(2,1)S(1)}, u32[]{:S(2)}, u32[]{:S(2)}) %collective-permute-start.8) | collective-permute-done | bytes 16416 | tf_op jit(solution)/shard_map/ppermute | solution.py:313
  124.1 4.2 %collective-permute-done.9 = bf16[2,64,128]{2,1,0:T(8,128)(2,1)S(1)} collective-permute-done((bf16[2,64,128]{2,1,0:T(8,128)(2,1)S(1)}, bf16[2,64,128]{2,1,0:T(8,128)(2,1)S(1)}, u32[]{:S(2)}, u32[]{:S(2)}) %collective-permute-start.9) | collective-permute-done | bytes 32800 | tf_op jit(solution)/shard_map/ppermute | solution.py:313
  128.3 4.5 %collective-permute-start.10 = (bf16[4,64,128]{2,1,0:T(8,128)(2,1)S(1)}, bf16[4,64,128]{2,1,0:T(8,128)(2,1)S(1)}, u32[]{:S(2)}, u32[]{:S(2)}) collective-permute-start(bf16[4,64,128]{2,1,0:T(8,128)(2,1)S(1)} %pad_maximum_fusion.3), channel_id=1, source_target_pairs={{0,8},{1,9},{2,10},{3,11},{4,12},{5,13},{6,14},{7,15},{8,0},{9,1},... | collective-permute-start | bytes 196616 | tf_op jit(solution)/shard_map/ppermute | solution.py:313
  132.9 10.9 %collective-permute-done.10 = bf16[4,64,128]{2,1,0:T(8,128)(2,1)S(1)} collective-permute-done((bf16[4,64,128]{2,1,0:T(8,128)(2,1)S(1)}, bf16[4,64,128]{2,1,0:T(8,128)(2,1)S(1)}, u32[]{:S(2)}, u32[]{:S(2)}) %collective-permute-start.10) | collective-permute-done | bytes 65568 | tf_op jit(solution)/shard_map/ppermute | solution.py:313
  143.9 11.9 %collective-permute-done.13.after = bf16[2,256,128]{2,1,0:T(8,128)(2,1)S(1)} collective-permute-done((bf16[2,256,128]{2,1,0:T(8,128)(2,1)S(1)}, bf16[2,256,128]{2,1,0:T(8,128)(2,1)S(1)}, u32[]{:S(2)}, u32[]{:S(2)}) %collective-permute-start.13) | collective-permute-done | bytes 131104 | tf_op jit(solution)/shard_map/ppermute | solution.py:288
  155.8 3.1 %collective-permute-done.12.before = bf16[2,256,128]{2,1,0:T(8,128)(2,1)S(1)} collective-permute-done((bf16[2,256,128]{2,1,0:T(8,128)(2,1)S(1)}, bf16[2,256,128]{2,1,0:T(8,128)(2,1)S(1)}, u32[]{:S(2)}, u32[]{:S(2)}) %collective-permute-start.12) | collective-permute-done | bytes 131104 | tf_op jit(solution)/shard_map/ppermute | solution.py:287
  158.9 2.8 %copy-done.1 = bf16[16,3,256,256]{3,2,1,0:T(8,128)(2,1)S(1)} copy-done((bf16[16,3,256,256]{3,2,1,0:T(8,128)(2,1)S(1)}, bf16[16,3,256,256]{3,2,1,0:T(8,128)(2,1)}, u32[]{:S(2)}) %copy-start.1) | copy-done | bytes 6291480
  161.7 2.9 %near_field.3.near = f32[16,256,128]{2,1,0:T(8,128)S(1)} custom-call(s32[32]{0:T(128)S(1)} %reshape.54.ids, bf16[2,256,128]{2,1,0:T(8,128)(2,1)S(1)} %collective-permute-done.12.before, bf16[16,256,128]{2,1,0:T(8,128)(2,1)S(1)} %copy-done.23, bf16[2,256,128]{2,1,0:T(8,128)(2,1)S(1)} %collective-permute-done.13.after, bf16[16,3,256,256]{3,2,1,0:T(8,128)(2,1)S(1)} %copy-done.1), custom_call_target="tpu_custom_call" | custom-call | flops 805306368 | bytes 6291456 | tf_op jit(solution)/shard_map/near_field/pallas_call | solution.py:290
  164.7 1.6 coarse_field.3.parent
  166.4 1.6 copy-done.3
  169.2 6.2 %last_scores.1 = (f32[16,256,128]{2,1,0:T(8,128)}, f32[16,256,128]{2,1,0:T(8,128)}) custom-call(s32[124]{0:T(128)S(1)} %multiply_add_fusion.landing, s32[128]{0:T(128)S(1)} %reshape.50.chosen, bf16[128,64,128]{2,1,0:T(8,128)(2,1)} %all-to-all-done.2.incoming, bf16[31,64,256]{2,1,0:T(8,128)(2,1)S(1)} %copy-done.12, bf16[31,64,64]{2,1,0:T(8,128)(2,1)S(1)} %copy-done.10, ...), custom_call_target="tpu_custom_call" | custom-call | flops 130023424 | bytes 6291456 | tf_op jit(solution)/shard_map/last_scores/pallas_call | solution.py:364
  (102 shorter events, 20.0 us)
Async XLA Ops:
  3.5 11.1 %all-to-all-start = ((s32[32,1,4]{2,1,0:T(1,128)}), s32[32,1,4]{2,1,0:T(1,128)S(1)}, u32[]{:S(2)}, u32[]{:S(2)}) async-start(s32[32,1,4]{2,1,0:T(1,128)} %bitcast), calls=%async_computation | async-start | bytes 32768 | tf_op jit(solution)/shard_map/all_to_all | solution.py:208
  14.6 9.5 %copy-start.20 = (bf16[16,256,128]{2,1,0:T(8,128)(2,1)}, bf16[16,256,128]{2,1,0:T(8,128)(2,1)S(1)}, u32[]{:S(2)}) copy-start(bf16[16,256,128]{2,1,0:T(8,128)(2,1)S(1)} %get-tuple-element.13.own) | copy-start | bytes 3145732
  18.0 13.0 %copy-start.24 = (s32[4096]{0:T(1024)S(1)}, s32[4096]{0:T(1024)}, u32[]{:S(2)}) copy-start(s32[4096]{0:T(1024)} %param.16) | copy-start | bytes 49156
  18.0 13.1 %copy-start.5 = (f32[4096,128]{1,0:T(8,128)S(1)}, f32[4096,128]{1,0:T(8,128)}, u32[]{:S(2)}) copy-start(f32[4096,128]{1,0:T(8,128)} %param.15) | copy-start | bytes 6291460
  18.0 69.1 %all-to-all-start.1 = ((bf16[128,64,128]{2,1,0:T(8,128)(2,1)}), bf16[128,64,128]{2,1,0:T(8,128)(2,1)}, u32[]{:S(2)}, u32[]{:S(2)}) async-start(bf16[128,64,128]{2,1,0:T(8,128)(2,1)} %copy-done.6), calls=%async_computation.1 | async-start | bytes 4194304 | tf_op jit(solution)/shard_map/all_to_all | solution.py:282
  23.9 8.9 %collective-permute-start = (f32[64,128]{1,0:T(8,128)S(1)}, f32[64,128]{1,0:T(8,128)S(1)}, u32[]{:S(2)}, u32[]{:S(2)}) collective-permute-start(f32[64,128]{1,0:T(8,128)S(1)} %get-tuple-element.12), channel_id=1, source_target_pairs={{0,1},{1,0},{2,3},{3,2},{4,5},{5,4},{6,7},{7,6},{8,9},{9,8},{10,11... | collective-permute-start | bytes 98312 | tf_op jit(solution)/shard_map/ppermute | solution.py:309
  24.9 50.5 %collective-permute-start.6 = (bf16[2,256,128]{2,1,0:T(8,128)(2,1)}, bf16[2,256,128]{2,1,0:T(8,128)(2,1)S(1)}, u32[]{:S(2)}, u32[]{:S(2)}) collective-permute-start(bf16[2,256,128]{2,1,0:T(8,128)(2,1)} %get-tuple-element.26), channel_id=1, source_target_pairs={{1,0},{2,1},{3,2},{4,3},{5,4},{6,5},{7,6},{8,7},{9,8},{10,9},{11,1... | collective-permute-start | bytes 393224 | tf_op jit(solution)/shard_map/ppermute | solution.py:288
  29.1 49.3 %collective-permute-start.5 = (bf16[2,256,128]{2,1,0:T(8,128)(2,1)}, bf16[2,256,128]{2,1,0:T(8,128)(2,1)S(1)}, u32[]{:S(2)}, u32[]{:S(2)}) collective-permute-start(bf16[2,256,128]{2,1,0:T(8,128)(2,1)} %get-tuple-element.27), channel_id=1, source_target_pairs={{0,1},{1,2},{2,3},{3,4},{4,5},{5,6},{6,7},{7,8},{8,9},{9,10},{10,1... | collective-permute-start | bytes 393224 | tf_op jit(solution)/shard_map/ppermute | solution.py:287
  31.1 1.8 %copy-start.26 = (s32[16,2]{0,1:T(2,128)S(1)}, s32[16,2]{0,1:T(2,128)}, u32[]{:S(2)}) copy-start(s32[16,2]{0,1:T(2,128)} %param.19) | copy-start | bytes 388
  31.1 2.0 %copy-start.25 = (s32[30,4]{0,1:T(4,128)S(1)}, s32[30,4]{0,1:T(4,128)}, u32[]{:S(2)}) copy-start(s32[30,4]{0,1:T(4,128)} %param.25) | copy-start | bytes 1444
  32.8 10.7 %collective-permute-start.1 = (bf16[1,64,128]{2,1,0:T(8,128)(2,1)S(1)}, bf16[1,64,128]{2,1,0:T(8,128)(2,1)S(1)}, u32[]{:S(2)}, u32[]{:S(2)}) collective-permute-start(bf16[1,64,128]{2,1,0:T(8,128)(2,1)S(1)} %get-tuple-element.23), channel_id=1, source_target_pairs={{0,2},{1,3},{2,0},{3,1},{4,6},{5,7},{6,4},{7,5},{8,10},{9,11},{10,... | collective-permute-start | bytes 49160 | tf_op jit(solution)/shard_map/ppermute | solution.py:313
  43.5 4.3 %collective-permute-start.2 = (bf16[2,64,128]{2,1,0:T(8,128)(2,1)S(1)}, bf16[2,64,128]{2,1,0:T(8,128)(2,1)S(1)}, u32[]{:S(2)}, u32[]{:S(2)}) collective-permute-start(bf16[2,64,128]{2,1,0:T(8,128)(2,1)S(1)} %pad_maximum_fusion.4), channel_id=1, source_target_pairs={{0,4},{1,5},{2,6},{3,7},{4,0},{5,1},{6,2},{7,3},{8,12},{9,13},{10,... | collective-permute-start | bytes 98312 | tf_op jit(solution)/shard_map/ppermute | solution.py:313
  47.8 15.4 %collective-permute-start.3 = (bf16[4,64,128]{2,1,0:T(8,128)(2,1)S(1)}, bf16[4,64,128]{2,1,0:T(8,128)(2,1)S(1)}, u32[]{:S(2)}, u32[]{:S(2)}) collective-permute-start(bf16[4,64,128]{2,1,0:T(8,128)(2,1)S(1)} %pad_maximum_fusion.2), channel_id=1, source_target_pairs={{0,8},{1,9},{2,10},{3,11},{4,12},{5,13},{6,14},{7,15},{8,0},{9,1},... | collective-permute-start | bytes 196616 | tf_op jit(solution)/shard_map/ppermute | solution.py:313
  63.3 22.1 %collective-permute-start.4 = (bf16[8,64,128]{2,1,0:T(8,128)(2,1)S(1)}, bf16[8,64,128]{2,1,0:T(8,128)(2,1)S(1)}, u32[]{:S(2)}, u32[]{:S(2)}) collective-permute-start(bf16[8,64,128]{2,1,0:T(8,128)(2,1)S(1)} %pad_maximum_fusion), channel_id=1, source_target_pairs={{0,16},{1,17},{2,18},{3,19},{4,20},{5,21},{6,22},{7,23},{8,24},{9,... | collective-permute-start | bytes 393224 | tf_op jit(solution)/shard_map/ppermute | solution.py:313
  78.4 2.8 %copy-start = (bf16[16,3,256,256]{3,2,1,0:T(8,128)(2,1)S(1)}, bf16[16,3,256,256]{3,2,1,0:T(8,128)(2,1)}, u32[]{:S(2)}) copy-start(bf16[16,3,256,256]{3,2,1,0:T(8,128)(2,1)} %tiles.3) | copy-start | bytes 18874372
  82.4 3.0 %copy-start.13 = (bf16[30,64,256]{2,1,0:T(8,128)(2,1)S(1)}, bf16[30,64,256]{2,1,0:T(8,128)(2,1)}, u32[]{:S(2)}) copy-start(bf16[30,64,256]{2,1,0:T(8,128)(2,1)} %couplings.6) | copy-start | bytes 2949124
  82.4 3.0 %copy-start.18 = (bf16[28,64,64]{2,1,0:T(8,128)(2,1)S(1)}, bf16[28,64,64]{2,1,0:T(8,128)(2,1)}, u32[]{:S(2)}) copy-start(bf16[28,64,64]{2,1,0:T(8,128)(2,1)} %transfer.8) | copy-start | bytes 688132
  85.4 1.7 copy-start.8
  85.4 1.7 copy-start.10
  101.3 10.6 %copy-start.17 = (f32[16,256,128]{2,1,0:T(8,128)S(1)}, f32[16,256,128]{2,1,0:T(8,128)}, u32[]{:S(2)}) copy-start(f32[16,256,128]{2,1,0:T(8,128)} %copy-done.16) | copy-start | bytes 6291460
  101.3 65.0 %all-to-all-start.2 = ((bf16[128,64,128]{2,1,0:T(8,128)(2,1)}), bf16[128,64,128]{2,1,0:T(8,128)(2,1)}, u32[]{:S(2)}, u32[]{:S(2)}) async-start(bf16[128,64,128]{2,1,0:T(8,128)(2,1)} %copy-done.15), calls=%async_computation.2 | async-start | bytes 4194304 | tf_op jit(solution)/shard_map/all_to_all | solution.py:282
  104.7 7.1 %collective-permute-start.7 = (f32[64,128]{1,0:T(8,128)S(1)}, f32[64,128]{1,0:T(8,128)S(1)}, u32[]{:S(2)}, u32[]{:S(2)}) collective-permute-start(f32[64,128]{1,0:T(8,128)S(1)} %get-tuple-element.15), channel_id=1, source_target_pairs={{0,1},{1,0},{2,3},{3,2},{4,5},{5,4},{6,7},{7,6},{8,9},{9,8},{10,11... | collective-permute-start | bytes 98312 | tf_op jit(solution)/shard_map/ppermute | solution.py:309
  105.8 50.0 %collective-permute-start.13 = (bf16[2,256,128]{2,1,0:T(8,128)(2,1)S(1)}, bf16[2,256,128]{2,1,0:T(8,128)(2,1)S(1)}, u32[]{:S(2)}, u32[]{:S(2)}) collective-permute-start(bf16[2,256,128]{2,1,0:T(8,128)(2,1)S(1)} %get-tuple-element.24), channel_id=1, source_target_pairs={{1,0},{2,1},{3,2},{4,3},{5,4},{6,5},{7,6},{8,7},{9,8},{10,9},{11,1... | collective-permute-start | bytes 393224 | tf_op jit(solution)/shard_map/ppermute | solution.py:288
  109.9 49.0 %collective-permute-start.12 = (bf16[2,256,128]{2,1,0:T(8,128)(2,1)S(1)}, bf16[2,256,128]{2,1,0:T(8,128)(2,1)S(1)}, u32[]{:S(2)}, u32[]{:S(2)}) collective-permute-start(bf16[2,256,128]{2,1,0:T(8,128)(2,1)S(1)} %get-tuple-element.25), channel_id=1, source_target_pairs={{0,1},{1,2},{2,3},{3,4},{4,5},{5,6},{6,7},{7,8},{8,9},{9,10},{10,1... | collective-permute-start | bytes 393224 | tf_op jit(solution)/shard_map/ppermute | solution.py:287
  111.8 12.2 %collective-permute-start.8 = (bf16[1,64,128]{2,1,0:T(8,128)(2,1)S(1)}, bf16[1,64,128]{2,1,0:T(8,128)(2,1)S(1)}, u32[]{:S(2)}, u32[]{:S(2)}) collective-permute-start(bf16[1,64,128]{2,1,0:T(8,128)(2,1)S(1)} %get-tuple-element.21), channel_id=1, source_target_pairs={{0,2},{1,3},{2,0},{3,1},{4,6},{5,7},{6,4},{7,5},{8,10},{9,11},{10,... | collective-permute-start | bytes 49160 | tf_op jit(solution)/shard_map/ppermute | solution.py:313
  111.9 47.0 %copy-start.23 = (bf16[16,256,128]{2,1,0:T(8,128)(2,1)S(1)}, bf16[16,256,128]{2,1,0:T(8,128)(2,1)}, u32[]{:S(2)}) copy-start(bf16[16,256,128]{2,1,0:T(8,128)(2,1)} %copy-done.22) | copy-start | bytes 3145732
  124.1 4.3 %collective-permute-start.9 = (bf16[2,64,128]{2,1,0:T(8,128)(2,1)S(1)}, bf16[2,64,128]{2,1,0:T(8,128)(2,1)S(1)}, u32[]{:S(2)}, u32[]{:S(2)}) collective-permute-start(bf16[2,64,128]{2,1,0:T(8,128)(2,1)S(1)} %pad_maximum_fusion.5), channel_id=1, source_target_pairs={{0,4},{1,5},{2,6},{3,7},{4,0},{5,1},{6,2},{7,3},{8,12},{9,13},{10,... | collective-permute-start | bytes 98312 | tf_op jit(solution)/shard_map/ppermute | solution.py:313
  128.3 15.4 %collective-permute-start.10 = (bf16[4,64,128]{2,1,0:T(8,128)(2,1)S(1)}, bf16[4,64,128]{2,1,0:T(8,128)(2,1)S(1)}, u32[]{:S(2)}, u32[]{:S(2)}) collective-permute-start(bf16[4,64,128]{2,1,0:T(8,128)(2,1)S(1)} %pad_maximum_fusion.3), channel_id=1, source_target_pairs={{0,8},{1,9},{2,10},{3,11},{4,12},{5,13},{6,14},{7,15},{8,0},{9,1},... | collective-permute-start | bytes 196616 | tf_op jit(solution)/shard_map/ppermute | solution.py:313
  143.8 20.9 %collective-permute-start.11 = (bf16[8,64,128]{2,1,0:T(8,128)(2,1)S(1)}, bf16[8,64,128]{2,1,0:T(8,128)(2,1)S(1)}, u32[]{:S(2)}, u32[]{:S(2)}) collective-permute-start(bf16[8,64,128]{2,1,0:T(8,128)(2,1)S(1)} %pad_maximum_fusion.1), channel_id=1, source_target_pairs={{0,16},{1,17},{2,18},{3,19},{4,20},{5,21},{6,22},{7,23},{8,24},{9,... | collective-permute-start | bytes 393224 | tf_op jit(solution)/shard_map/ppermute | solution.py:313
  158.9 2.8 %copy-start.1 = (bf16[16,3,256,256]{3,2,1,0:T(8,128)(2,1)S(1)}, bf16[16,3,256,256]{3,2,1,0:T(8,128)(2,1)}, u32[]{:S(2)}) copy-start(bf16[16,3,256,256]{3,2,1,0:T(8,128)(2,1)} %tiles.3) | copy-start | bytes 18874372
  161.7 3.0 %copy-start.14 = (bf16[30,64,256]{2,1,0:T(8,128)(2,1)S(1)}, bf16[30,64,256]{2,1,0:T(8,128)(2,1)}, u32[]{:S(2)}) copy-start(bf16[30,64,256]{2,1,0:T(8,128)(2,1)} %couplings.6) | copy-start | bytes 2949124
  161.7 3.0 %copy-start.19 = (bf16[28,64,64]{2,1,0:T(8,128)(2,1)S(1)}, bf16[28,64,64]{2,1,0:T(8,128)(2,1)}, u32[]{:S(2)}) copy-start(bf16[28,64,64]{2,1,0:T(8,128)(2,1)} %transfer.8) | copy-start | bytes 688132
  (12 other events, 15.5 us)

commit v2 on v1

v2 whole, which is shorter than its diff:
```python
import functools

import jax
import jax.numpy as jnp
import numpy as np
from jax import lax
from jax.experimental import pallas as pl
from jax.experimental.pallas import tpu as pltpu
from jax.sharding import PartitionSpec as P

REACH = 2
STEP_SIZE = 0.5
MIB = 1 << 20
F32 = jnp.float32
BF16 = jnp.bfloat16


def rows_dot(left, right):
    return lax.dot_general(left, right, (((0,), (0,)), ((), ())), preferred_element_type=F32)


def dot(left, right):
    return jnp.dot(left, right, preferred_element_type=F32)


def pair_rows(ref, first):
    both = ref[pl.ds(first, 2)]
    return both.reshape(2 * both.shape[1], both.shape[2])


def tree_rows(per_dev):
    counts = [per_dev >> height for height in range(per_dev.bit_length())]
    starts = [sum(counts[:height]) for height in range(len(counts))]
    return counts, starts


def go_up(coef, transfer, per_dev):
    counts, starts = tree_rows(per_dev)
    for height in range(1, len(counts)):
        for node in range(counts[height]):
            kids = starts[height - 1] + 2 * node
            coef[starts[height] + node] = rows_dot(
                pair_rows(transfer, kids), pair_rows(coef, kids)
            ).astype(BF16)


def go_down(field, coupled, transfer, parent, per_dev):
    counts, starts = tree_rows(per_dev)
    top = starts[-1]
    field[top] = (coupled[top] + dot(transfer[top], parent)).astype(BF16)
    for height in range(len(counts) - 2, -1, -1):
        for node in range(counts[height + 1]):
            kids = starts[height] + 2 * node
            pushed = dot(pair_rows(transfer, kids), field[starts[height + 1] + node])
            both = pair_rows(coupled, kids) + pushed
            field[pl.ds(kids, 2)] = both.reshape(2, -1, both.shape[1]).astype(BF16)


def chunks(total, size):
    return [(low, min(size, total - low)) for low in range(0, total, size)]


class Mover:
    def __init__(self, sems):
        self.sems = sems
        self.used = 0

    def start(self, source, target):
        copy = pltpu.make_async_copy(source, target, self.sems.at[self.used])
        self.used += 1
        copy.start()
        return copy


LEAVES = 8


def first_kernel(per_dev, weights, basis, transfer, coef, top_part, wbuf, bbuf, tbuf, sems):
    mover = Mover(sems)
    parts = chunks(per_dev, LEAVES)
    basis_in = mover.start(basis, bbuf)
    arriving = [mover.start(weights.at[pl.ds(*part)], wbuf.at[pl.ds(*part)]) for part in parts]
    transfer_in = mover.start(transfer, tbuf)
    basis_in.wait()
    for (low, size), copy in zip(parts, arriving):
        copy.wait()
        for leaf in range(low, low + size):
            coef[leaf] = dot(bbuf[leaf], wbuf[leaf].astype(BF16)).astype(BF16)
    transfer_in.wait()
    go_up(coef, tbuf, per_dev)
    top = coef.shape[0] - 1
    top_part[...] = rows_dot(tbuf[top], coef[top])


def pick(mover, chosen, coef, buffer, payload):
    leaving = []
    total, width = payload.shape[0], chosen.shape[2]
    for low, size in chunks(total, max(total // 2, 1)):
        for slot in range(low, low + size):
            buffer[slot] = coef[chosen[slot // width, 0, slot % width]]
        rows = pl.ds(low, size)
        leaving.append(mover.start(buffer.at[rows], payload.at[rows]))
    return leaving


def pick_kernel(chosen, coef, payload, buffer, sems):
    for copy in pick(Mover(sems), chosen, coef, buffer, payload):
        copy.wait()


def near_kernel(ids, own, tiles, out, padded):
    step = pl.program_id(0)
    block = tiles.shape[0]
    inner = own.shape[0]

    @pl.when(step == 0)
    def _():
        nothing = jnp.zeros((REACH,) + own.shape[1:], BF16)
        padded[pl.ds(0, REACH)] = nothing
        padded[pl.ds(REACH, inner)] = own[...]
        padded[pl.ds(REACH + inner, REACH)] = nothing

    for leaf in range(block):
        row = step * block + leaf
        out[leaf] = (
            dot(tiles[leaf, 0], padded[row + REACH])
            + dot(tiles[leaf, 1], padded[ids[2 * row]])
            + dot(tiles[leaf, 2], padded[ids[2 * row + 1]])
        )


def join_kernel(first, second, *rest):
    joined = rest[-1]
    size = first.shape[0]
    joined[pl.ds(0, size)] = first[...]
    joined[pl.ds(size, size)] = second[...]


def edge_scores(ids, leaf, tiles, halo, per_dev):
    total = None
    for member in range(2):
        row = ids[2 * leaf + member]
        place = jnp.where(row < REACH, row, jnp.where(row < REACH + per_dev, 2 * REACH, row - per_dev))
        term = dot(tiles[member], halo[place])
        total = term if total is None else total + term
    return total


def coarse_parent(devices, order, mine, listed, halves, transfer, couplings, coef):
    levels = devices.bit_length() - 2
    links = couplings.shape[2] // couplings.shape[1]
    offsets = [devices - (devices >> level - 1) for level in range(1, levels + 1)]
    depth = halves[0].shape[1]
    for turn, half in enumerate(halves):
        rows = pl.ds(pl.multiple_of(jnp.bitwise_xor(mine & 1, turn) * depth, depth), depth)
        for place in range(devices // 2):
            coef[jnp.bitwise_xor(mine >> 1, order[place]), rows] = half[place]
    for level in range(1, levels):
        for node in range(devices >> level + 1):
            kids = offsets[level - 1] + 2 * node
            coef[offsets[level] + node] = rows_dot(
                pair_rows(transfer, kids), pair_rows(coef, kids)
            ).astype(BF16)
    field = None
    for level in range(levels, 0, -1):
        offset = offsets[level - 1]
        node = offset + (mine >> level)
        blocks = jnp.concatenate(
            [coef[offset + listed[node * links + link]] for link in range(links)], axis=0
        )
        term = dot(couplings[level - 1], blocks)
        if level < levels:
            term = term + dot(transfer[node], field)
        field = term.astype(BF16)
    return field


def finish_kernel(
    devices,
    order,
    per_dev,
    last,
    me,
    listed,
    landing,
    chosen,
    ids,
    incoming,
    couplings,
    transfer,
    half,
    other_half,
    coarse_transfer,
    coarse_couplings,
    near,
    base,
    basis,
    before,
    after,
    tiles,
    *rest,
):
    if last:
        new_out, scores_out = rest[:2]
        rest = rest[2:]
    else:
        payload, new_out, values_out, top_part = rest[:4]
        rest = rest[4:]
        coef, buffer, values = rest[-4:-1]
    inbuf, cbuf, tbuf, nbuf, abuf, bbuf, halo, edge_tiles, field, coupled = rest[:10]
    coarse_maps, coarse_mats, coarse_coef = rest[10:13]
    sems = rest[-1]
    mine = me[0]
    nodes = couplings.shape[0]
    links = couplings.shape[2] // couplings.shape[1]
    mover = Mover(sems)
    low_edge, high_edge = pl.ds(0, REACH), pl.ds(per_dev - REACH, REACH)
    others = pl.ds(1, 2)
    coarse_in = [mover.start(coarse_transfer, coarse_maps)]
    for level in range(1, coarse_mats.shape[0] + 1):
        node = devices - (devices >> level - 1) + (mine >> level)
        coarse_in.append(mover.start(coarse_couplings.at[node], coarse_mats.at[level - 1]))
    blocks_in, mats_in, maps_in, *leaves_in = [
        mover.start(*pair)
        for pair in (
            (incoming, inbuf),
            (couplings, cbuf),
            (transfer, tbuf),
            (before, halo.at[pl.ds(0, REACH)]),
            (after, halo.at[pl.ds(REACH, REACH)]),
            (tiles.at[low_edge, others], edge_tiles.at[pl.ds(0, REACH)]),
            (tiles.at[high_edge, others], edge_tiles.at[pl.ds(REACH, REACH)]),
            (basis, bbuf),
            (near, nbuf),
            (base, abuf),
        )
    ]
    halo[2 * REACH] = jnp.zeros(halo.shape[1:], BF16)
    for copy in coarse_in:
        copy.wait()
    parent = coarse_parent(
        devices, order, mine, listed, (half, other_half), coarse_maps, coarse_mats, coarse_coef
    )
    blocks_in.wait()
    mats_in.wait()
    for node in range(nodes - 1, -1, -1):
        blocks = jnp.concatenate(
            [inbuf[landing[node * links + link]] for link in range(links)], axis=0
        )
        coupled[node] = dot(cbuf[node], blocks)
    maps_in.wait()
    go_down(field, coupled, tbuf, parent, per_dev)
    leaving = []
    for copy in leaves_in:
        copy.wait()
    for low, size in chunks(per_dev, LEAVES):
        rows = pl.ds(low, size)
        for leaf in range(low, low + size):
            scores = nbuf[leaf] + rows_dot(bbuf[leaf], field[leaf])
            edge = leaf if leaf < REACH else leaf - (per_dev - 2 * REACH)
            if leaf < REACH or leaf >= per_dev - REACH:
                scores = scores + edge_scores(ids, leaf, edge_tiles.at[edge], halo, per_dev)
            new = abuf[leaf] - gradient(scores)
            abuf[leaf] = new
            if last:
                nbuf[leaf] = scores
            else:
                rounded = new.astype(BF16)
                values[leaf] = rounded
                coef[leaf] = dot(bbuf[leaf], rounded).astype(BF16)
        if last:
            leaving.append(mover.start(nbuf.at[rows], scores_out.at[rows]))
        else:
            leaving.append(mover.start(values.at[rows], values_out.at[rows]))
        leaving.append(mover.start(abuf.at[rows], new_out.at[rows]))
    if not last:
        go_up(coef, tbuf, per_dev)
        leaving += pick(mover, chosen, coef, buffer, payload)
        top_part[...] = rows_dot(tbuf[nodes - 1], coef[nodes - 1])
    for copy in leaving:
        copy.wait()


def gradient(scores):
    return (0.5 * STEP_SIZE) * (1.0 + jnp.tanh(0.5 * scores))


def shifted(new, labels, classes):
    marks = lax.broadcasted_iota(jnp.int32, (classes, labels.shape[1]), 0) == labels
    eye = lax.broadcasted_iota(jnp.int32, (classes, classes), 0) == lax.broadcasted_iota(
        jnp.int32, (classes, classes), 1
    )
    return new + STEP_SIZE * rows_dot(marks.astype(BF16), eye.astype(BF16))


def shift_kernel(new, labels, base):
    for leaf in range(new.shape[0]):
        base[leaf] = shifted(new[leaf], labels[leaf], new.shape[2])


def whole(shape):
    return pl.BlockSpec(shape, lambda i, *_: (0,) * len(shape), pipeline_mode=pl.Buffered(1))


def whole_out(shape):
    return pl.BlockSpec(shape, lambda i, *_: (0,) * len(shape))


def per_step(block, shape):
    return pl.BlockSpec((block,) + tuple(shape[1:]), lambda i, *_: (i,) + (0,) * (len(shape) - 1))


def params(limit):
    return pltpu.CompilerParams(
        dimension_semantics=("arbitrary",), vmem_limit_bytes=limit * MIB
    )


def cost(flops, moved):
    return pl.CostEstimate(flops=int(flops), bytes_accessed=int(moved), transcendentals=0)


def plan(sources, devices, per_dev, capacity):
    counts, starts = tree_rows(per_dev)
    links = sources.shape[1]
    heights = np.repeat(np.arange(len(counts)), np.array(counts) * links)
    shift = jnp.asarray((len(counts) - 1 - heights).astype(np.int32))
    start = jnp.asarray(np.array(starts)[heights].astype(np.int32))
    mask = jnp.asarray((np.array(counts)[heights] - 1).astype(np.int32))
    flat = sources.reshape(-1)
    owner = flat >> shift
    row = start + (flat & mask)
    width = flat.shape[0]
    earlier = jnp.asarray(np.tril(np.ones((width, width), dtype=bool), -1))
    rank = jnp.sum(((owner[:, None] == owner[None, :]) & earlier).astype(jnp.int32), axis=1)
    landing = owner * capacity + rank
    slots = jnp.arange(devices * capacity, dtype=jnp.int32)
    wanted = jnp.sum(jnp.where(landing[None, :] == slots[:, None], row[None, :], 0), axis=1)
    chosen = lax.all_to_all(
        wanted.reshape(devices, 1, capacity), "leaf", split_axis=0, concat_axis=0, tiled=True
    )
    return landing, chosen


def local(
    weights,
    labels,
    basis,
    near_tiles,
    near_ids,
    transfer,
    couplings,
    sources,
    coarse_transfer,
    coarse_couplings,
    coarse_sources,
):
    devices = lax.axis_size("leaf")
    me = lax.axis_index("leaf")
    per_dev, rank_dim, leaf_size = basis.shape
    classes = weights.shape[1]
    nodes = transfer.shape[0]
    links = sources.shape[1]
    capacity = nodes * links // devices + 1
    slots = devices * capacity
    block = next(size for size in (4, 2, 1) if per_dev % size == 0)
    steps = per_dev // block
    node_shape = (rank_dim, classes)
    leaf_shape = (per_dev, leaf_size, classes)
    weights3 = weights.reshape(leaf_shape)
    offset_ids = (near_ids - (me * per_dev - REACH)).reshape(-1)

    landing, chosen = plan(sources, devices, per_dev, capacity)
    coef_shape = (nodes,) + node_shape
    payload_shape = pltpu.HBM((slots,) + node_shape, BF16)
    smem = pl.BlockSpec(memory_space=pltpu.SMEM)
    vmem = pl.BlockSpec(memory_space=pltpu.VMEM)
    hbm = pl.BlockSpec(memory_space=pltpu.HBM)

    coef, top_part = pl.pallas_call(
        functools.partial(first_kernel, per_dev),
        in_specs=[hbm, hbm, hbm],
        out_specs=[vmem, vmem],
        out_shape=[pltpu.VMEM(coef_shape, BF16), jax.ShapeDtypeStruct(node_shape, F32)],
        scratch_shapes=[
            pltpu.VMEM(leaf_shape, F32),
            pltpu.VMEM(basis.shape, BF16),
            pltpu.VMEM(transfer.shape, BF16),
            pltpu.SemaphoreType.DMA((2 * per_dev + 1,)),
        ],
        compiler_params=pltpu.CompilerParams(vmem_limit_bytes=60 * MIB),
        cost_estimate=cost(2 * basis.size * classes, 4 * weights.size),
        name="leaf_coefs",
    )(weights3, basis, transfer)
    payload = pl.pallas_call(
        pick_kernel,
        in_specs=[smem, vmem],
        out_specs=hbm,
        out_shape=payload_shape,
        scratch_shapes=[
            pltpu.VMEM(payload_shape.shape, BF16),
            pltpu.SemaphoreType.DMA((8,)),
        ],
        compiler_params=pltpu.CompilerParams(vmem_limit_bytes=60 * MIB),
        cost_estimate=cost(0, 4 * slots * rank_dim * classes),
        name="pick_rows",
    )(chosen, coef)

    def exchange(payload):
        return lax.all_to_all(payload, "leaf", split_axis=0, concat_axis=0, tiled=True)

    halo_shape = (REACH, leaf_size, classes)

    def halo_of(values):
        up = [(i, i + 1) for i in range(devices - 1)]
        down = [(j, i) for i, j in up]
        before = lax.ppermute(values[per_dev - REACH :], "leaf", up)
        after = lax.ppermute(values[:REACH], "leaf", down)
        return before, after

    def near_field(values):
        return pl.pallas_call(
            near_kernel,
            grid=(steps,),
            in_specs=[smem, whole(leaf_shape), per_step(block, near_tiles.shape)],
            out_specs=per_step(block, leaf_shape),
            out_shape=jax.ShapeDtypeStruct(leaf_shape, F32),
            scratch_shapes=[pltpu.VMEM((per_dev + 2 * REACH, leaf_size, classes), BF16)],
            compiler_params=params(16),
            cost_estimate=cost(2 * near_tiles.size * classes, 2 * near_tiles.size),
            name="near_field",
        )(offset_ids, values, near_tiles)

    def with_labels(new):
        return pl.pallas_call(
            shift_kernel,
            grid=(steps,),
            in_specs=[per_step(block, leaf_shape), per_step(block, labels3.shape)],
            out_specs=per_step(block, leaf_shape),
            out_shape=jax.ShapeDtypeStruct(leaf_shape, F32),
            compiler_params=params(16),
            cost_estimate=cost(0, 8 * weights.size),
            name="with_labels",
        )(new, labels3)

    def join(first, second, ahead):
        return pl.pallas_call(
            join_kernel,
            in_specs=[vmem, vmem] + [hbm] * len(ahead),
            out_specs=vmem,
            out_shape=jax.ShapeDtypeStruct((2 * first.shape[0],) + first.shape[1:], BF16),
            compiler_params=pltpu.CompilerParams(vmem_limit_bytes=16 * MIB),
            cost_estimate=cost(0, 4 * first.size),
            name="join_rows",
        )(first, second, *ahead)

    def coarse_rows(top_part, ahead):
        swap = [(i, i ^ 1) for i in range(devices)]
        depth = rank_dim // 2
        core = me & 1
        kept = lax.dynamic_slice_in_dim(top_part, core * depth, depth, axis=0)
        given = lax.dynamic_slice_in_dim(top_part, (1 - core) * depth, depth, axis=0)
        gathered = (kept + lax.ppermute(given, "leaf", swap)).astype(BF16)[None]
        order, hop = [0], 2
        while hop < devices:
            arrived = lax.ppermute(gathered, "leaf", [(i, i ^ hop) for i in range(devices)])
            if 4 * hop == devices:
                gathered = join(gathered, arrived, ahead)
            else:
                gathered = jnp.concatenate([gathered, arrived], axis=0)
            order = order + [place ^ (hop // 2) for place in order]
            hop *= 2
        return order, (gathered, lax.ppermute(gathered, "leaf", swap))

    def finish(incoming, order, halves, near, base, halos, last):
        coarse_levels = devices.bit_length() - 2
        leaf_out = pltpu.HBM(leaf_shape, F32)
        scratch = [
            pltpu.VMEM(payload_shape.shape, BF16),
            pltpu.VMEM(couplings.shape, BF16),
            pltpu.VMEM(transfer.shape, BF16),
            pltpu.VMEM(leaf_shape, F32),
            pltpu.VMEM(leaf_shape, F32),
            pltpu.VMEM(basis.shape, BF16),
            pltpu.VMEM((2 * REACH + 1, leaf_size, classes), BF16),
            pltpu.VMEM((2 * REACH, 2) + near_tiles.shape[2:], BF16),
            pltpu.VMEM(coef_shape, BF16),
            pltpu.VMEM(coef_shape, F32),
            pltpu.VMEM(coarse_transfer.shape, BF16),
            pltpu.VMEM((coarse_levels,) + coarse_couplings.shape[1:], BF16),
            pltpu.VMEM((coarse_couplings.shape[0],) + node_shape, BF16),
        ]
        if last:
            out_shape, out_specs = [leaf_out, leaf_out], [hbm, hbm]
        else:
            out_shape = [
                payload_shape,
                leaf_out,
                pltpu.HBM(leaf_shape, BF16),
                jax.ShapeDtypeStruct(node_shape, F32),
            ]
            out_specs = [hbm, hbm, hbm, vmem]
            scratch += [
                pltpu.VMEM(coef_shape, BF16),
                pltpu.VMEM(payload_shape.shape, BF16),
                pltpu.VMEM(leaf_shape, BF16),
            ]
        scratch.append(pltpu.SemaphoreType.DMA((2 * per_dev + devices,)))
        return pl.pallas_call(
            functools.partial(finish_kernel, devices, order, per_dev, last),
            in_specs=[smem] * 5 + [hbm] * 3 + [vmem] * 2 + [hbm] * 8,
            out_specs=out_specs,
            scratch_shapes=scratch,
            out_shape=out_shape,
            compiler_params=pltpu.CompilerParams(vmem_limit_bytes=60 * MIB),
            cost_estimate=cost(2 * couplings.size * classes, 12 * weights.size),
            name="last_scores" if last else "first_scores",
        )(
            me.reshape(1),
            coarse_sources.reshape(-1),
            landing,
            chosen,
            offset_ids,
            incoming,
            couplings,
            transfer,
            *halves,
            coarse_transfer,
            coarse_couplings,
            near,
            base,
            basis,
            *halos,
            near_tiles,
        )

    labels3 = labels.reshape(per_dev, 1, leaf_size)
    values = weights3.astype(BF16)
    halos = halo_of(values)
    incoming = exchange(payload)
    near = near_field(values)
    base = with_labels(weights3)
    rows = coarse_rows(top_part, (near, base))
    payload, middle, values, top_part = finish(incoming, *rows, near, base, halos, False)
    halos = halo_of(values)
    incoming = exchange(payload)
    near = near_field(values)
    base = with_labels(middle)
    rows = coarse_rows(top_part, (near, base))
    updated, second_scores = finish(incoming, *rows, near, base, halos, True)
    return updated.reshape(weights.shape), second_scores.reshape(weights.shape)


def solution(mesh):
    in_specs = (
        P("leaf", None),
        P("leaf"),
        P("leaf", None, None),
        P("leaf", None, None, None),
        P("leaf", None),
        P("leaf", None, None),
        P("leaf", None, None),
        P("leaf", None),
        P(),
        P(),
        P(),
    )
    out_specs = (P("leaf", None), P("leaf", None))
    return jax.shard_map(local, mesh=mesh, in_specs=in_specs, out_specs=out_specs, check_vma=False)
```

time: 176 us -> 156 us (0.89)
  waiting for transfers between devices: 81.1 us -> 62.9 us
  local copies, waits for them, and re-layouts: 25 us -> 10.5 us
  Pallas kernels: 25.2 us -> 33.9 us
  starting transfers between devices: 37 us -> 44.2 us
  other arithmetic: 5.88 us -> 1.99 us
    ppermute x14 -> x16, waiting for transfers between devices: 81.1 us -> 62.3 us  [the longest x8 52.1 us: coarse_rows(): lax.ppermute(gathered, 'leaf', [(i, i ^ hop) for i in range(devices)])]
    unnamed x61 -> x57, local copies, waits for them, and re-layouts: 21.2 us -> 8.53 us
    pallas_call x8 -> x10, Pallas kernels: 25.2 us -> 33.9 us  [the longest x2 19.6 us: finish(): pl.pallas_call(functools.partial(finish_kernel, devices, order, per_dev,...]
    ppermute x14 -> x16, starting transfers between devices: 21.8 us -> 28.6 us  [the longest x8 16.7 us: coarse_rows(): lax.ppermute(gathered, 'leaf', [(i, i ^ hop) for i in range(devices)])]
    add x2 -> x0, other arithmetic: 3.35 us -> none  [the longest x1 1.68 us: local(): weights3 + shift_up]
  transfers between devices with their start and end apart: 17 -> 19, of which waited for: 10 -> 15; matrix products, arithmetic and copies ran while one was open for 3% -> 1% of each run, Pallas kernels for 6% -> 8%
where the time goes in v2:
time: 156 us; the launch traced here: 155 us
  waiting for transfers between devices  62.9 us (40%)
  starting transfers between devices  44.2 us (28%)
  Pallas kernels  33.9 us (22%)
  local copies, waits for them, and re-layouts  10.5 us (7%)
  other arithmetic  1.99 us (1%)
    ppermute x8, waiting for transfers between devices, coarse_rows(): lax.ppermute(gathered, 'leaf', [(i, i ^ hop) for i in range(devices)])  52.1 us
    pallas_call x2, Pallas kernels, finish(): pl.pallas_call(functools.partial(finish_kernel, devices, order, per_dev,...  19.6 us
    ppermute x8, starting transfers between devices, coarse_rows(): lax.ppermute(gathered, 'leaf', [(i, i ^ hop) for i in range(devices)])  16.7 us
    all_to_all x2, starting transfers between devices, exchange(): lax.all_to_all(payload, 'leaf', split_axis=0, concat_axis=0, tiled=True)  9.64 us
    unnamed x57, local copies, waits for them, and re-layouts  8.53 us
    ppermute x2, starting transfers between devices, halo_of(): after = lax.ppermute(values[:REACH], 'leaf', down)  7.5 us
    ppermute x2, waiting for transfers between devices, halo_of(): before = lax.ppermute(values[per_dev - REACH:], 'leaf', up)  6.26 us
    all_to_all x1, starting transfers between devices, plan(): lax.all_to_all(wanted.reshape(devices, 1, capacity), 'leaf', split_axis=0...  5.93 us
  transfers between devices with their start and end apart: 19, of which 15 were waited for; matrix products, arithmetic and copies ran while one was open for 1% of the time, Pallas kernels for 8%

profile of v2, /device:TPU:16, one launch (start us, length us, event | category | flops | bytes accessed | tf_op | source)
XLA Modules:
  0.0 154.6 jit_solution(5193081126265047821)
XLA Ops:
  3.5 5.9 %all-to-all-start = ((s32[32,1,4]{2,1,0:T(1,128)}), s32[32,1,4]{2,1,0:T(1,128)S(1)}, u32[]{:S(2)}, u32[]{:S(2)}) async-start(s32[32,1,4]{2,1,0:T(1,128)} %bitcast.1), calls=%async_computation | async-start | bytes 32768 | tf_op jit(solution)/shard_map/all_to_all | solution.py:339
  9.5 3.6 %leaf_coefs.1 = (bf16[31,64,128]{2,1,0:T(8,128)(2,1)S(1)}, f32[64,128]{1,0:T(8,128)}) custom-call(f32[16,256,128]{2,1,0:T(8,128)} %bitcast.10, bf16[16,64,256]{2,1,0:T(8,128)(2,1)} %basis.5, bf16[31,64,64]{2,1,0:T(8,128)(2,1)} %transfer.5), custom_call_target="tpu_custom_call" | custom-call | flops 67108864 | bytes 2097152 | tf_op jit(solution)/shard_map/leaf_coefs/pallas_call | solution.py:380
  15.1 2.5 %pick_rows.1 = bf16[128,64,128]{2,1,0:T(8,128)(2,1)} custom-call(s32[32,1,4]{2,1,0:T(1,128)} %copy-done.16, bf16[31,64,128]{2,1,0:T(8,128)(2,1)} %copy-done.10), custom_call_target="tpu_custom_call" | custom-call | bytes 4194304 | tf_op jit(solution)/shard_map/pick_rows/pallas_call | solution.py:395
  17.6 5.6 %all-to-all-start.1 = ((bf16[128,64,128]{2,1,0:T(8,128)(2,1)}), bf16[128,64,128]{2,1,0:T(8,128)(2,1)}, u32[]{:S(2)}, u32[]{:S(2)}) async-start(bf16[128,64,128]{2,1,0:T(8,128)(2,1)} %pick_rows.1), calls=%async_computation.1 | async-start | bytes 4194304 | tf_op jit(solution)/shard_map/all_to_all | solution.py:410
  24.6 1.5 collective-permute-start.1
  26.0 9.9 %collective-permute-done.1 = bf16[1,32,128]{2,1,0:T(8,128)(2,1)S(1)} collective-permute-done((bf16[1,32,128]{2,1,0:T(8,128)(2,1)S(1)}, bf16[1,32,128]{2,1,0:T(8,128)(2,1)S(1)}, u32[]{:S(2)}, u32[]{:S(2)}) %collective-permute-start.1) | collective-permute-done | bytes 8224 | tf_op jit(solution)/shard_map/ppermute | solution.py:466
  35.9 2.8 %collective-permute-start.2 = (bf16[2,32,128]{2,1,0:T(8,128)(2,1)S(1)}, bf16[2,32,128]{2,1,0:T(8,128)(2,1)S(1)}, u32[]{:S(2)}, u32[]{:S(2)}) collective-permute-start(bf16[2,32,128]{2,1,0:T(8,128)(2,1)S(1)} %pad_maximum_fusion.4), channel_id=1, source_target_pairs={{0,4},{1,5},{2,6},{3,7},{4,0},{5,1},{6,2},{7,3},{8,12},{9,13},{10,... | collective-permute-start | bytes 49160 | tf_op jit(solution)/shard_map/ppermute | solution.py:466
  39.0 2.6 %collective-permute-done.2 = bf16[2,32,128]{2,1,0:T(8,128)(2,1)S(1)} collective-permute-done((bf16[2,32,128]{2,1,0:T(8,128)(2,1)S(1)}, bf16[2,32,128]{2,1,0:T(8,128)(2,1)S(1)}, u32[]{:S(2)}, u32[]{:S(2)}) %collective-permute-start.2) | collective-permute-done | bytes 16416 | tf_op jit(solution)/shard_map/ppermute | solution.py:466
  41.7 3.4 %collective-permute-start.3 = (bf16[4,32,128]{2,1,0:T(8,128)(2,1)S(1)}, bf16[4,32,128]{2,1,0:T(8,128)(2,1)S(1)}, u32[]{:S(2)}, u32[]{:S(2)}) collective-permute-start(bf16[4,32,128]{2,1,0:T(8,128)(2,1)S(1)} %pad_maximum_fusion.2.first), channel_id=1, source_target_pairs={{0,8},{1,9},{2,10},{3,11},{4,12},{5,13},{6,14},{7,15},{8,0},{9,1},... | collective-permute-start | bytes 98312 | tf_op jit(solution)/shard_map/ppermute | solution.py:466
  45.1 2.8 %copy-done = bf16[16,3,256,256]{3,2,1,0:T(8,128)(2,1)S(1)} copy-done((bf16[16,3,256,256]{3,2,1,0:T(8,128)(2,1)S(1)}, bf16[16,3,256,256]{3,2,1,0:T(8,128)(2,1)}, u32[]{:S(2)}) %copy-start) | copy-done | bytes 6291480
  47.9 3.0 %near_field.2.rest_0_.near = f32[16,256,128]{2,1,0:T(8,128)S(1)} custom-call(s32[32]{0:T(128)S(1)} %reshape.41.ids, bf16[16,256,128]{2,1,0:T(8,128)(2,1)S(1)} %convert_element_type.14.own, bf16[16,3,256,256]{3,2,1,0:T(8,128)(2,1)S(1)} %copy-done), custom_call_target="tpu_custom_call" | custom-call | flops 805306368 | bytes 6291456 | tf_op jit(solution)/shard_map/near_field/pallas_call | solution.py:422
  52.0 8.4 %collective-permute-done.3.second = bf16[4,32,128]{2,1,0:T(8,128)(2,1)S(1)} collective-permute-done((bf16[4,32,128]{2,1,0:T(8,128)(2,1)S(1)}, bf16[4,32,128]{2,1,0:T(8,128)(2,1)S(1)}, u32[]{:S(2)}, u32[]{:S(2)}) %collective-permute-start.3) | collective-permute-done | bytes 32800 | tf_op jit(solution)/shard_map/ppermute | solution.py:466
  60.6 3.8 %collective-permute-start.7 = (bf16[2,256,128]{2,1,0:T(8,128)(2,1)S(1)}, bf16[2,256,128]{2,1,0:T(8,128)(2,1)S(1)}, u32[]{:S(2)}, u32[]{:S(2)}) collective-permute-start(bf16[2,256,128]{2,1,0:T(8,128)(2,1)S(1)} %get-tuple-element.20), channel_id=1, source_target_pairs={{1,0},{2,1},{3,2},{4,3},{5,4},{6,5},{7,6},{8,7},{9,8},{10,9},{11,1... | collective-permute-start | bytes 393224 | tf_op jit(solution)/shard_map/ppermute | solution.py:418
  64.4 1.9 %collective-permute-start.6 = (bf16[2,256,128]{2,1,0:T(8,128)(2,1)S(1)}, bf16[2,256,128]{2,1,0:T(8,128)(2,1)S(1)}, u32[]{:S(2)}, u32[]{:S(2)}) collective-permute-start(bf16[2,256,128]{2,1,0:T(8,128)(2,1)S(1)} %get-tuple-element.21), channel_id=1, source_target_pairs={{0,1},{1,2},{2,3},{3,4},{4,5},{5,6},{6,7},{7,8},{8,9},{9,10},{10,1... | collective-permute-start | bytes 393224 | tf_op jit(solution)/shard_map/ppermute | solution.py:417
  66.3 5.5 %collective-permute-done.4 = bf16[8,32,128]{2,1,0:T(8,128)(2,1)S(1)} collective-permute-done((bf16[8,32,128]{2,1,0:T(8,128)(2,1)S(1)}, bf16[8,32,128]{2,1,0:T(8,128)(2,1)S(1)}, u32[]{:S(2)}, u32[]{:S(2)}) %collective-permute-start.4) | collective-permute-done | bytes 65568 | tf_op jit(solution)/shard_map/ppermute | solution.py:466
  73.3 3.1 %collective-permute-done.6.before = bf16[2,256,128]{2,1,0:T(8,128)(2,1)S(1)} collective-permute-done((bf16[2,256,128]{2,1,0:T(8,128)(2,1)S(1)}, bf16[2,256,128]{2,1,0:T(8,128)(2,1)S(1)}, u32[]{:S(2)}, u32[]{:S(2)}) %collective-permute-start.6) | collective-permute-done | bytes 131104 | tf_op jit(solution)/shard_map/ppermute | solution.py:417
  77.1 11.5 %first_scores.1 = (bf16[128,64,128]{2,1,0:T(8,128)(2,1)}, f32[16,256,128]{2,1,0:T(8,128)}, bf16[16,256,128]{2,1,0:T(8,128)(2,1)}, f32[64,128]{1,0:T(8,128)}) custom-call(s32[1]{0:T(128)} %bitcast.me, s32[120]{0:T(128)} %reshape.38.listed, s32[124]{0:T(128)} %copy-done.25, s32[32,1,4]{2,1,0:T(1,128)} %copy-done.16, s32[32]{0:T(128)} %copy-done.12, ...), custom_call_target="tpu_custom_call" | custom-call | flops 130023424 | bytes 6291456 | tf_op jit(solution)/shard_map/first_scores/pallas_call | solution.py:509
  88.6 4.0 %all-to-all-start.2 = ((bf16[128,64,128]{2,1,0:T(8,128)(2,1)}), bf16[128,64,128]{2,1,0:T(8,128)(2,1)}, u32[]{:S(2)}, u32[]{:S(2)}) async-start(bf16[128,64,128]{2,1,0:T(8,128)(2,1)} %get-tuple-element.12), calls=%async_computation.2 | async-start | bytes 4194304 | tf_op jit(solution)/shard_map/all_to_all | solution.py:410
  93.9 1.5 collective-permute-start.9
  95.4 9.9 %collective-permute-done.9 = bf16[1,32,128]{2,1,0:T(8,128)(2,1)S(1)} collective-permute-done((bf16[1,32,128]{2,1,0:T(8,128)(2,1)S(1)}, bf16[1,32,128]{2,1,0:T(8,128)(2,1)S(1)}, u32[]{:S(2)}, u32[]{:S(2)}) %collective-permute-start.9) | collective-permute-done | bytes 8224 | tf_op jit(solution)/shard_map/ppermute | solution.py:466
  105.2 2.7 %collective-permute-start.10 = (bf16[2,32,128]{2,1,0:T(8,128)(2,1)S(1)}, bf16[2,32,128]{2,1,0:T(8,128)(2,1)S(1)}, u32[]{:S(2)}, u32[]{:S(2)}) collective-permute-start(bf16[2,32,128]{2,1,0:T(8,128)(2,1)S(1)} %pad_maximum_fusion.5), channel_id=1, source_target_pairs={{0,4},{1,5},{2,6},{3,7},{4,0},{5,1},{6,2},{7,3},{8,12},{9,13},{10,... | collective-permute-start | bytes 49160 | tf_op jit(solution)/shard_map/ppermute | solution.py:466
  107.9 1.9 %collective-permute-done.10 = bf16[2,32,128]{2,1,0:T(8,128)(2,1)S(1)} collective-permute-done((bf16[2,32,128]{2,1,0:T(8,128)(2,1)S(1)}, bf16[2,32,128]{2,1,0:T(8,128)(2,1)S(1)}, u32[]{:S(2)}, u32[]{:S(2)}) %collective-permute-start.10) | collective-permute-done | bytes 16416 | tf_op jit(solution)/shard_map/ppermute | solution.py:466
  109.7 4.7 %collective-permute-start.11 = (bf16[4,32,128]{2,1,0:T(8,128)(2,1)S(1)}, bf16[4,32,128]{2,1,0:T(8,128)(2,1)S(1)}, u32[]{:S(2)}, u32[]{:S(2)}) collective-permute-start(bf16[4,32,128]{2,1,0:T(8,128)(2,1)S(1)} %pad_maximum_fusion.3.first), channel_id=1, source_target_pairs={{0,8},{1,9},{2,10},{3,11},{4,12},{5,13},{6,14},{7,15},{8,0},{9,1},... | collective-permute-start | bytes 98312 | tf_op jit(solution)/shard_map/ppermute | solution.py:466
  114.5 2.8 %copy-done.1 = bf16[16,3,256,256]{3,2,1,0:T(8,128)(2,1)S(1)} copy-done((bf16[16,3,256,256]{3,2,1,0:T(8,128)(2,1)S(1)}, bf16[16,3,256,256]{3,2,1,0:T(8,128)(2,1)}, u32[]{:S(2)}) %copy-start.1) | copy-done | bytes 6291480
  117.3 3.0 %near_field.3.rest_0_.near = f32[16,256,128]{2,1,0:T(8,128)S(1)} custom-call(s32[32]{0:T(128)S(1)} %copy-done.13, bf16[16,256,128]{2,1,0:T(8,128)(2,1)S(1)} %copy-done.9, bf16[16,3,256,256]{3,2,1,0:T(8,128)(2,1)S(1)} %copy-done.1), custom_call_target="tpu_custom_call" | custom-call | flops 805306368 | bytes 6291456 | tf_op jit(solution)/shard_map/near_field/pallas_call | solution.py:422
  121.4 8.4 %collective-permute-done.11.second = bf16[4,32,128]{2,1,0:T(8,128)(2,1)S(1)} collective-permute-done((bf16[4,32,128]{2,1,0:T(8,128)(2,1)S(1)}, bf16[4,32,128]{2,1,0:T(8,128)(2,1)S(1)}, u32[]{:S(2)}, u32[]{:S(2)}) %collective-permute-start.11) | collective-permute-done | bytes 32800 | tf_op jit(solution)/shard_map/ppermute | solution.py:466
  129.9 3.7 %collective-permute-start.15 = (bf16[2,256,128]{2,1,0:T(8,128)(2,1)S(1)}, bf16[2,256,128]{2,1,0:T(8,128)(2,1)S(1)}, u32[]{:S(2)}, u32[]{:S(2)}) collective-permute-start(bf16[2,256,128]{2,1,0:T(8,128)(2,1)S(1)} %get-tuple-element.18), channel_id=1, source_target_pairs={{1,0},{2,1},{3,2},{4,3},{5,4},{6,5},{7,6},{8,7},{9,8},{10,9},{11,1... | collective-permute-start | bytes 393224 | tf_op jit(solution)/shard_map/ppermute | solution.py:418
  133.7 1.9 %collective-permute-start.14 = (bf16[2,256,128]{2,1,0:T(8,128)(2,1)S(1)}, bf16[2,256,128]{2,1,0:T(8,128)(2,1)S(1)}, u32[]{:S(2)}, u32[]{:S(2)}) collective-permute-start(bf16[2,256,128]{2,1,0:T(8,128)(2,1)S(1)} %get-tuple-element.19), channel_id=1, source_target_pairs={{0,1},{1,2},{2,3},{3,4},{4,5},{5,6},{6,7},{7,8},{8,9},{9,10},{10,1... | collective-permute-start | bytes 393224 | tf_op jit(solution)/shard_map/ppermute | solution.py:417
  135.6 5.5 %collective-permute-done.12 = bf16[8,32,128]{2,1,0:T(8,128)(2,1)S(1)} collective-permute-done((bf16[8,32,128]{2,1,0:T(8,128)(2,1)S(1)}, bf16[8,32,128]{2,1,0:T(8,128)(2,1)S(1)}, u32[]{:S(2)}, u32[]{:S(2)}) %collective-permute-start.12) | collective-permute-done | bytes 65568 | tf_op jit(solution)/shard_map/ppermute | solution.py:466
  141.2 1.3 collective-permute-done.15.after
  142.5 3.2 %collective-permute-done.14.before = bf16[2,256,128]{2,1,0:T(8,128)(2,1)S(1)} collective-permute-done((bf16[2,256,128]{2,1,0:T(8,128)(2,1)S(1)}, bf16[2,256,128]{2,1,0:T(8,128)(2,1)S(1)}, u32[]{:S(2)}, u32[]{:S(2)}) %collective-permute-start.14) | collective-permute-done | bytes 131104 | tf_op jit(solution)/shard_map/ppermute | solution.py:417
  146.4 8.1 %last_scores.1 = (f32[16,256,128]{2,1,0:T(8,128)}, f32[16,256,128]{2,1,0:T(8,128)}) custom-call(s32[1]{0:T(128)} %bitcast.me, s32[120]{0:T(128)} %reshape.38.listed, s32[124]{0:T(128)} %copy-done.25, s32[32,1,4]{2,1,0:T(1,128)} %copy-done.16, s32[32]{0:T(128)} %copy-done.12, bf16[128,64,128]{2,1,0:T(8,128)(2,1)} %all-to-all-done.2.incoming, ...), custom_call_target="tpu_custom_call" | custom-call | flops 130023424 | bytes 6291456 | tf_op jit(solution)/shard_map/last_scores/pallas_call | solution.py:509
  (99 shorter events, 13.1 us)
Async XLA Ops:
  2.7 14.9 %copy-start.25 = (s32[124]{0:T(128)}, s32[124]{0:T(128)S(1)}, u32[]{:S(2)}) copy-start(s32[124]{0:T(128)S(1)} %multiply_add_fusion.landing) | copy-start | bytes 1492
  3.5 10.9 %all-to-all-start = ((s32[32,1,4]{2,1,0:T(1,128)}), s32[32,1,4]{2,1,0:T(1,128)S(1)}, u32[]{:S(2)}, u32[]{:S(2)}) async-start(s32[32,1,4]{2,1,0:T(1,128)} %bitcast.1), calls=%async_computation | async-start | bytes 32768 | tf_op jit(solution)/shard_map/all_to_all | solution.py:339
  17.6 5.7 %copy-start.23 = (f32[64,128]{1,0:T(8,128)S(1)}, f32[64,128]{1,0:T(8,128)}, u32[]{:S(2)}) copy-start(f32[64,128]{1,0:T(8,128)} %get-tuple-element.11) | copy-start | bytes 98308
  17.6 21.1 %copy-start.27 = (s32[16,2]{0,1:T(2,128)S(1)}, s32[16,2]{0,1:T(2,128)}, u32[]{:S(2)}) copy-start(s32[16,2]{0,1:T(2,128)} %param.19) | copy-start | bytes 388
  17.6 21.0 %copy-start.4 = (f32[4096,128]{1,0:T(8,128)S(1)}, f32[4096,128]{1,0:T(8,128)}, u32[]{:S(2)}) copy-start(f32[4096,128]{1,0:T(8,128)} %param.15) | copy-start | bytes 6291460
  17.6 58.7 %all-to-all-start.1 = ((bf16[128,64,128]{2,1,0:T(8,128)(2,1)}), bf16[128,64,128]{2,1,0:T(8,128)(2,1)}, u32[]{:S(2)}, u32[]{:S(2)}) async-start(bf16[128,64,128]{2,1,0:T(8,128)(2,1)} %pick_rows.1), calls=%async_computation.1 | async-start | bytes 4194304 | tf_op jit(solution)/shard_map/all_to_all | solution.py:410
  23.3 1.2 collective-permute-start
  24.6 11.3 %collective-permute-start.1 = (bf16[1,32,128]{2,1,0:T(8,128)(2,1)S(1)}, bf16[1,32,128]{2,1,0:T(8,128)(2,1)S(1)}, u32[]{:S(2)}, u32[]{:S(2)}) collective-permute-start(bf16[1,32,128]{2,1,0:T(8,128)(2,1)S(1)} %fusion), channel_id=1, source_target_pairs={{0,2},{1,3},{2,0},{3,1},{4,6},{5,7},{6,4},{7,5},{8,10},{9,11},{10,... | collective-permute-start | bytes 24584 | tf_op jit(solution)/shard_map/ppermute | solution.py:466
  35.9 5.8 %collective-permute-start.2 = (bf16[2,32,128]{2,1,0:T(8,128)(2,1)S(1)}, bf16[2,32,128]{2,1,0:T(8,128)(2,1)S(1)}, u32[]{:S(2)}, u32[]{:S(2)}) collective-permute-start(bf16[2,32,128]{2,1,0:T(8,128)(2,1)S(1)} %pad_maximum_fusion.4), channel_id=1, source_target_pairs={{0,4},{1,5},{2,6},{3,7},{4,0},{5,1},{6,2},{7,3},{8,12},{9,13},{10,... | collective-permute-start | bytes 49160 | tf_op jit(solution)/shard_map/ppermute | solution.py:466
  39.0 11.8 %copy-start.12 = (s32[32]{0:T(128)}, s32[32]{0:T(128)S(1)}, u32[]{:S(2)}) copy-start(s32[32]{0:T(128)S(1)} %reshape.41.ids) | copy-start | bytes 388
  41.7 18.8 %collective-permute-start.3 = (bf16[4,32,128]{2,1,0:T(8,128)(2,1)S(1)}, bf16[4,32,128]{2,1,0:T(8,128)(2,1)S(1)}, u32[]{:S(2)}, u32[]{:S(2)}) collective-permute-start(bf16[4,32,128]{2,1,0:T(8,128)(2,1)S(1)} %pad_maximum_fusion.2.first), channel_id=1, source_target_pairs={{0,8},{1,9},{2,10},{3,11},{4,12},{5,13},{6,14},{7,15},{8,0},{9,1},... | collective-permute-start | bytes 98312 | tf_op jit(solution)/shard_map/ppermute | solution.py:466
  50.9 9.6 %copy-start.3 = (f32[16,256,128]{2,1,0:T(8,128)}, f32[16,256,128]{2,1,0:T(8,128)S(1)}, u32[]{:S(2)}) copy-start(f32[16,256,128]{2,1,0:T(8,128)S(1)} %near_field.2.rest_0_.near) | copy-start | bytes 6291460
  52.0 8.5 %copy-start.7 = (f32[16,256,128]{2,1,0:T(8,128)}, f32[16,256,128]{2,1,0:T(8,128)S(1)}, u32[]{:S(2)}) copy-start(f32[16,256,128]{2,1,0:T(8,128)S(1)} %with_labels.2.rest_1_.base) | copy-start | bytes 6291460
  52.0 19.9 %copy-start.26 = (s32[30,4]{0,1:T(4,128)S(1)}, s32[30,4]{0,1:T(4,128)}, u32[]{:S(2)}) copy-start(s32[30,4]{0,1:T(4,128)} %param.25) | copy-start | bytes 1444
  60.5 11.4 %collective-permute-start.4 = (bf16[8,32,128]{2,1,0:T(8,128)(2,1)S(1)}, bf16[8,32,128]{2,1,0:T(8,128)(2,1)S(1)}, u32[]{:S(2)}, u32[]{:S(2)}) collective-permute-start(bf16[8,32,128]{2,1,0:T(8,128)(2,1)S(1)} %join_rows.2), channel_id=1, source_target_pairs={{0,16},{1,17},{2,18},{3,19},{4,20},{5,21},{6,22},{7,23},{8,24},{9,... | collective-permute-start | bytes 196616 | tf_op jit(solution)/shard_map/ppermute | solution.py:466
  60.6 12.7 %collective-permute-start.7 = (bf16[2,256,128]{2,1,0:T(8,128)(2,1)S(1)}, bf16[2,256,128]{2,1,0:T(8,128)(2,1)S(1)}, u32[]{:S(2)}, u32[]{:S(2)}) collective-permute-start(bf16[2,256,128]{2,1,0:T(8,128)(2,1)S(1)} %get-tuple-element.20), channel_id=1, source_target_pairs={{1,0},{2,1},{3,2},{4,3},{5,4},{6,5},{7,6},{8,7},{9,8},{10,9},{11,1... | collective-permute-start | bytes 393224 | tf_op jit(solution)/shard_map/ppermute | solution.py:418
  64.4 11.9 %collective-permute-start.6 = (bf16[2,256,128]{2,1,0:T(8,128)(2,1)S(1)}, bf16[2,256,128]{2,1,0:T(8,128)(2,1)S(1)}, u32[]{:S(2)}, u32[]{:S(2)}) collective-permute-start(bf16[2,256,128]{2,1,0:T(8,128)(2,1)S(1)} %get-tuple-element.21), channel_id=1, source_target_pairs={{0,1},{1,2},{2,3},{3,4},{4,5},{5,6},{6,7},{7,8},{8,9},{9,10},{10,1... | collective-permute-start | bytes 393224 | tf_op jit(solution)/shard_map/ppermute | solution.py:417
  71.9 4.4 %collective-permute-start.5 = (bf16[16,32,128]{2,1,0:T(8,128)(2,1)S(1)}, bf16[16,32,128]{2,1,0:T(8,128)(2,1)S(1)}, u32[]{:S(2)}, u32[]{:S(2)}) collective-permute-start(bf16[16,32,128]{2,1,0:T(8,128)(2,1)S(1)} %pad_maximum_fusion.half), channel_id=1, source_target_pairs={{0,1},{1,0},{2,3},{3,2},{4,5},{5,4},{6,7},{7,6},{8,9},{9,8},{10,11... | collective-permute-start | bytes 393224 | tf_op jit(solution)/shard_map/ppermute | solution.py:473
  88.6 25.9 %copy-start.9 = (bf16[16,256,128]{2,1,0:T(8,128)(2,1)S(1)}, bf16[16,256,128]{2,1,0:T(8,128)(2,1)}, u32[]{:S(2)}) copy-start(bf16[16,256,128]{2,1,0:T(8,128)(2,1)} %get-tuple-element.14.own) | copy-start | bytes 3145732
  88.6 25.9 %copy-start.13 = (s32[32]{0:T(128)S(1)}, s32[32]{0:T(128)}, u32[]{:S(2)}) copy-start(s32[32]{0:T(128)} %copy-done.12) | copy-start | bytes 388
  88.6 57.2 %all-to-all-start.2 = ((bf16[128,64,128]{2,1,0:T(8,128)(2,1)}), bf16[128,64,128]{2,1,0:T(8,128)(2,1)}, u32[]{:S(2)}, u32[]{:S(2)}) async-start(bf16[128,64,128]{2,1,0:T(8,128)(2,1)} %get-tuple-element.12), calls=%async_computation.2 | async-start | bytes 4194304 | tf_op jit(solution)/shard_map/all_to_all | solution.py:410
  92.6 1.2 collective-permute-start.8
  93.9 11.3 %collective-permute-start.9 = (bf16[1,32,128]{2,1,0:T(8,128)(2,1)S(1)}, bf16[1,32,128]{2,1,0:T(8,128)(2,1)S(1)}, u32[]{:S(2)}, u32[]{:S(2)}) collective-permute-start(bf16[1,32,128]{2,1,0:T(8,128)(2,1)S(1)} %fusion.1), channel_id=1, source_target_pairs={{0,2},{1,3},{2,0},{3,1},{4,6},{5,7},{6,4},{7,5},{8,10},{9,11},{10,... | collective-permute-start | bytes 24584 | tf_op jit(solution)/shard_map/ppermute | solution.py:466
  105.2 4.5 %collective-permute-start.10 = (bf16[2,32,128]{2,1,0:T(8,128)(2,1)S(1)}, bf16[2,32,128]{2,1,0:T(8,128)(2,1)S(1)}, u32[]{:S(2)}, u32[]{:S(2)}) collective-permute-start(bf16[2,32,128]{2,1,0:T(8,128)(2,1)S(1)} %pad_maximum_fusion.5), channel_id=1, source_target_pairs={{0,4},{1,5},{2,6},{3,7},{4,0},{5,1},{6,2},{7,3},{8,12},{9,13},{10,... | collective-permute-start | bytes 49160 | tf_op jit(solution)/shard_map/ppermute | solution.py:466
  109.7 20.0 %collective-permute-start.11 = (bf16[4,32,128]{2,1,0:T(8,128)(2,1)S(1)}, bf16[4,32,128]{2,1,0:T(8,128)(2,1)S(1)}, u32[]{:S(2)}, u32[]{:S(2)}) collective-permute-start(bf16[4,32,128]{2,1,0:T(8,128)(2,1)S(1)} %pad_maximum_fusion.3.first), channel_id=1, source_target_pairs={{0,8},{1,9},{2,10},{3,11},{4,12},{5,13},{6,14},{7,15},{8,0},{9,1},... | collective-permute-start | bytes 98312 | tf_op jit(solution)/shard_map/ppermute | solution.py:466
  120.2 9.5 %copy-start.2 = (f32[16,256,128]{2,1,0:T(8,128)}, f32[16,256,128]{2,1,0:T(8,128)S(1)}, u32[]{:S(2)}) copy-start(f32[16,256,128]{2,1,0:T(8,128)S(1)} %near_field.3.rest_0_.near) | copy-start | bytes 6291460
  121.4 8.4 %copy-start.6 = (f32[16,256,128]{2,1,0:T(8,128)}, f32[16,256,128]{2,1,0:T(8,128)S(1)}, u32[]{:S(2)}) copy-start(f32[16,256,128]{2,1,0:T(8,128)S(1)} %with_labels.3.rest_1_.base) | copy-start | bytes 6291460
  129.8 11.3 %collective-permute-start.12 = (bf16[8,32,128]{2,1,0:T(8,128)(2,1)S(1)}, bf16[8,32,128]{2,1,0:T(8,128)(2,1)S(1)}, u32[]{:S(2)}, u32[]{:S(2)}) collective-permute-start(bf16[8,32,128]{2,1,0:T(8,128)(2,1)S(1)} %join_rows.3), channel_id=1, source_target_pairs={{0,16},{1,17},{2,18},{3,19},{4,20},{5,21},{6,22},{7,23},{8,24},{9,... | collective-permute-start | bytes 196616 | tf_op jit(solution)/shard_map/ppermute | solution.py:466
  129.9 12.6 %collective-permute-start.15 = (bf16[2,256,128]{2,1,0:T(8,128)(2,1)S(1)}, bf16[2,256,128]{2,1,0:T(8,128)(2,1)S(1)}, u32[]{:S(2)}, u32[]{:S(2)}) collective-permute-start(bf16[2,256,128]{2,1,0:T(8,128)(2,1)S(1)} %get-tuple-element.18), channel_id=1, source_target_pairs={{1,0},{2,1},{3,2},{4,3},{5,4},{6,5},{7,6},{8,7},{9,8},{10,9},{11,1... | collective-permute-start | bytes 393224 | tf_op jit(solution)/shard_map/ppermute | solution.py:418
  133.7 12.1 %collective-permute-start.14 = (bf16[2,256,128]{2,1,0:T(8,128)(2,1)S(1)}, bf16[2,256,128]{2,1,0:T(8,128)(2,1)S(1)}, u32[]{:S(2)}, u32[]{:S(2)}) collective-permute-start(bf16[2,256,128]{2,1,0:T(8,128)(2,1)S(1)} %get-tuple-element.19), channel_id=1, source_target_pairs={{0,1},{1,2},{2,3},{3,4},{4,5},{5,6},{6,7},{7,8},{8,9},{9,10},{10,1... | collective-permute-start | bytes 393224 | tf_op jit(solution)/shard_map/ppermute | solution.py:417
  141.1 4.6 %copy-start.15 = (bf16[16,32,128]{2,1,0:T(8,128)(2,1)}, bf16[16,32,128]{2,1,0:T(8,128)(2,1)S(1)}, u32[]{:S(2)}) copy-start(bf16[16,32,128]{2,1,0:T(8,128)(2,1)S(1)} %pad_maximum_fusion.1.half) | copy-start | bytes 393220
  141.2 4.6 %collective-permute-start.13 = (bf16[16,32,128]{2,1,0:T(8,128)(2,1)S(1)}, bf16[16,32,128]{2,1,0:T(8,128)(2,1)S(1)}, u32[]{:S(2)}, u32[]{:S(2)}) collective-permute-start(bf16[16,32,128]{2,1,0:T(8,128)(2,1)S(1)} %pad_maximum_fusion.1.half), channel_id=1, source_target_pairs={{0,1},{1,0},{2,3},{3,2},{4,5},{5,4},{6,7},{7,6},{8,9},{9,8},{10,11... | collective-permute-start | bytes 393224 | tf_op jit(solution)/shard_map/ppermute | solution.py:473
  (15 other events, 33.5 us)

commit v3 on v2

--- a/solution.py
+++ b/solution.py
@@ -94,17 +94,20 @@
 
 def pick(mover, chosen, coef, buffer, payload):
     leaving = []
-    total, width = payload.shape[0], chosen.shape[2]
+    total = payload.shape[0]
     for low, size in chunks(total, max(total // 2, 1)):
         for slot in range(low, low + size):
-            buffer[slot] = coef[chosen[slot // width, 0, slot % width]]
+            buffer[slot] = coef[chosen(slot)]
         rows = pl.ds(low, size)
         leaving.append(mover.start(buffer.at[rows], payload.at[rows]))
     return leaving
 
 
 def pick_kernel(chosen, coef, payload, buffer, sems):
-    for copy in pick(Mover(sems), chosen, coef, buffer, payload):
+    width = chosen.shape[2]
+    for copy in pick(
+        Mover(sems), lambda slot: chosen[slot // width, 0, slot % width], coef, buffer, payload
+    ):
         copy.wait()
 
 
@@ -126,7 +129,7 @@
             dot(tiles[leaf, 0], padded[row + REACH])
             + dot(tiles[leaf, 1], padded[ids[2 * row]])
             + dot(tiles[leaf, 2], padded[ids[2 * row + 1]])
-        )
+        ).astype(out.dtype)
 
 
 def join_kernel(first, second, *rest):
@@ -139,7 +142,7 @@
 def edge_scores(ids, leaf, tiles, halo, per_dev):
     total = None
     for member in range(2):
-        row = ids[2 * leaf + member]
+        row = ids(2 * leaf + member)
         place = jnp.where(row < REACH, row, jnp.where(row < REACH + per_dev, 2 * REACH, row - per_dev))
         term = dot(tiles[member], halo[place])
         total = term if total is None else total + term
@@ -166,7 +169,7 @@
         offset = offsets[level - 1]
         node = offset + (mine >> level)
         blocks = jnp.concatenate(
-            [coef[offset + listed[node * links + link]] for link in range(links)], axis=0
+            [coef[offset + listed(node * links + link)] for link in range(links)], axis=0
         )
         term = dot(couplings[level - 1], blocks)
         if level < levels:
@@ -180,11 +183,7 @@
     order,
     per_dev,
     last,
-    me,
-    listed,
-    landing,
-    chosen,
-    ids,
+    table,
     incoming,
     couplings,
     transfer,
@@ -203,16 +202,31 @@
     if last:
         new_out, scores_out = rest[:2]
         rest = rest[2:]
+        scores_buf = rest[-2]
     else:
-        payload, new_out, values_out, top_part = rest[:4]
-        rest = rest[4:]
-        coef, buffer, values = rest[-4:-1]
+        payload, grads_out, top_part = rest[:3]
+        rest = rest[3:]
+        coef, buffer, grads = rest[-4:-1]
     inbuf, cbuf, tbuf, nbuf, abuf, bbuf, halo, edge_tiles, field, coupled = rest[:10]
     coarse_maps, coarse_mats, coarse_coef = rest[10:13]
     sems = rest[-1]
-    mine = me[0]
     nodes = couplings.shape[0]
     links = couplings.shape[2] // couplings.shape[1]
+    mine = table[0]
+    places = {}
+    used = 1
+    for name, size in (
+        ("listed", coarse_couplings.shape[0] * links),
+        ("landing", (nodes + 1) * links),
+        ("chosen", incoming.shape[0]),
+        ("ids", 2 * per_dev),
+    ):
+        places[name] = used
+        used += size
+
+    def entry(name, place):
+        return table[places[name] + place]
+
     mover = Mover(sems)
     low_edge, high_edge = pl.ds(0, REACH), pl.ds(per_dev - REACH, REACH)
     others = pl.ds(1, 2)
@@ -220,62 +234,70 @@
     for level in range(1, coarse_mats.shape[0] + 1):
         node = devices - (devices >> level - 1) + (mine >> level)
         coarse_in.append(mover.start(coarse_couplings.at[node], coarse_mats.at[level - 1]))
-    blocks_in, mats_in, maps_in, *leaves_in = [
+    blocks_in, mats_in, maps_in, *edges_in = [
         mover.start(*pair)
         for pair in (
             (incoming, inbuf),
             (couplings, cbuf),
             (transfer, tbuf),
+            (basis, bbuf),
             (before, halo.at[pl.ds(0, REACH)]),
             (after, halo.at[pl.ds(REACH, REACH)]),
             (tiles.at[low_edge, others], edge_tiles.at[pl.ds(0, REACH)]),
             (tiles.at[high_edge, others], edge_tiles.at[pl.ds(REACH, REACH)]),
-            (basis, bbuf),
-            (near, nbuf),
-            (base, abuf),
         )
+    ]
+    leaves_in = [
+        [
+            mover.start(source.at[pl.ds(*part)], target.at[pl.ds(*part)])
+            for source, target in ((near, nbuf), (base, abuf))
+        ]
+        for part in chunks(per_dev, LEAVES)
     ]
     halo[2 * REACH] = jnp.zeros(halo.shape[1:], BF16)
     for copy in coarse_in:
         copy.wait()
     parent = coarse_parent(
-        devices, order, mine, listed, (half, other_half), coarse_maps, coarse_mats, coarse_coef
+        devices, order, mine, functools.partial(entry, "listed"), (half, other_half), coarse_maps, coarse_mats, coarse_coef
     )
     blocks_in.wait()
     mats_in.wait()
     for node in range(nodes - 1, -1, -1):
         blocks = jnp.concatenate(
-            [inbuf[landing[node * links + link]] for link in range(links)], axis=0
+            [inbuf[entry("landing", link * (nodes + 1) + node)] for link in range(links)], axis=0
         )
         coupled[node] = dot(cbuf[node], blocks)
     maps_in.wait()
     go_down(field, coupled, tbuf, parent, per_dev)
     leaving = []
-    for copy in leaves_in:
+    for copy in edges_in:
         copy.wait()
-    for low, size in chunks(per_dev, LEAVES):
+    for (low, size), copies in zip(chunks(per_dev, LEAVES), leaves_in):
+        for copy in copies:
+            copy.wait()
         rows = pl.ds(low, size)
         for leaf in range(low, low + size):
-            scores = nbuf[leaf] + rows_dot(bbuf[leaf], field[leaf])
+            scores = nbuf[leaf].astype(F32) + rows_dot(bbuf[leaf], field[leaf])
             edge = leaf if leaf < REACH else leaf - (per_dev - 2 * REACH)
             if leaf < REACH or leaf >= per_dev - REACH:
-                scores = scores + edge_scores(ids, leaf, edge_tiles.at[edge], halo, per_dev)
-            new = abuf[leaf] - gradient(scores)
-            abuf[leaf] = new
+                scores = scores + edge_scores(
+                    functools.partial(entry, "ids"), leaf, edge_tiles.at[edge], halo, per_dev
+                )
+            step = gradient(scores)
+            new = abuf[leaf] - step
             if last:
-                nbuf[leaf] = scores
+                scores_buf[leaf] = scores
+                abuf[leaf] = new
             else:
-                rounded = new.astype(BF16)
-                values[leaf] = rounded
-                coef[leaf] = dot(bbuf[leaf], rounded).astype(BF16)
+                grads[leaf] = step.astype(BF16)
+                coef[leaf] = dot(bbuf[leaf], new.astype(BF16)).astype(BF16)
         if last:
-            leaving.append(mover.start(nbuf.at[rows], scores_out.at[rows]))
-        else:
-            leaving.append(mover.start(values.at[rows], values_out.at[rows]))
-        leaving.append(mover.start(abuf.at[rows], new_out.at[rows]))
+            leaving.append(mover.start(scores_buf.at[rows], scores_out.at[rows]))
+            leaving.append(mover.start(abuf.at[rows], new_out.at[rows]))
     if not last:
         go_up(coef, tbuf, per_dev)
-        leaving += pick(mover, chosen, coef, buffer, payload)
+        leaving += pick(mover, functools.partial(entry, "chosen"), coef, buffer, payload)
+        leaving.append(mover.start(grads, grads_out))
         top_part[...] = rows_dot(tbuf[nodes - 1], coef[nodes - 1])
     for copy in leaving:
         copy.wait()
@@ -293,6 +315,13 @@
     return new + STEP_SIZE * rows_dot(marks.astype(BF16), eye.astype(BF16))
 
 
+def step_kernel(old, grads, labels, base, values):
+    for leaf in range(old.shape[0]):
+        new = old[leaf] - grads[leaf].astype(F32)
+        values[leaf] = new.astype(BF16)
+        base[leaf] = shifted(new, labels[leaf], new.shape[1])
+
+
 def shift_kernel(new, labels, base):
     for leaf in range(new.shape[0]):
         base[leaf] = shifted(new[leaf], labels[leaf], new.shape[2])
@@ -320,26 +349,57 @@
     return pl.CostEstimate(flops=int(flops), bytes_accessed=int(moved), transcendentals=0)
 
 
+def plan_kernel(per_dev, capacity, sources, landing, wanted):
+    links, nodes = sources.shape
+    devices = wanted.shape[0]
+    counts, starts = tree_rows(per_dev)
+    padded = nodes + 1
+    width = links * padded
+    node = lax.broadcasted_iota(jnp.int32, (links, padded), 1)
+    shift = jnp.zeros_like(node)
+    start = jnp.zeros_like(node)
+    for height, first in enumerate(starts):
+        shift = jnp.where(node >= first, len(counts) - 1 - height, shift)
+        start = jnp.where(node >= first, first, start)
+    listed = jnp.concatenate([sources[...], jnp.zeros((links, 1), jnp.int32)], axis=1)
+    owner = jnp.where(node < nodes, listed >> shift, -1)
+    row = start + (listed & ((1 << shift) - 1))
+
+    def in_line(values):
+        return jnp.concatenate([values[link : link + 1] for link in range(links)], axis=1)
+
+    rows_along = in_line(row)
+    along = jnp.broadcast_to(in_line(owner), (width, width))
+    down = along.T
+    later = lax.broadcasted_iota(jnp.int32, (width, width), 0) < lax.broadcasted_iota(
+        jnp.int32, (width, width), 1
+    )
+    rank = jnp.sum(jnp.where((down == along) & later, 1.0, 0.0), axis=0, keepdims=True)
+    rank = rank.astype(jnp.int32)
+    landing[...] = along[:1] * capacity + rank
+    device = lax.broadcasted_iota(jnp.int32, (devices, width), 0)
+    named = jnp.where(device == along[:1], rows_along.astype(F32), 0.0)
+    wanted[:, 0, :] = jnp.concatenate(
+        [
+            jnp.sum(jnp.where(rank == place, named, 0.0), axis=1, keepdims=True)
+            for place in range(capacity)
+        ],
+        axis=1,
+    ).astype(jnp.int32)
+
+
 def plan(sources, devices, per_dev, capacity):
-    counts, starts = tree_rows(per_dev)
-    links = sources.shape[1]
-    heights = np.repeat(np.arange(len(counts)), np.array(counts) * links)
-    shift = jnp.asarray((len(counts) - 1 - heights).astype(np.int32))
-    start = jnp.asarray(np.array(starts)[heights].astype(np.int32))
-    mask = jnp.asarray((np.array(counts)[heights] - 1).astype(np.int32))
-    flat = sources.reshape(-1)
-    owner = flat >> shift
-    row = start + (flat & mask)
-    width = flat.shape[0]
-    earlier = jnp.asarray(np.tril(np.ones((width, width), dtype=bool), -1))
-    rank = jnp.sum(((owner[:, None] == owner[None, :]) & earlier).astype(jnp.int32), axis=1)
-    landing = owner * capacity + rank
-    slots = jnp.arange(devices * capacity, dtype=jnp.int32)
-    wanted = jnp.sum(jnp.where(landing[None, :] == slots[:, None], row[None, :], 0), axis=1)
-    chosen = lax.all_to_all(
-        wanted.reshape(devices, 1, capacity), "leaf", split_axis=0, concat_axis=0, tiled=True
-    )
-    return landing, chosen
+    nodes, links = sources.shape
+    landing, wanted = pl.pallas_call(
+        functools.partial(plan_kernel, per_dev, capacity),
+        out_shape=[
+            jax.ShapeDtypeStruct((1, links * (nodes + 1)), jnp.int32),
+            jax.ShapeDtypeStruct((devices, 1, capacity), jnp.int32),
+        ],
+        name="plan",
+    )(sources.T)
+    chosen = lax.all_to_all(wanted, "leaf", split_axis=0, concat_axis=0, tiled=True)
+    return landing.reshape(-1), chosen
 
 
 def local(
@@ -377,6 +437,7 @@
     vmem = pl.BlockSpec(memory_space=pltpu.VMEM)
     hbm = pl.BlockSpec(memory_space=pltpu.HBM)
 
+    far = functools.partial(pltpu.with_memory_space_constraint, memory_space=pltpu.HBM)
     coef, top_part = pl.pallas_call(
         functools.partial(first_kernel, per_dev),
         in_specs=[hbm, hbm, hbm],
@@ -388,10 +449,10 @@
             pltpu.VMEM(transfer.shape, BF16),
             pltpu.SemaphoreType.DMA((2 * per_dev + 1,)),
         ],
-        compiler_params=pltpu.CompilerParams(vmem_limit_bytes=60 * MIB),
+        compiler_params=pltpu.CompilerParams(vmem_limit_bytes=20 * MIB),
         cost_estimate=cost(2 * basis.size * classes, 4 * weights.size),
         name="leaf_coefs",
-    )(weights3, basis, transfer)
+    )(*[far(value) for value in (weights3, basis, transfer)])
     payload = pl.pallas_call(
         pick_kernel,
         in_specs=[smem, vmem],
@@ -401,7 +462,7 @@
             pltpu.VMEM(payload_shape.shape, BF16),
             pltpu.SemaphoreType.DMA((8,)),
         ],
-        compiler_params=pltpu.CompilerParams(vmem_limit_bytes=60 * MIB),
+        compiler_params=pltpu.CompilerParams(vmem_limit_bytes=20 * MIB),
         cost_estimate=cost(0, 4 * slots * rank_dim * classes),
         name="pick_rows",
     )(chosen, coef)
@@ -424,24 +485,43 @@
             grid=(steps,),
             in_specs=[smem, whole(leaf_shape), per_step(block, near_tiles.shape)],
             out_specs=per_step(block, leaf_shape),
-            out_shape=jax.ShapeDtypeStruct(leaf_shape, F32),
+            out_shape=jax.ShapeDtypeStruct(leaf_shape, BF16),
             scratch_shapes=[pltpu.VMEM((per_dev + 2 * REACH, leaf_size, classes), BF16)],
             compiler_params=params(16),
             cost_estimate=cost(2 * near_tiles.size * classes, 2 * near_tiles.size),
             name="near_field",
         )(offset_ids, values, near_tiles)
 
+    labels3 = labels.reshape(per_dev, 1, leaf_size)
+    part = per_step(block, leaf_shape)
+    label_part = per_step(block, labels3.shape)
+
     def with_labels(new):
         return pl.pallas_call(
             shift_kernel,
             grid=(steps,),
-            in_specs=[per_step(block, leaf_shape), per_step(block, labels3.shape)],
-            out_specs=per_step(block, leaf_shape),
+            in_specs=[part, label_part],
+            out_specs=part,
             out_shape=jax.ShapeDtypeStruct(leaf_shape, F32),
             compiler_params=params(16),
             cost_estimate=cost(0, 8 * weights.size),
             name="with_labels",
         )(new, labels3)
+
+    def step_with_labels(old, grads):
+        return pl.pallas_call(
+            step_kernel,
+            grid=(steps,),
+            in_specs=[part, part, label_part],
+            out_specs=[part, part],
+            out_shape=[
+                jax.ShapeDtypeStruct(leaf_shape, F32),
+                jax.ShapeDtypeStruct(leaf_shape, BF16),
+            ],
+            compiler_params=params(16),
+            cost_estimate=cost(0, 12 * weights.size),
+            name="step_with_labels",
+        )(old, grads, labels3)
 
     def join(first, second, ahead):
         return pl.pallas_call(
@@ -479,7 +559,7 @@
             pltpu.VMEM(payload_shape.shape, BF16),
             pltpu.VMEM(couplings.shape, BF16),
             pltpu.VMEM(transfer.shape, BF16),
-            pltpu.VMEM(leaf_shape, F32),
+            pltpu.VMEM(leaf_shape, BF16),
             pltpu.VMEM(leaf_shape, F32),
             pltpu.VMEM(basis.shape, BF16),
             pltpu.VMEM((2 * REACH + 1, leaf_size, classes), BF16),
@@ -492,14 +572,14 @@
         ]
         if last:
             out_shape, out_specs = [leaf_out, leaf_out], [hbm, hbm]
+            scratch.append(pltpu.VMEM(leaf_shape, F32))
         else:
             out_shape = [
                 payload_shape,
-                leaf_out,
                 pltpu.HBM(leaf_shape, BF16),
                 jax.ShapeDtypeStruct(node_shape, F32),
             ]
-            out_specs = [hbm, hbm, hbm, vmem]
+            out_specs = [hbm, hbm, vmem]
             scratch += [
                 pltpu.VMEM(coef_shape, BF16),
                 pltpu.VMEM(payload_shape.shape, BF16),
@@ -508,45 +588,43 @@
         scratch.append(pltpu.SemaphoreType.DMA((2 * per_dev + devices,)))
         return pl.pallas_call(
             functools.partial(finish_kernel, devices, order, per_dev, last),
-            in_specs=[smem] * 5 + [hbm] * 3 + [vmem] * 2 + [hbm] * 8,
+            in_specs=[smem] + [hbm] * 3 + [vmem] * 2 + [hbm] * 8,
             out_specs=out_specs,
             scratch_shapes=scratch,
             out_shape=out_shape,
-            compiler_params=pltpu.CompilerParams(vmem_limit_bytes=60 * MIB),
+            compiler_params=pltpu.CompilerParams(vmem_limit_bytes=40 * MIB),
             cost_estimate=cost(2 * couplings.size * classes, 12 * weights.size),
             name="last_scores" if last else "first_scores",
         )(
-            me.reshape(1),
-            coarse_sources.reshape(-1),
-            landing,
-            chosen,
-            offset_ids,
-            incoming,
-            couplings,
-            transfer,
+            table,
+            far(incoming),
+            far(couplings),
+            far(transfer),
             *halves,
-            coarse_transfer,
-            coarse_couplings,
-            near,
-            base,
-            basis,
-            *halos,
-            near_tiles,
+            far(coarse_transfer),
+            far(coarse_couplings),
+            far(near),
+            far(base),
+            far(basis),
+            *[far(halo) for halo in halos],
+            far(near_tiles),
         )
 
-    labels3 = labels.reshape(per_dev, 1, leaf_size)
+    table = jnp.concatenate(
+        [me.reshape(1), coarse_sources.reshape(-1), landing, chosen.reshape(-1), offset_ids]
+    )
     values = weights3.astype(BF16)
     halos = halo_of(values)
     incoming = exchange(payload)
     near = near_field(values)
     base = with_labels(weights3)
-    rows = coarse_rows(top_part, (near, base))
-    payload, middle, values, top_part = finish(incoming, *rows, near, base, halos, False)
+    rows = coarse_rows(top_part, (near, base, table))
+    payload, grads, top_part = finish(incoming, *rows, near, base, halos, False)
+    incoming = exchange(payload)
+    base, values = step_with_labels(base, grads)
     halos = halo_of(values)
-    incoming = exchange(payload)
     near = near_field(values)
-    base = with_labels(middle)
-    rows = coarse_rows(top_part, (near, base))
+    rows = coarse_rows(top_part, (near, base, table))
     updated, second_scores = finish(incoming, *rows, near, base, halos, True)
     return updated.reshape(weights.shape), second_scores.reshape(weights.shape)
 

time: 156 us -> 151 us (0.968)
  waiting for transfers between devices: 62.9 us -> 58.7 us
    ppermute x8, waiting for transfers between devices: 52.1 us -> 45.7 us  [coarse_rows(): lax.ppermute(gathered, 'leaf', [(i, i ^ hop) for i in range(devices)])]
    pallas_call x2, Pallas kernels: 19.6 us -> 17.4 us  [finish(): pl.pallas_call(functools.partial(finish_kernel, devices, order, per_dev,...]
    pallas_call x2 -> x3, Pallas kernels: 2.22 us -> 3.78 us  [the longest x1 1.59 us: plan(): pl.pallas_call(functools.partial(plan_kernel, per_dev, capacity), out_sha...]
    unnamed x57 -> x39, local copies, waits for them, and re-layouts: 8.53 us -> 9.93 us
  transfers between devices with their start and end apart: 19 -> 19, of which waited for: 15 -> 15; matrix products, arithmetic and copies ran while one was open for 1% -> 3% of each run, Pallas kernels for 8% -> 7%
where the time goes in v3:
time: 151 us; the launch traced here: 149 us
  waiting for transfers between devices  58.7 us (39%)
  starting transfers between devices  43.5 us (29%)
  Pallas kernels  32.4 us (21%)
  local copies, waits for them, and re-layouts  12 us (8%)
  other arithmetic  1.89 us (1%)
    ppermute x8, waiting for transfers between devices, coarse_rows(): lax.ppermute(gathered, 'leaf', [(i, i ^ hop) for i in range(devices)])  45.7 us
    pallas_call x2, Pallas kernels, finish(): pl.pallas_call(functools.partial(finish_kernel, devices, order, per_dev,...  17.4 us
    ppermute x8, starting transfers between devices, coarse_rows(): lax.ppermute(gathered, 'leaf', [(i, i ^ hop) for i in range(devices)])  16.6 us
    unnamed x39, local copies, waits for them, and re-layouts  9.93 us
    all_to_all x2, starting transfers between devices, exchange(): lax.all_to_all(payload, 'leaf', split_axis=0, concat_axis=0, tiled=True)  9.13 us
    ppermute x2, starting transfers between devices, halo_of(): after = lax.ppermute(values[:REACH], 'leaf', down)  7.51 us
    ppermute x2, waiting for transfers between devices, halo_of(): before = lax.ppermute(values[per_dev - REACH:], 'leaf', up)  6.26 us
    all_to_all x1, starting transfers between devices, plan(): lax.all_to_all(wanted, 'leaf', split_axis=0, concat_axis=0, tiled=True)  5.93 us
  transfers between devices with their start and end apart: 19, of which 15 were waited for; matrix products, arithmetic and copies ran while one was open for 3% of the time, Pallas kernels for 7%

profile of v3, /device:TPU:16, one launch (start us, length us, event | category | flops | bytes accessed | tf_op | source)
XLA Modules:
  0.0 149.5 jit_solution(10658632994237361100)
XLA Ops:
  0.6 1.6 %plan.1 = (s32[1,128]{1,0:T(1,128)}, s32[32,1,4]{2,1,0:T(1,128)}) custom-call(s32[4,31]{1,0:T(4,128)} %bitcast.16), custom_call_target="tpu_custom_call" | custom-call | tf_op jit(solution)/shard_map/plan/pallas_call | solution.py:393
  2.2 5.9 %all-to-all-start = ((s32[32,1,4]{2,1,0:T(1,128)}), s32[32,1,4]{2,1,0:T(1,128)S(1)}, u32[]{:S(2)}, u32[]{:S(2)}) async-start(s32[32,1,4]{2,1,0:T(1,128)} %get-tuple-element.14), calls=%async_computation | async-start | bytes 32768 | tf_op jit(solution)/shard_map/all_to_all | solution.py:401
  8.2 3.0 %leaf_coefs.1 = (bf16[31,64,128]{2,1,0:T(8,128)(2,1)S(1)}, f32[64,128]{1,0:T(8,128)S(1)}) custom-call(f32[16,256,128]{2,1,0:T(8,128)} %bitcast.11, bf16[16,64,256]{2,1,0:T(8,128)(2,1)} %basis.5, bf16[31,64,64]{2,1,0:T(8,128)(2,1)} %transfer.5), custom_call_target="tpu_custom_call" | custom-call | flops 67108864 | bytes 2097152 | tf_op jit(solution)/shard_map/leaf_coefs/pallas_call | solution.py:441
  11.2 2.0 %all-to-all-done.chosen = s32[32,1,4]{2,1,0:T(1,128)S(1)} async-done(((s32[32,1,4]{2,1,0:T(1,128)}), s32[32,1,4]{2,1,0:T(1,128)S(1)}, u32[]{:S(2)}, u32[]{:S(2)}) %all-to-all-start) | async-done | bytes 544 | tf_op jit(solution)/shard_map/all_to_all | solution.py:401
  13.2 2.3 %pick_rows.1 = bf16[128,64,128]{2,1,0:T(8,128)(2,1)} custom-call(s32[32,1,4]{2,1,0:T(1,128)S(1)} %all-to-all-done.chosen, bf16[31,64,128]{2,1,0:T(8,128)(2,1)S(1)} %get-tuple-element.15.coef), custom_call_target="tpu_custom_call" | custom-call | bytes 4194304 | tf_op jit(solution)/shard_map/pick_rows/pallas_call | solution.py:456
  15.4 5.6 %all-to-all-start.1 = ((bf16[128,64,128]{2,1,0:T(8,128)(2,1)}), bf16[128,64,128]{2,1,0:T(8,128)(2,1)}, u32[]{:S(2)}, u32[]{:S(2)}) async-start(bf16[128,64,128]{2,1,0:T(8,128)(2,1)} %pick_rows.1), calls=%async_computation.1 | async-start | bytes 4194304 | tf_op jit(solution)/shard_map/all_to_all | solution.py:471
  22.3 1.5 collective-permute-start.1
  23.8 9.9 %collective-permute-done.1 = bf16[1,32,128]{2,1,0:T(8,128)(2,1)S(1)} collective-permute-done((bf16[1,32,128]{2,1,0:T(8,128)(2,1)S(1)}, bf16[1,32,128]{2,1,0:T(8,128)(2,1)S(1)}, u32[]{:S(2)}, u32[]{:S(2)}) %collective-permute-start.1) | collective-permute-done | bytes 8224 | tf_op jit(solution)/shard_map/ppermute | solution.py:546
  33.7 2.8 %collective-permute-start.2 = (bf16[2,32,128]{2,1,0:T(8,128)(2,1)S(1)}, bf16[2,32,128]{2,1,0:T(8,128)(2,1)S(1)}, u32[]{:S(2)}, u32[]{:S(2)}) collective-permute-start(bf16[2,32,128]{2,1,0:T(8,128)(2,1)S(1)} %pad_maximum_fusion.4), channel_id=1, source_target_pairs={{0,4},{1,5},{2,6},{3,7},{4,0},{5,1},{6,2},{7,3},{8,12},{9,13},{10,... | collective-permute-start | bytes 49160 | tf_op jit(solution)/shard_map/ppermute | solution.py:546
  37.8 1.7 %collective-permute-done.2 = bf16[2,32,128]{2,1,0:T(8,128)(2,1)S(1)} collective-permute-done((bf16[2,32,128]{2,1,0:T(8,128)(2,1)S(1)}, bf16[2,32,128]{2,1,0:T(8,128)(2,1)S(1)}, u32[]{:S(2)}, u32[]{:S(2)}) %collective-permute-start.2) | collective-permute-done | bytes 16416 | tf_op jit(solution)/shard_map/ppermute | solution.py:546
  39.5 3.4 %collective-permute-start.3 = (bf16[4,32,128]{2,1,0:T(8,128)(2,1)S(1)}, bf16[4,32,128]{2,1,0:T(8,128)(2,1)S(1)}, u32[]{:S(2)}, u32[]{:S(2)}) collective-permute-start(bf16[4,32,128]{2,1,0:T(8,128)(2,1)S(1)} %pad_maximum_fusion.2.first), channel_id=1, source_target_pairs={{0,8},{1,9},{2,10},{3,11},{4,12},{5,13},{6,14},{7,15},{8,0},{9,1},... | collective-permute-start | bytes 98312 | tf_op jit(solution)/shard_map/ppermute | solution.py:546
  42.9 2.8 %copy-done = bf16[16,3,256,256]{3,2,1,0:T(8,128)(2,1)S(1)} copy-done((bf16[16,3,256,256]{3,2,1,0:T(8,128)(2,1)S(1)}, bf16[16,3,256,256]{3,2,1,0:T(8,128)(2,1)}, u32[]{:S(2)}) %copy-start) | copy-done | bytes 6291480
  46.9 3.0 %near_field.2.rest_0_.near = bf16[16,256,128]{2,1,0:T(8,128)(2,1)S(1)} custom-call(s32[32]{0:T(128)S(1)} %reshape.35.ids, bf16[16,256,128]{2,1,0:T(8,128)(2,1)S(1)} %copy-done.9, bf16[16,3,256,256]{3,2,1,0:T(8,128)(2,1)S(1)} %copy-done), custom_call_target="tpu_custom_call" | custom-call | flops 805306368 | bytes 6291456 | tf_op jit(solution)/shard_map/near_field/pallas_call | solution.py:483
  50.1 1.7 %copy-done.5 = f32[4096,128]{1,0:T(8,128)S(1)} copy-done((f32[4096,128]{1,0:T(8,128)S(1)}, f32[4096,128]{1,0:T(8,128)}, u32[]{:S(2)}) %copy-start.5) | copy-done | bytes 2097176
  54.4 3.9 %collective-permute-done.3.second = bf16[4,32,128]{2,1,0:T(8,128)(2,1)S(1)} collective-permute-done((bf16[4,32,128]{2,1,0:T(8,128)(2,1)S(1)}, bf16[4,32,128]{2,1,0:T(8,128)(2,1)S(1)}, u32[]{:S(2)}, u32[]{:S(2)}) %collective-permute-start.3) | collective-permute-done | bytes 32800 | tf_op jit(solution)/shard_map/ppermute | solution.py:546
  59.3 3.8 %collective-permute-start.7 = (bf16[2,256,128]{2,1,0:T(8,128)(2,1)S(1)}, bf16[2,256,128]{2,1,0:T(8,128)(2,1)S(1)}, u32[]{:S(2)}, u32[]{:S(2)}) collective-permute-start(bf16[2,256,128]{2,1,0:T(8,128)(2,1)S(1)} %get-tuple-element.26), channel_id=1, source_target_pairs={{1,0},{2,1},{3,2},{4,3},{5,4},{6,5},{7,6},{8,7},{9,8},{10,9},{11,1... | collective-permute-start | bytes 393224 | tf_op jit(solution)/shard_map/ppermute | solution.py:479
  63.1 1.9 %collective-permute-start.6 = (bf16[2,256,128]{2,1,0:T(8,128)(2,1)S(1)}, bf16[2,256,128]{2,1,0:T(8,128)(2,1)S(1)}, u32[]{:S(2)}, u32[]{:S(2)}) collective-permute-start(bf16[2,256,128]{2,1,0:T(8,128)(2,1)S(1)} %get-tuple-element.27), channel_id=1, source_target_pairs={{0,1},{1,2},{2,3},{3,4},{4,5},{5,6},{6,7},{7,8},{8,9},{9,10},{10,1... | collective-permute-start | bytes 393224 | tf_op jit(solution)/shard_map/ppermute | solution.py:478
  65.1 4.6 %collective-permute-done.4 = bf16[8,32,128]{2,1,0:T(8,128)(2,1)S(1)} collective-permute-done((bf16[8,32,128]{2,1,0:T(8,128)(2,1)S(1)}, bf16[8,32,128]{2,1,0:T(8,128)(2,1)S(1)}, u32[]{:S(2)}, u32[]{:S(2)}) %collective-permute-start.4) | collective-permute-done | bytes 65568 | tf_op jit(solution)/shard_map/ppermute | solution.py:546
  71.1 3.1 %collective-permute-done.6.before = bf16[2,256,128]{2,1,0:T(8,128)(2,1)S(1)} collective-permute-done((bf16[2,256,128]{2,1,0:T(8,128)(2,1)S(1)}, bf16[2,256,128]{2,1,0:T(8,128)(2,1)S(1)}, u32[]{:S(2)}, u32[]{:S(2)}) %collective-permute-start.6) | collective-permute-done | bytes 131104 | tf_op jit(solution)/shard_map/ppermute | solution.py:478
  74.8 10.3 %first_scores.1 = (bf16[128,64,128]{2,1,0:T(8,128)(2,1)}, bf16[16,256,128]{2,1,0:T(8,128)(2,1)}, f32[64,128]{1,0:T(8,128)S(1)}) custom-call(s32[409]{0:T(512)S(1)} %concatenate.23.rest_2_.table, bf16[128,64,128]{2,1,0:T(8,128)(2,1)} %all-to-all-done.1.incoming, bf16[31,64,256]{2,1,0:T(8,128)(2,1)} %couplings.3, bf16[31,64,64]{2,1,0:T(8,128)(2,1)} %transfer.5, ...), custom_call_target="tpu_custom_call" | custom-call | flops 130023424 | bytes 6291456 | tf_op jit(solution)/shard_map/first_scores/pallas_call | solution.py:589
  85.2 3.5 %all-to-all-start.2 = ((bf16[128,64,128]{2,1,0:T(8,128)(2,1)}), bf16[128,64,128]{2,1,0:T(8,128)(2,1)}, u32[]{:S(2)}, u32[]{:S(2)}) async-start(bf16[128,64,128]{2,1,0:T(8,128)(2,1)} %get-tuple-element.17), calls=%async_computation.2 | async-start | bytes 4194304 | tf_op jit(solution)/shard_map/all_to_all | solution.py:471
  91.4 9.9 %collective-permute-done.9 = bf16[1,32,128]{2,1,0:T(8,128)(2,1)S(1)} collective-permute-done((bf16[1,32,128]{2,1,0:T(8,128)(2,1)S(1)}, bf16[1,32,128]{2,1,0:T(8,128)(2,1)S(1)}, u32[]{:S(2)}, u32[]{:S(2)}) %collective-permute-start.9) | collective-permute-done | bytes 8224 | tf_op jit(solution)/shard_map/ppermute | solution.py:546
  101.3 2.7 %collective-permute-start.10 = (bf16[2,32,128]{2,1,0:T(8,128)(2,1)S(1)}, bf16[2,32,128]{2,1,0:T(8,128)(2,1)S(1)}, u32[]{:S(2)}, u32[]{:S(2)}) collective-permute-start(bf16[2,32,128]{2,1,0:T(8,128)(2,1)S(1)} %pad_maximum_fusion.5), channel_id=1, source_target_pairs={{0,4},{1,5},{2,6},{3,7},{4,0},{5,1},{6,2},{7,3},{8,12},{9,13},{10,... | collective-permute-start | bytes 49160 | tf_op jit(solution)/shard_map/ppermute | solution.py:546
  105.8 4.7 %collective-permute-start.11 = (bf16[4,32,128]{2,1,0:T(8,128)(2,1)S(1)}, bf16[4,32,128]{2,1,0:T(8,128)(2,1)S(1)}, u32[]{:S(2)}, u32[]{:S(2)}) collective-permute-start(bf16[4,32,128]{2,1,0:T(8,128)(2,1)S(1)} %pad_maximum_fusion.3.first), channel_id=1, source_target_pairs={{0,8},{1,9},{2,10},{3,11},{4,12},{5,13},{6,14},{7,15},{8,0},{9,1},... | collective-permute-start | bytes 98312 | tf_op jit(solution)/shard_map/ppermute | solution.py:546
  110.5 2.8 %copy-done.1 = bf16[16,3,256,256]{3,2,1,0:T(8,128)(2,1)S(1)} copy-done((bf16[16,3,256,256]{3,2,1,0:T(8,128)(2,1)S(1)}, bf16[16,3,256,256]{3,2,1,0:T(8,128)(2,1)}, u32[]{:S(2)}) %copy-start.1) | copy-done | bytes 6291480
  113.3 3.0 %near_field.3.rest_0_.near = bf16[16,256,128]{2,1,0:T(8,128)(2,1)S(1)} custom-call(s32[32]{0:T(128)S(1)} %reshape.35.ids, bf16[16,256,128]{2,1,0:T(8,128)(2,1)S(1)} %get-tuple-element.20.own, bf16[16,3,256,256]{3,2,1,0:T(8,128)(2,1)S(1)} %copy-done.1), custom_call_target="tpu_custom_call" | custom-call | flops 805306368 | bytes 6291456 | tf_op jit(solution)/shard_map/near_field/pallas_call | solution.py:483
  116.3 9.5 %collective-permute-done.11.second = bf16[4,32,128]{2,1,0:T(8,128)(2,1)S(1)} collective-permute-done((bf16[4,32,128]{2,1,0:T(8,128)(2,1)S(1)}, bf16[4,32,128]{2,1,0:T(8,128)(2,1)S(1)}, u32[]{:S(2)}, u32[]{:S(2)}) %collective-permute-start.11) | collective-permute-done | bytes 32800 | tf_op jit(solution)/shard_map/ppermute | solution.py:546
  125.9 3.7 %collective-permute-start.15 = (bf16[2,256,128]{2,1,0:T(8,128)(2,1)S(1)}, bf16[2,256,128]{2,1,0:T(8,128)(2,1)S(1)}, u32[]{:S(2)}, u32[]{:S(2)}) collective-permute-start(bf16[2,256,128]{2,1,0:T(8,128)(2,1)S(1)} %get-tuple-element.24), channel_id=1, source_target_pairs={{1,0},{2,1},{3,2},{4,3},{5,4},{6,5},{7,6},{8,7},{9,8},{10,9},{11,1... | collective-permute-start | bytes 393224 | tf_op jit(solution)/shard_map/ppermute | solution.py:479
  129.7 1.9 %collective-permute-start.14 = (bf16[2,256,128]{2,1,0:T(8,128)(2,1)S(1)}, bf16[2,256,128]{2,1,0:T(8,128)(2,1)S(1)}, u32[]{:S(2)}, u32[]{:S(2)}) collective-permute-start(bf16[2,256,128]{2,1,0:T(8,128)(2,1)S(1)} %get-tuple-element.25), channel_id=1, source_target_pairs={{0,1},{1,2},{2,3},{3,4},{4,5},{5,6},{6,7},{7,8},{8,9},{9,10},{10,1... | collective-permute-start | bytes 393224 | tf_op jit(solution)/shard_map/ppermute | solution.py:478
  131.6 5.6 %collective-permute-done.12 = bf16[8,32,128]{2,1,0:T(8,128)(2,1)S(1)} collective-permute-done((bf16[8,32,128]{2,1,0:T(8,128)(2,1)S(1)}, bf16[8,32,128]{2,1,0:T(8,128)(2,1)S(1)}, u32[]{:S(2)}, u32[]{:S(2)}) %collective-permute-start.12) | collective-permute-done | bytes 65568 | tf_op jit(solution)/shard_map/ppermute | solution.py:546
  138.6 3.2 %collective-permute-done.14.before = bf16[2,256,128]{2,1,0:T(8,128)(2,1)S(1)} collective-permute-done((bf16[2,256,128]{2,1,0:T(8,128)(2,1)S(1)}, bf16[2,256,128]{2,1,0:T(8,128)(2,1)S(1)}, u32[]{:S(2)}, u32[]{:S(2)}) %collective-permute-start.14) | collective-permute-done | bytes 131104 | tf_op jit(solution)/shard_map/ppermute | solution.py:478
  142.4 7.1 %last_scores.1 = (f32[16,256,128]{2,1,0:T(8,128)}, f32[16,256,128]{2,1,0:T(8,128)}) custom-call(s32[409]{0:T(512)S(1)} %concatenate.23.rest_2_.table, bf16[128,64,128]{2,1,0:T(8,128)(2,1)} %all-to-all-done.2.incoming, bf16[31,64,256]{2,1,0:T(8,128)(2,1)} %couplings.3, bf16[31,64,64]{2,1,0:T(8,128)(2,1)} %transfer.5, ...), custom_call_target="tpu_custom_call" | custom-call | flops 130023424 | bytes 6291456 | tf_op jit(solution)/shard_map/last_scores/pallas_call | solution.py:589
  (77 shorter events, 16.3 us)
Async XLA Ops:
  2.2 10.9 %all-to-all-start = ((s32[32,1,4]{2,1,0:T(1,128)}), s32[32,1,4]{2,1,0:T(1,128)S(1)}, u32[]{:S(2)}, u32[]{:S(2)}) async-start(s32[32,1,4]{2,1,0:T(1,128)} %get-tuple-element.14), calls=%async_computation | async-start | bytes 32768 | tf_op jit(solution)/shard_map/all_to_all | solution.py:401
  15.4 21.0 %copy-start.17 = (s32[16,2]{0,1:T(2,128)S(1)}, s32[16,2]{0,1:T(2,128)}, u32[]{:S(2)}) copy-start(s32[16,2]{0,1:T(2,128)} %param.15) | copy-start | bytes 388
  15.4 21.0 %copy-start.4 = (f32[4096,128]{1,0:T(8,128)S(1)}, f32[4096,128]{1,0:T(8,128)}, u32[]{:S(2)}) copy-start(f32[4096,128]{1,0:T(8,128)} %param.11) | copy-start | bytes 6291460
  15.4 58.7 %all-to-all-start.1 = ((bf16[128,64,128]{2,1,0:T(8,128)(2,1)}), bf16[128,64,128]{2,1,0:T(8,128)(2,1)}, u32[]{:S(2)}, u32[]{:S(2)}) async-start(bf16[128,64,128]{2,1,0:T(8,128)(2,1)} %pick_rows.1), calls=%async_computation.1 | async-start | bytes 4194304 | tf_op jit(solution)/shard_map/all_to_all | solution.py:471
  21.1 1.2 collective-permute-start
  22.3 11.3 %collective-permute-start.1 = (bf16[1,32,128]{2,1,0:T(8,128)(2,1)S(1)}, bf16[1,32,128]{2,1,0:T(8,128)(2,1)S(1)}, u32[]{:S(2)}, u32[]{:S(2)}) collective-permute-start(bf16[1,32,128]{2,1,0:T(8,128)(2,1)S(1)} %fusion), channel_id=1, source_target_pairs={{0,2},{1,3},{2,0},{3,1},{4,6},{5,7},{6,4},{7,5},{8,10},{9,11},{10,... | collective-permute-start | bytes 24584 | tf_op jit(solution)/shard_map/ppermute | solution.py:546
  33.7 5.8 %collective-permute-start.2 = (bf16[2,32,128]{2,1,0:T(8,128)(2,1)S(1)}, bf16[2,32,128]{2,1,0:T(8,128)(2,1)S(1)}, u32[]{:S(2)}, u32[]{:S(2)}) collective-permute-start(bf16[2,32,128]{2,1,0:T(8,128)(2,1)S(1)} %pad_maximum_fusion.4), channel_id=1, source_target_pairs={{0,4},{1,5},{2,6},{3,7},{4,0},{5,1},{6,2},{7,3},{8,12},{9,13},{10,... | collective-permute-start | bytes 49160 | tf_op jit(solution)/shard_map/ppermute | solution.py:546
  39.5 18.8 %collective-permute-start.3 = (bf16[4,32,128]{2,1,0:T(8,128)(2,1)S(1)}, bf16[4,32,128]{2,1,0:T(8,128)(2,1)S(1)}, u32[]{:S(2)}, u32[]{:S(2)}) collective-permute-start(bf16[4,32,128]{2,1,0:T(8,128)(2,1)S(1)} %pad_maximum_fusion.2.first), channel_id=1, source_target_pairs={{0,8},{1,9},{2,10},{3,11},{4,12},{5,13},{6,14},{7,15},{8,0},{9,1},... | collective-permute-start | bytes 98312 | tf_op jit(solution)/shard_map/ppermute | solution.py:546
  42.9 2.8 %copy-start = (bf16[16,3,256,256]{3,2,1,0:T(8,128)(2,1)S(1)}, bf16[16,3,256,256]{3,2,1,0:T(8,128)(2,1)}, u32[]{:S(2)}) copy-start(bf16[16,3,256,256]{3,2,1,0:T(8,128)(2,1)} %tiles.7) | copy-start | bytes 18874372
  46.9 3.0 %copy-start.16 = (s32[30,4]{0,1:T(4,128)S(1)}, s32[30,4]{0,1:T(4,128)}, u32[]{:S(2)}) copy-start(s32[30,4]{0,1:T(4,128)} %param.21) | copy-start | bytes 1444
  46.9 3.2 %copy-start.11 = (s32[4096]{0:T(1024)S(1)}, s32[4096]{0:T(1024)}, u32[]{:S(2)}) copy-start(s32[4096]{0:T(1024)} %param.12) | copy-start | bytes 49156
  49.9 8.4 %copy-start.6 = (bf16[16,256,128]{2,1,0:T(8,128)(2,1)}, bf16[16,256,128]{2,1,0:T(8,128)(2,1)S(1)}, u32[]{:S(2)}) copy-start(bf16[16,256,128]{2,1,0:T(8,128)(2,1)S(1)} %near_field.2.rest_0_.near) | copy-start | bytes 3145732
  53.0 21.2 %copy-start.2 = (f32[16,256,128]{2,1,0:T(8,128)}, f32[16,256,128]{2,1,0:T(8,128)S(1)}, u32[]{:S(2)}) copy-start(f32[16,256,128]{2,1,0:T(8,128)S(1)} %with_labels.1.rest_1_.base.old) | copy-start | bytes 6291460
  58.3 11.4 %collective-permute-start.4 = (bf16[8,32,128]{2,1,0:T(8,128)(2,1)S(1)}, bf16[8,32,128]{2,1,0:T(8,128)(2,1)S(1)}, u32[]{:S(2)}, u32[]{:S(2)}) collective-permute-start(bf16[8,32,128]{2,1,0:T(8,128)(2,1)S(1)} %join_rows.2), channel_id=1, source_target_pairs={{0,16},{1,17},{2,18},{3,19},{4,20},{5,21},{6,22},{7,23},{8,24},{9,... | collective-permute-start | bytes 196616 | tf_op jit(solution)/shard_map/ppermute | solution.py:546
  59.3 11.8 %collective-permute-start.7 = (bf16[2,256,128]{2,1,0:T(8,128)(2,1)S(1)}, bf16[2,256,128]{2,1,0:T(8,128)(2,1)S(1)}, u32[]{:S(2)}, u32[]{:S(2)}) collective-permute-start(bf16[2,256,128]{2,1,0:T(8,128)(2,1)S(1)} %get-tuple-element.26), channel_id=1, source_target_pairs={{1,0},{2,1},{3,2},{4,3},{5,4},{6,5},{7,6},{8,7},{9,8},{10,9},{11,1... | collective-permute-start | bytes 393224 | tf_op jit(solution)/shard_map/ppermute | solution.py:479
  63.1 11.0 %collective-permute-start.6 = (bf16[2,256,128]{2,1,0:T(8,128)(2,1)S(1)}, bf16[2,256,128]{2,1,0:T(8,128)(2,1)S(1)}, u32[]{:S(2)}, u32[]{:S(2)}) collective-permute-start(bf16[2,256,128]{2,1,0:T(8,128)(2,1)S(1)} %get-tuple-element.27), channel_id=1, source_target_pairs={{0,1},{1,2},{2,3},{3,4},{4,5},{5,6},{6,7},{7,8},{8,9},{9,10},{10,1... | collective-permute-start | bytes 393224 | tf_op jit(solution)/shard_map/ppermute | solution.py:478
  69.7 4.5 %collective-permute-start.5 = (bf16[16,32,128]{2,1,0:T(8,128)(2,1)S(1)}, bf16[16,32,128]{2,1,0:T(8,128)(2,1)S(1)}, u32[]{:S(2)}, u32[]{:S(2)}) collective-permute-start(bf16[16,32,128]{2,1,0:T(8,128)(2,1)S(1)} %pad_maximum_fusion.half), channel_id=1, source_target_pairs={{0,1},{1,0},{2,3},{3,2},{4,5},{5,4},{6,7},{7,6},{8,9},{9,8},{10,11... | collective-permute-start | bytes 393224 | tf_op jit(solution)/shard_map/ppermute | solution.py:553
  71.1 3.1 %copy-start.13 = (bf16[2,256,128]{2,1,0:T(8,128)(2,1)}, bf16[2,256,128]{2,1,0:T(8,128)(2,1)S(1)}, u32[]{:S(2)}) copy-start(bf16[2,256,128]{2,1,0:T(8,128)(2,1)S(1)} %collective-permute-done.7.after) | copy-start | bytes 393220
  85.1 18.8 %copy-start.3 = (f32[16,256,128]{2,1,0:T(8,128)S(1)}, f32[16,256,128]{2,1,0:T(8,128)}, u32[]{:S(2)}) copy-start(f32[16,256,128]{2,1,0:T(8,128)} %copy-done.2) | copy-start | bytes 6291460
  85.2 18.8 %copy-start.10 = (bf16[16,256,128]{2,1,0:T(8,128)(2,1)S(1)}, bf16[16,256,128]{2,1,0:T(8,128)(2,1)}, u32[]{:S(2)}) copy-start(bf16[16,256,128]{2,1,0:T(8,128)(2,1)} %get-tuple-element.19.grads) | copy-start | bytes 3145732
  85.2 56.6 %all-to-all-start.2 = ((bf16[128,64,128]{2,1,0:T(8,128)(2,1)}), bf16[128,64,128]{2,1,0:T(8,128)(2,1)}, u32[]{:S(2)}, u32[]{:S(2)}) async-start(bf16[128,64,128]{2,1,0:T(8,128)(2,1)} %get-tuple-element.17), calls=%async_computation.2 | async-start | bytes 4194304 | tf_op jit(solution)/shard_map/all_to_all | solution.py:471
  88.7 1.2 collective-permute-start.8
  90.0 11.3 %collective-permute-start.9 = (bf16[1,32,128]{2,1,0:T(8,128)(2,1)S(1)}, bf16[1,32,128]{2,1,0:T(8,128)(2,1)S(1)}, u32[]{:S(2)}, u32[]{:S(2)}) collective-permute-start(bf16[1,32,128]{2,1,0:T(8,128)(2,1)S(1)} %fusion.1), channel_id=1, source_target_pairs={{0,2},{1,3},{2,0},{3,1},{4,6},{5,7},{6,4},{7,5},{8,10},{9,11},{10,... | collective-permute-start | bytes 24584 | tf_op jit(solution)/shard_map/ppermute | solution.py:546
  101.3 4.5 %collective-permute-start.10 = (bf16[2,32,128]{2,1,0:T(8,128)(2,1)S(1)}, bf16[2,32,128]{2,1,0:T(8,128)(2,1)S(1)}, u32[]{:S(2)}, u32[]{:S(2)}) collective-permute-start(bf16[2,32,128]{2,1,0:T(8,128)(2,1)S(1)} %pad_maximum_fusion.5), channel_id=1, source_target_pairs={{0,4},{1,5},{2,6},{3,7},{4,0},{5,1},{6,2},{7,3},{8,12},{9,13},{10,... | collective-permute-start | bytes 49160 | tf_op jit(solution)/shard_map/ppermute | solution.py:546
  105.0 20.8 %copy-start.8 = (f32[16,256,128]{2,1,0:T(8,128)}, f32[16,256,128]{2,1,0:T(8,128)S(1)}, u32[]{:S(2)}) copy-start(f32[16,256,128]{2,1,0:T(8,128)S(1)} %get-tuple-element.21.rest_1_.base) | copy-start | bytes 6291460
  105.8 20.0 %collective-permute-start.11 = (bf16[4,32,128]{2,1,0:T(8,128)(2,1)S(1)}, bf16[4,32,128]{2,1,0:T(8,128)(2,1)S(1)}, u32[]{:S(2)}, u32[]{:S(2)}) collective-permute-start(bf16[4,32,128]{2,1,0:T(8,128)(2,1)S(1)} %pad_maximum_fusion.3.first), channel_id=1, source_target_pairs={{0,8},{1,9},{2,10},{3,11},{4,12},{5,13},{6,14},{7,15},{8,0},{9,1},... | collective-permute-start | bytes 98312 | tf_op jit(solution)/shard_map/ppermute | solution.py:546
  116.3 25.5 %copy-start.7 = (bf16[16,256,128]{2,1,0:T(8,128)(2,1)}, bf16[16,256,128]{2,1,0:T(8,128)(2,1)S(1)}, u32[]{:S(2)}) copy-start(bf16[16,256,128]{2,1,0:T(8,128)(2,1)S(1)} %near_field.3.rest_0_.near) | copy-start | bytes 3145732
  125.8 11.3 %collective-permute-start.12 = (bf16[8,32,128]{2,1,0:T(8,128)(2,1)S(1)}, bf16[8,32,128]{2,1,0:T(8,128)(2,1)S(1)}, u32[]{:S(2)}, u32[]{:S(2)}) collective-permute-start(bf16[8,32,128]{2,1,0:T(8,128)(2,1)S(1)} %join_rows.3), channel_id=1, source_target_pairs={{0,16},{1,17},{2,18},{3,19},{4,20},{5,21},{6,22},{7,23},{8,24},{9,... | collective-permute-start | bytes 196616 | tf_op jit(solution)/shard_map/ppermute | solution.py:546
  125.9 12.6 %collective-permute-start.15 = (bf16[2,256,128]{2,1,0:T(8,128)(2,1)S(1)}, bf16[2,256,128]{2,1,0:T(8,128)(2,1)S(1)}, u32[]{:S(2)}, u32[]{:S(2)}) collective-permute-start(bf16[2,256,128]{2,1,0:T(8,128)(2,1)S(1)} %get-tuple-element.24), channel_id=1, source_target_pairs={{1,0},{2,1},{3,2},{4,3},{5,4},{6,5},{7,6},{8,7},{9,8},{10,9},{11,1... | collective-permute-start | bytes 393224 | tf_op jit(solution)/shard_map/ppermute | solution.py:479
  129.7 12.1 %collective-permute-start.14 = (bf16[2,256,128]{2,1,0:T(8,128)(2,1)S(1)}, bf16[2,256,128]{2,1,0:T(8,128)(2,1)S(1)}, u32[]{:S(2)}, u32[]{:S(2)}) collective-permute-start(bf16[2,256,128]{2,1,0:T(8,128)(2,1)S(1)} %get-tuple-element.25), channel_id=1, source_target_pairs={{0,1},{1,2},{2,3},{3,4},{4,5},{5,6},{6,7},{7,8},{8,9},{9,10},{10,1... | collective-permute-start | bytes 393224 | tf_op jit(solution)/shard_map/ppermute | solution.py:478
  137.2 4.6 %collective-permute-start.13 = (bf16[16,32,128]{2,1,0:T(8,128)(2,1)S(1)}, bf16[16,32,128]{2,1,0:T(8,128)(2,1)S(1)}, u32[]{:S(2)}, u32[]{:S(2)}) collective-permute-start(bf16[16,32,128]{2,1,0:T(8,128)(2,1)S(1)} %pad_maximum_fusion.1.half), channel_id=1, source_target_pairs={{0,1},{1,0},{2,3},{3,2},{4,5},{5,4},{6,7},{7,6},{8,9},{9,8},{10,11... | collective-permute-start | bytes 393224 | tf_op jit(solution)/shard_map/ppermute | solution.py:553
  138.6 3.2 %copy-start.12 = (bf16[2,256,128]{2,1,0:T(8,128)(2,1)}, bf16[2,256,128]{2,1,0:T(8,128)(2,1)S(1)}, u32[]{:S(2)}) copy-start(bf16[2,256,128]{2,1,0:T(8,128)(2,1)S(1)} %collective-permute-done.15.after) | copy-start | bytes 393220
  (6 other events, 9.5 us)

commit v4 on v3

--- a/solution.py
+++ b/solution.py
@@ -42,6 +42,17 @@
             coef[starts[height] + node] = rows_dot(
                 pair_rows(transfer, kids), pair_rows(coef, kids)
             ).astype(BF16)
+
+
+def go_up_from(leaf, coef, transfer, per_dev):
+    counts, starts = tree_rows(per_dev)
+    for height in range(1, len(counts)):
+        if (leaf + 1) % (1 << height):
+            break
+        kids = starts[height - 1] + 2 * (leaf >> height)
+        coef[starts[height] + (leaf >> height)] = rows_dot(
+            pair_rows(transfer, kids), pair_rows(coef, kids)
+        ).astype(BF16)
 
 
 def go_down(field, coupled, transfer, parent, per_dev):
@@ -95,7 +106,7 @@
 def pick(mover, chosen, coef, buffer, payload):
     leaving = []
     total = payload.shape[0]
-    for low, size in chunks(total, max(total // 2, 1)):
+    for low, size in chunks(total, max(total // 4, 1)):
         for slot in range(low, low + size):
             buffer[slot] = coef[chosen(slot)]
         rows = pl.ds(low, size)
@@ -291,11 +302,11 @@
             else:
                 grads[leaf] = step.astype(BF16)
                 coef[leaf] = dot(bbuf[leaf], new.astype(BF16)).astype(BF16)
+                go_up_from(leaf, coef, tbuf, per_dev)
         if last:
             leaving.append(mover.start(scores_buf.at[rows], scores_out.at[rows]))
             leaving.append(mover.start(abuf.at[rows], new_out.at[rows]))
     if not last:
-        go_up(coef, tbuf, per_dev)
         leaving += pick(mover, functools.partial(entry, "chosen"), coef, buffer, payload)
         leaving.append(mover.start(grads, grads_out))
         top_part[...] = rows_dot(tbuf[nodes - 1], coef[nodes - 1])

time: 151 us -> 152 us (level)
  no operation moved by 1% of the time
where the time goes in v4:
time: 152 us; the launch traced here: 150 us
  waiting for transfers between devices  58.7 us (39%)
  starting transfers between devices  43.5 us (29%)
  Pallas kernels  33.3 us (22%)
  local copies, waits for them, and re-layouts  12 us (8%)
  other arithmetic  1.89 us (1%)
    ppermute x8, waiting for transfers between devices, coarse_rows(): lax.ppermute(gathered, 'leaf', [(i, i ^ hop) for i in range(devices)])  45.7 us
    pallas_call x2, Pallas kernels, finish(): pl.pallas_call(functools.partial(finish_kernel, devices, order, per_dev,...  18.4 us
    ppermute x8, starting transfers between devices, coarse_rows(): lax.ppermute(gathered, 'leaf', [(i, i ^ hop) for i in range(devices)])  16.6 us
    unnamed x39, local copies, waits for them, and re-layouts  9.93 us
    all_to_all x2, starting transfers between devices, exchange(): lax.all_to_all(payload, 'leaf', split_axis=0, concat_axis=0, tiled=True)  9.13 us
    ppermute x2, starting transfers between devices, halo_of(): after = lax.ppermute(values[:REACH], 'leaf', down)  7.51 us
    ppermute x2, waiting for transfers between devices, halo_of(): before = lax.ppermute(values[per_dev - REACH:], 'leaf', up)  6.26 us
    all_to_all x1, starting transfers between devices, plan(): lax.all_to_all(wanted, 'leaf', split_axis=0, concat_axis=0, tiled=True)  5.93 us
  transfers between devices with their start and end apart: 19, of which 15 were waited for; matrix products, arithmetic and copies ran while one was open for 3% of the time, Pallas kernels for 7%

profile of v4, /device:TPU:16, one launch (start us, length us, event | category | flops | bytes accessed | tf_op | source)
XLA Modules:
  0.0 150.4 jit_solution(12975195724761119918)
XLA Ops:
  0.6 1.6 %plan.1 = (s32[1,128]{1,0:T(1,128)}, s32[32,1,4]{2,1,0:T(1,128)}) custom-call(s32[4,31]{1,0:T(4,128)} %bitcast.16), custom_call_target="tpu_custom_call" | custom-call | tf_op jit(solution)/shard_map/plan/pallas_call | solution.py:404
  2.2 5.9 %all-to-all-start = ((s32[32,1,4]{2,1,0:T(1,128)}), s32[32,1,4]{2,1,0:T(1,128)S(1)}, u32[]{:S(2)}, u32[]{:S(2)}) async-start(s32[32,1,4]{2,1,0:T(1,128)} %get-tuple-element.14), calls=%async_computation | async-start | bytes 32768 | tf_op jit(solution)/shard_map/all_to_all | solution.py:412
  8.2 3.0 %leaf_coefs.1 = (bf16[31,64,128]{2,1,0:T(8,128)(2,1)S(1)}, f32[64,128]{1,0:T(8,128)S(1)}) custom-call(f32[16,256,128]{2,1,0:T(8,128)} %bitcast.11, bf16[16,64,256]{2,1,0:T(8,128)(2,1)} %basis.5, bf16[31,64,64]{2,1,0:T(8,128)(2,1)} %transfer.5), custom_call_target="tpu_custom_call" | custom-call | flops 67108864 | bytes 2097152 | tf_op jit(solution)/shard_map/leaf_coefs/pallas_call | solution.py:452
  11.2 2.0 %all-to-all-done.chosen = s32[32,1,4]{2,1,0:T(1,128)S(1)} async-done(((s32[32,1,4]{2,1,0:T(1,128)}), s32[32,1,4]{2,1,0:T(1,128)S(1)}, u32[]{:S(2)}, u32[]{:S(2)}) %all-to-all-start) | async-done | bytes 544 | tf_op jit(solution)/shard_map/all_to_all | solution.py:412
  13.2 2.2 %pick_rows.1 = bf16[128,64,128]{2,1,0:T(8,128)(2,1)} custom-call(s32[32,1,4]{2,1,0:T(1,128)S(1)} %all-to-all-done.chosen, bf16[31,64,128]{2,1,0:T(8,128)(2,1)S(1)} %get-tuple-element.15.coef), custom_call_target="tpu_custom_call" | custom-call | bytes 4194304 | tf_op jit(solution)/shard_map/pick_rows/pallas_call | solution.py:467
  15.4 5.6 %all-to-all-start.1 = ((bf16[128,64,128]{2,1,0:T(8,128)(2,1)}), bf16[128,64,128]{2,1,0:T(8,128)(2,1)}, u32[]{:S(2)}, u32[]{:S(2)}) async-start(bf16[128,64,128]{2,1,0:T(8,128)(2,1)} %pick_rows.1), calls=%async_computation.1 | async-start | bytes 4194304 | tf_op jit(solution)/shard_map/all_to_all | solution.py:482
  22.3 1.5 collective-permute-start.1
  23.8 9.9 %collective-permute-done.1 = bf16[1,32,128]{2,1,0:T(8,128)(2,1)S(1)} collective-permute-done((bf16[1,32,128]{2,1,0:T(8,128)(2,1)S(1)}, bf16[1,32,128]{2,1,0:T(8,128)(2,1)S(1)}, u32[]{:S(2)}, u32[]{:S(2)}) %collective-permute-start.1) | collective-permute-done | bytes 8224 | tf_op jit(solution)/shard_map/ppermute | solution.py:557
  33.6 2.8 %collective-permute-start.2 = (bf16[2,32,128]{2,1,0:T(8,128)(2,1)S(1)}, bf16[2,32,128]{2,1,0:T(8,128)(2,1)S(1)}, u32[]{:S(2)}, u32[]{:S(2)}) collective-permute-start(bf16[2,32,128]{2,1,0:T(8,128)(2,1)S(1)} %pad_maximum_fusion.4), channel_id=1, source_target_pairs={{0,4},{1,5},{2,6},{3,7},{4,0},{5,1},{6,2},{7,3},{8,12},{9,13},{10,... | collective-permute-start | bytes 49160 | tf_op jit(solution)/shard_map/ppermute | solution.py:557
  37.8 1.7 %collective-permute-done.2 = bf16[2,32,128]{2,1,0:T(8,128)(2,1)S(1)} collective-permute-done((bf16[2,32,128]{2,1,0:T(8,128)(2,1)S(1)}, bf16[2,32,128]{2,1,0:T(8,128)(2,1)S(1)}, u32[]{:S(2)}, u32[]{:S(2)}) %collective-permute-start.2) | collective-permute-done | bytes 16416 | tf_op jit(solution)/shard_map/ppermute | solution.py:557
  39.4 3.4 %collective-permute-start.3 = (bf16[4,32,128]{2,1,0:T(8,128)(2,1)S(1)}, bf16[4,32,128]{2,1,0:T(8,128)(2,1)S(1)}, u32[]{:S(2)}, u32[]{:S(2)}) collective-permute-start(bf16[4,32,128]{2,1,0:T(8,128)(2,1)S(1)} %pad_maximum_fusion.2.first), channel_id=1, source_target_pairs={{0,8},{1,9},{2,10},{3,11},{4,12},{5,13},{6,14},{7,15},{8,0},{9,1},... | collective-permute-start | bytes 98312 | tf_op jit(solution)/shard_map/ppermute | solution.py:557
  42.9 2.8 %copy-done = bf16[16,3,256,256]{3,2,1,0:T(8,128)(2,1)S(1)} copy-done((bf16[16,3,256,256]{3,2,1,0:T(8,128)(2,1)S(1)}, bf16[16,3,256,256]{3,2,1,0:T(8,128)(2,1)}, u32[]{:S(2)}) %copy-start) | copy-done | bytes 6291480
  46.9 3.0 %near_field.2.rest_0_.near = bf16[16,256,128]{2,1,0:T(8,128)(2,1)S(1)} custom-call(s32[32]{0:T(128)S(1)} %reshape.35.ids, bf16[16,256,128]{2,1,0:T(8,128)(2,1)S(1)} %copy-done.9, bf16[16,3,256,256]{3,2,1,0:T(8,128)(2,1)S(1)} %copy-done), custom_call_target="tpu_custom_call" | custom-call | flops 805306368 | bytes 6291456 | tf_op jit(solution)/shard_map/near_field/pallas_call | solution.py:494
  50.1 1.7 %copy-done.5 = f32[4096,128]{1,0:T(8,128)S(1)} copy-done((f32[4096,128]{1,0:T(8,128)S(1)}, f32[4096,128]{1,0:T(8,128)}, u32[]{:S(2)}) %copy-start.5) | copy-done | bytes 2097176
  54.4 3.9 %collective-permute-done.3.second = bf16[4,32,128]{2,1,0:T(8,128)(2,1)S(1)} collective-permute-done((bf16[4,32,128]{2,1,0:T(8,128)(2,1)S(1)}, bf16[4,32,128]{2,1,0:T(8,128)(2,1)S(1)}, u32[]{:S(2)}, u32[]{:S(2)}) %collective-permute-start.3) | collective-permute-done | bytes 32800 | tf_op jit(solution)/shard_map/ppermute | solution.py:557
  59.3 3.8 %collective-permute-start.7 = (bf16[2,256,128]{2,1,0:T(8,128)(2,1)S(1)}, bf16[2,256,128]{2,1,0:T(8,128)(2,1)S(1)}, u32[]{:S(2)}, u32[]{:S(2)}) collective-permute-start(bf16[2,256,128]{2,1,0:T(8,128)(2,1)S(1)} %get-tuple-element.26), channel_id=1, source_target_pairs={{1,0},{2,1},{3,2},{4,3},{5,4},{6,5},{7,6},{8,7},{9,8},{10,9},{11,1... | collective-permute-start | bytes 393224 | tf_op jit(solution)/shard_map/ppermute | solution.py:490
  63.1 1.9 %collective-permute-start.6 = (bf16[2,256,128]{2,1,0:T(8,128)(2,1)S(1)}, bf16[2,256,128]{2,1,0:T(8,128)(2,1)S(1)}, u32[]{:S(2)}, u32[]{:S(2)}) collective-permute-start(bf16[2,256,128]{2,1,0:T(8,128)(2,1)S(1)} %get-tuple-element.27), channel_id=1, source_target_pairs={{0,1},{1,2},{2,3},{3,4},{4,5},{5,6},{6,7},{7,8},{8,9},{9,10},{10,1... | collective-permute-start | bytes 393224 | tf_op jit(solution)/shard_map/ppermute | solution.py:489
  65.0 4.6 %collective-permute-done.4 = bf16[8,32,128]{2,1,0:T(8,128)(2,1)S(1)} collective-permute-done((bf16[8,32,128]{2,1,0:T(8,128)(2,1)S(1)}, bf16[8,32,128]{2,1,0:T(8,128)(2,1)S(1)}, u32[]{:S(2)}, u32[]{:S(2)}) %collective-permute-start.4) | collective-permute-done | bytes 65568 | tf_op jit(solution)/shard_map/ppermute | solution.py:557
  71.1 3.1 %collective-permute-done.6.before = bf16[2,256,128]{2,1,0:T(8,128)(2,1)S(1)} collective-permute-done((bf16[2,256,128]{2,1,0:T(8,128)(2,1)S(1)}, bf16[2,256,128]{2,1,0:T(8,128)(2,1)S(1)}, u32[]{:S(2)}, u32[]{:S(2)}) %collective-permute-start.6) | collective-permute-done | bytes 131104 | tf_op jit(solution)/shard_map/ppermute | solution.py:489
  74.8 11.3 %first_scores.1 = (bf16[128,64,128]{2,1,0:T(8,128)(2,1)}, bf16[16,256,128]{2,1,0:T(8,128)(2,1)}, f32[64,128]{1,0:T(8,128)S(1)}) custom-call(s32[409]{0:T(512)S(1)} %concatenate.23.rest_2_.table, bf16[128,64,128]{2,1,0:T(8,128)(2,1)} %all-to-all-done.1.incoming, bf16[31,64,256]{2,1,0:T(8,128)(2,1)} %couplings.3, bf16[31,64,64]{2,1,0:T(8,128)(2,1)} %transfer.5, ...), custom_call_target="tpu_custom_call" | custom-call | flops 130023424 | bytes 6291456 | tf_op jit(solution)/shard_map/first_scores/pallas_call | solution.py:600
  86.1 3.5 %all-to-all-start.2 = ((bf16[128,64,128]{2,1,0:T(8,128)(2,1)}), bf16[128,64,128]{2,1,0:T(8,128)(2,1)}, u32[]{:S(2)}, u32[]{:S(2)}) async-start(bf16[128,64,128]{2,1,0:T(8,128)(2,1)} %get-tuple-element.17), calls=%async_computation.2 | async-start | bytes 4194304 | tf_op jit(solution)/shard_map/all_to_all | solution.py:482
  92.3 9.9 %collective-permute-done.9 = bf16[1,32,128]{2,1,0:T(8,128)(2,1)S(1)} collective-permute-done((bf16[1,32,128]{2,1,0:T(8,128)(2,1)S(1)}, bf16[1,32,128]{2,1,0:T(8,128)(2,1)S(1)}, u32[]{:S(2)}, u32[]{:S(2)}) %collective-permute-start.9) | collective-permute-done | bytes 8224 | tf_op jit(solution)/shard_map/ppermute | solution.py:557
  102.2 2.7 %collective-permute-start.10 = (bf16[2,32,128]{2,1,0:T(8,128)(2,1)S(1)}, bf16[2,32,128]{2,1,0:T(8,128)(2,1)S(1)}, u32[]{:S(2)}, u32[]{:S(2)}) collective-permute-start(bf16[2,32,128]{2,1,0:T(8,128)(2,1)S(1)} %pad_maximum_fusion.5), channel_id=1, source_target_pairs={{0,4},{1,5},{2,6},{3,7},{4,0},{5,1},{6,2},{7,3},{8,12},{9,13},{10,... | collective-permute-start | bytes 49160 | tf_op jit(solution)/shard_map/ppermute | solution.py:557
  106.8 4.7 %collective-permute-start.11 = (bf16[4,32,128]{2,1,0:T(8,128)(2,1)S(1)}, bf16[4,32,128]{2,1,0:T(8,128)(2,1)S(1)}, u32[]{:S(2)}, u32[]{:S(2)}) collective-permute-start(bf16[4,32,128]{2,1,0:T(8,128)(2,1)S(1)} %pad_maximum_fusion.3.first), channel_id=1, source_target_pairs={{0,8},{1,9},{2,10},{3,11},{4,12},{5,13},{6,14},{7,15},{8,0},{9,1},... | collective-permute-start | bytes 98312 | tf_op jit(solution)/shard_map/ppermute | solution.py:557
  111.5 2.8 %copy-done.1 = bf16[16,3,256,256]{3,2,1,0:T(8,128)(2,1)S(1)} copy-done((bf16[16,3,256,256]{3,2,1,0:T(8,128)(2,1)S(1)}, bf16[16,3,256,256]{3,2,1,0:T(8,128)(2,1)}, u32[]{:S(2)}) %copy-start.1) | copy-done | bytes 6291480
  114.3 3.0 %near_field.3.rest_0_.near = bf16[16,256,128]{2,1,0:T(8,128)(2,1)S(1)} custom-call(s32[32]{0:T(128)S(1)} %reshape.35.ids, bf16[16,256,128]{2,1,0:T(8,128)(2,1)S(1)} %get-tuple-element.20.own, bf16[16,3,256,256]{3,2,1,0:T(8,128)(2,1)S(1)} %copy-done.1), custom_call_target="tpu_custom_call" | custom-call | flops 805306368 | bytes 6291456 | tf_op jit(solution)/shard_map/near_field/pallas_call | solution.py:494
  117.3 9.5 %collective-permute-done.11.second = bf16[4,32,128]{2,1,0:T(8,128)(2,1)S(1)} collective-permute-done((bf16[4,32,128]{2,1,0:T(8,128)(2,1)S(1)}, bf16[4,32,128]{2,1,0:T(8,128)(2,1)S(1)}, u32[]{:S(2)}, u32[]{:S(2)}) %collective-permute-start.11) | collective-permute-done | bytes 32800 | tf_op jit(solution)/shard_map/ppermute | solution.py:557
  126.9 3.7 %collective-permute-start.15 = (bf16[2,256,128]{2,1,0:T(8,128)(2,1)S(1)}, bf16[2,256,128]{2,1,0:T(8,128)(2,1)S(1)}, u32[]{:S(2)}, u32[]{:S(2)}) collective-permute-start(bf16[2,256,128]{2,1,0:T(8,128)(2,1)S(1)} %get-tuple-element.24), channel_id=1, source_target_pairs={{1,0},{2,1},{3,2},{4,3},{5,4},{6,5},{7,6},{8,7},{9,8},{10,9},{11,1... | collective-permute-start | bytes 393224 | tf_op jit(solution)/shard_map/ppermute | solution.py:490
  130.6 1.9 %collective-permute-start.14 = (bf16[2,256,128]{2,1,0:T(8,128)(2,1)S(1)}, bf16[2,256,128]{2,1,0:T(8,128)(2,1)S(1)}, u32[]{:S(2)}, u32[]{:S(2)}) collective-permute-start(bf16[2,256,128]{2,1,0:T(8,128)(2,1)S(1)} %get-tuple-element.25), channel_id=1, source_target_pairs={{0,1},{1,2},{2,3},{3,4},{4,5},{5,6},{6,7},{7,8},{8,9},{9,10},{10,1... | collective-permute-start | bytes 393224 | tf_op jit(solution)/shard_map/ppermute | solution.py:489
  132.6 5.6 %collective-permute-done.12 = bf16[8,32,128]{2,1,0:T(8,128)(2,1)S(1)} collective-permute-done((bf16[8,32,128]{2,1,0:T(8,128)(2,1)S(1)}, bf16[8,32,128]{2,1,0:T(8,128)(2,1)S(1)}, u32[]{:S(2)}, u32[]{:S(2)}) %collective-permute-start.12) | collective-permute-done | bytes 65568 | tf_op jit(solution)/shard_map/ppermute | solution.py:557
  139.5 3.2 %collective-permute-done.14.before = bf16[2,256,128]{2,1,0:T(8,128)(2,1)S(1)} collective-permute-done((bf16[2,256,128]{2,1,0:T(8,128)(2,1)S(1)}, bf16[2,256,128]{2,1,0:T(8,128)(2,1)S(1)}, u32[]{:S(2)}, u32[]{:S(2)}) %collective-permute-start.14) | collective-permute-done | bytes 131104 | tf_op jit(solution)/shard_map/ppermute | solution.py:489
  143.4 7.1 %last_scores.1 = (f32[16,256,128]{2,1,0:T(8,128)}, f32[16,256,128]{2,1,0:T(8,128)}) custom-call(s32[409]{0:T(512)S(1)} %concatenate.23.rest_2_.table, bf16[128,64,128]{2,1,0:T(8,128)(2,1)} %all-to-all-done.2.incoming, bf16[31,64,256]{2,1,0:T(8,128)(2,1)} %couplings.3, bf16[31,64,64]{2,1,0:T(8,128)(2,1)} %transfer.5, ...), custom_call_target="tpu_custom_call" | custom-call | flops 130023424 | bytes 6291456 | tf_op jit(solution)/shard_map/last_scores/pallas_call | solution.py:600
  (77 shorter events, 16.3 us)
Async XLA Ops:
  2.2 10.9 %all-to-all-start = ((s32[32,1,4]{2,1,0:T(1,128)}), s32[32,1,4]{2,1,0:T(1,128)S(1)}, u32[]{:S(2)}, u32[]{:S(2)}) async-start(s32[32,1,4]{2,1,0:T(1,128)} %get-tuple-element.14), calls=%async_computation | async-start | bytes 32768 | tf_op jit(solution)/shard_map/all_to_all | solution.py:412
  15.4 21.0 %copy-start.17 = (s32[16,2]{0,1:T(2,128)S(1)}, s32[16,2]{0,1:T(2,128)}, u32[]{:S(2)}) copy-start(s32[16,2]{0,1:T(2,128)} %param.15) | copy-start | bytes 388
  15.4 21.0 %copy-start.4 = (f32[4096,128]{1,0:T(8,128)S(1)}, f32[4096,128]{1,0:T(8,128)}, u32[]{:S(2)}) copy-start(f32[4096,128]{1,0:T(8,128)} %param.11) | copy-start | bytes 6291460
  15.4 58.7 %all-to-all-start.1 = ((bf16[128,64,128]{2,1,0:T(8,128)(2,1)}), bf16[128,64,128]{2,1,0:T(8,128)(2,1)}, u32[]{:S(2)}, u32[]{:S(2)}) async-start(bf16[128,64,128]{2,1,0:T(8,128)(2,1)} %pick_rows.1), calls=%async_computation.1 | async-start | bytes 4194304 | tf_op jit(solution)/shard_map/all_to_all | solution.py:482
  21.0 1.2 collective-permute-start
  22.3 11.3 %collective-permute-start.1 = (bf16[1,32,128]{2,1,0:T(8,128)(2,1)S(1)}, bf16[1,32,128]{2,1,0:T(8,128)(2,1)S(1)}, u32[]{:S(2)}, u32[]{:S(2)}) collective-permute-start(bf16[1,32,128]{2,1,0:T(8,128)(2,1)S(1)} %fusion), channel_id=1, source_target_pairs={{0,2},{1,3},{2,0},{3,1},{4,6},{5,7},{6,4},{7,5},{8,10},{9,11},{10,... | collective-permute-start | bytes 24584 | tf_op jit(solution)/shard_map/ppermute | solution.py:557
  33.6 5.8 %collective-permute-start.2 = (bf16[2,32,128]{2,1,0:T(8,128)(2,1)S(1)}, bf16[2,32,128]{2,1,0:T(8,128)(2,1)S(1)}, u32[]{:S(2)}, u32[]{:S(2)}) collective-permute-start(bf16[2,32,128]{2,1,0:T(8,128)(2,1)S(1)} %pad_maximum_fusion.4), channel_id=1, source_target_pairs={{0,4},{1,5},{2,6},{3,7},{4,0},{5,1},{6,2},{7,3},{8,12},{9,13},{10,... | collective-permute-start | bytes 49160 | tf_op jit(solution)/shard_map/ppermute | solution.py:557
  39.4 18.8 %collective-permute-start.3 = (bf16[4,32,128]{2,1,0:T(8,128)(2,1)S(1)}, bf16[4,32,128]{2,1,0:T(8,128)(2,1)S(1)}, u32[]{:S(2)}, u32[]{:S(2)}) collective-permute-start(bf16[4,32,128]{2,1,0:T(8,128)(2,1)S(1)} %pad_maximum_fusion.2.first), channel_id=1, source_target_pairs={{0,8},{1,9},{2,10},{3,11},{4,12},{5,13},{6,14},{7,15},{8,0},{9,1},... | collective-permute-start | bytes 98312 | tf_op jit(solution)/shard_map/ppermute | solution.py:557
  42.9 2.8 %copy-start = (bf16[16,3,256,256]{3,2,1,0:T(8,128)(2,1)S(1)}, bf16[16,3,256,256]{3,2,1,0:T(8,128)(2,1)}, u32[]{:S(2)}) copy-start(bf16[16,3,256,256]{3,2,1,0:T(8,128)(2,1)} %tiles.7) | copy-start | bytes 18874372
  46.9 3.0 %copy-start.16 = (s32[30,4]{0,1:T(4,128)S(1)}, s32[30,4]{0,1:T(4,128)}, u32[]{:S(2)}) copy-start(s32[30,4]{0,1:T(4,128)} %param.21) | copy-start | bytes 1444
  46.9 3.2 %copy-start.11 = (s32[4096]{0:T(1024)S(1)}, s32[4096]{0:T(1024)}, u32[]{:S(2)}) copy-start(s32[4096]{0:T(1024)} %param.12) | copy-start | bytes 49156
  49.9 8.4 %copy-start.6 = (bf16[16,256,128]{2,1,0:T(8,128)(2,1)}, bf16[16,256,128]{2,1,0:T(8,128)(2,1)S(1)}, u32[]{:S(2)}) copy-start(bf16[16,256,128]{2,1,0:T(8,128)(2,1)S(1)} %near_field.2.rest_0_.near) | copy-start | bytes 3145732
  52.9 21.2 %copy-start.2 = (f32[16,256,128]{2,1,0:T(8,128)}, f32[16,256,128]{2,1,0:T(8,128)S(1)}, u32[]{:S(2)}) copy-start(f32[16,256,128]{2,1,0:T(8,128)S(1)} %with_labels.1.rest_1_.base.old) | copy-start | bytes 6291460
  58.2 11.4 %collective-permute-start.4 = (bf16[8,32,128]{2,1,0:T(8,128)(2,1)S(1)}, bf16[8,32,128]{2,1,0:T(8,128)(2,1)S(1)}, u32[]{:S(2)}, u32[]{:S(2)}) collective-permute-start(bf16[8,32,128]{2,1,0:T(8,128)(2,1)S(1)} %join_rows.2), channel_id=1, source_target_pairs={{0,16},{1,17},{2,18},{3,19},{4,20},{5,21},{6,22},{7,23},{8,24},{9,... | collective-permute-start | bytes 196616 | tf_op jit(solution)/shard_map/ppermute | solution.py:557
  59.3 11.8 %collective-permute-start.7 = (bf16[2,256,128]{2,1,0:T(8,128)(2,1)S(1)}, bf16[2,256,128]{2,1,0:T(8,128)(2,1)S(1)}, u32[]{:S(2)}, u32[]{:S(2)}) collective-permute-start(bf16[2,256,128]{2,1,0:T(8,128)(2,1)S(1)} %get-tuple-element.26), channel_id=1, source_target_pairs={{1,0},{2,1},{3,2},{4,3},{5,4},{6,5},{7,6},{8,7},{9,8},{10,9},{11,1... | collective-permute-start | bytes 393224 | tf_op jit(solution)/shard_map/ppermute | solution.py:490
  63.1 11.0 %collective-permute-start.6 = (bf16[2,256,128]{2,1,0:T(8,128)(2,1)S(1)}, bf16[2,256,128]{2,1,0:T(8,128)(2,1)S(1)}, u32[]{:S(2)}, u32[]{:S(2)}) collective-permute-start(bf16[2,256,128]{2,1,0:T(8,128)(2,1)S(1)} %get-tuple-element.27), channel_id=1, source_target_pairs={{0,1},{1,2},{2,3},{3,4},{4,5},{5,6},{6,7},{7,8},{8,9},{9,10},{10,1... | collective-permute-start | bytes 393224 | tf_op jit(solution)/shard_map/ppermute | solution.py:489
  69.7 4.5 %collective-permute-start.5 = (bf16[16,32,128]{2,1,0:T(8,128)(2,1)S(1)}, bf16[16,32,128]{2,1,0:T(8,128)(2,1)S(1)}, u32[]{:S(2)}, u32[]{:S(2)}) collective-permute-start(bf16[16,32,128]{2,1,0:T(8,128)(2,1)S(1)} %pad_maximum_fusion.half), channel_id=1, source_target_pairs={{0,1},{1,0},{2,3},{3,2},{4,5},{5,4},{6,7},{7,6},{8,9},{9,8},{10,11... | collective-permute-start | bytes 393224 | tf_op jit(solution)/shard_map/ppermute | solution.py:564
  71.1 3.1 %copy-start.13 = (bf16[2,256,128]{2,1,0:T(8,128)(2,1)}, bf16[2,256,128]{2,1,0:T(8,128)(2,1)S(1)}, u32[]{:S(2)}) copy-start(bf16[2,256,128]{2,1,0:T(8,128)(2,1)S(1)} %collective-permute-done.7.after) | copy-start | bytes 393220
  86.1 18.8 %copy-start.3 = (f32[16,256,128]{2,1,0:T(8,128)S(1)}, f32[16,256,128]{2,1,0:T(8,128)}, u32[]{:S(2)}) copy-start(f32[16,256,128]{2,1,0:T(8,128)} %copy-done.2) | copy-start | bytes 6291460
  86.1 18.8 %copy-start.10 = (bf16[16,256,128]{2,1,0:T(8,128)(2,1)S(1)}, bf16[16,256,128]{2,1,0:T(8,128)(2,1)}, u32[]{:S(2)}) copy-start(bf16[16,256,128]{2,1,0:T(8,128)(2,1)} %get-tuple-element.19.grads) | copy-start | bytes 3145732
  86.1 56.6 %all-to-all-start.2 = ((bf16[128,64,128]{2,1,0:T(8,128)(2,1)}), bf16[128,64,128]{2,1,0:T(8,128)(2,1)}, u32[]{:S(2)}, u32[]{:S(2)}) async-start(bf16[128,64,128]{2,1,0:T(8,128)(2,1)} %get-tuple-element.17), calls=%async_computation.2 | async-start | bytes 4194304 | tf_op jit(solution)/shard_map/all_to_all | solution.py:482
  89.7 1.2 collective-permute-start.8
  90.9 11.3 %collective-permute-start.9 = (bf16[1,32,128]{2,1,0:T(8,128)(2,1)S(1)}, bf16[1,32,128]{2,1,0:T(8,128)(2,1)S(1)}, u32[]{:S(2)}, u32[]{:S(2)}) collective-permute-start(bf16[1,32,128]{2,1,0:T(8,128)(2,1)S(1)} %fusion.1), channel_id=1, source_target_pairs={{0,2},{1,3},{2,0},{3,1},{4,6},{5,7},{6,4},{7,5},{8,10},{9,11},{10,... | collective-permute-start | bytes 24584 | tf_op jit(solution)/shard_map/ppermute | solution.py:557
  102.2 4.5 %collective-permute-start.10 = (bf16[2,32,128]{2,1,0:T(8,128)(2,1)S(1)}, bf16[2,32,128]{2,1,0:T(8,128)(2,1)S(1)}, u32[]{:S(2)}, u32[]{:S(2)}) collective-permute-start(bf16[2,32,128]{2,1,0:T(8,128)(2,1)S(1)} %pad_maximum_fusion.5), channel_id=1, source_target_pairs={{0,4},{1,5},{2,6},{3,7},{4,0},{5,1},{6,2},{7,3},{8,12},{9,13},{10,... | collective-permute-start | bytes 49160 | tf_op jit(solution)/shard_map/ppermute | solution.py:557
  106.0 20.8 %copy-start.8 = (f32[16,256,128]{2,1,0:T(8,128)}, f32[16,256,128]{2,1,0:T(8,128)S(1)}, u32[]{:S(2)}) copy-start(f32[16,256,128]{2,1,0:T(8,128)S(1)} %get-tuple-element.21.rest_1_.base) | copy-start | bytes 6291460
  106.8 20.0 %collective-permute-start.11 = (bf16[4,32,128]{2,1,0:T(8,128)(2,1)S(1)}, bf16[4,32,128]{2,1,0:T(8,128)(2,1)S(1)}, u32[]{:S(2)}, u32[]{:S(2)}) collective-permute-start(bf16[4,32,128]{2,1,0:T(8,128)(2,1)S(1)} %pad_maximum_fusion.3.first), channel_id=1, source_target_pairs={{0,8},{1,9},{2,10},{3,11},{4,12},{5,13},{6,14},{7,15},{8,0},{9,1},... | collective-permute-start | bytes 98312 | tf_op jit(solution)/shard_map/ppermute | solution.py:557
  117.2 25.5 %copy-start.7 = (bf16[16,256,128]{2,1,0:T(8,128)(2,1)}, bf16[16,256,128]{2,1,0:T(8,128)(2,1)S(1)}, u32[]{:S(2)}) copy-start(bf16[16,256,128]{2,1,0:T(8,128)(2,1)S(1)} %near_field.3.rest_0_.near) | copy-start | bytes 3145732
  126.8 11.3 %collective-permute-start.12 = (bf16[8,32,128]{2,1,0:T(8,128)(2,1)S(1)}, bf16[8,32,128]{2,1,0:T(8,128)(2,1)S(1)}, u32[]{:S(2)}, u32[]{:S(2)}) collective-permute-start(bf16[8,32,128]{2,1,0:T(8,128)(2,1)S(1)} %join_rows.3), channel_id=1, source_target_pairs={{0,16},{1,17},{2,18},{3,19},{4,20},{5,21},{6,22},{7,23},{8,24},{9,... | collective-permute-start | bytes 196616 | tf_op jit(solution)/shard_map/ppermute | solution.py:557
  126.9 12.6 %collective-permute-start.15 = (bf16[2,256,128]{2,1,0:T(8,128)(2,1)S(1)}, bf16[2,256,128]{2,1,0:T(8,128)(2,1)S(1)}, u32[]{:S(2)}, u32[]{:S(2)}) collective-permute-start(bf16[2,256,128]{2,1,0:T(8,128)(2,1)S(1)} %get-tuple-element.24), channel_id=1, source_target_pairs={{1,0},{2,1},{3,2},{4,3},{5,4},{6,5},{7,6},{8,7},{9,8},{10,9},{11,1... | collective-permute-start | bytes 393224 | tf_op jit(solution)/shard_map/ppermute | solution.py:490
  130.6 12.1 %collective-permute-start.14 = (bf16[2,256,128]{2,1,0:T(8,128)(2,1)S(1)}, bf16[2,256,128]{2,1,0:T(8,128)(2,1)S(1)}, u32[]{:S(2)}, u32[]{:S(2)}) collective-permute-start(bf16[2,256,128]{2,1,0:T(8,128)(2,1)S(1)} %get-tuple-element.25), channel_id=1, source_target_pairs={{0,1},{1,2},{2,3},{3,4},{4,5},{5,6},{6,7},{7,8},{8,9},{9,10},{10,1... | collective-permute-start | bytes 393224 | tf_op jit(solution)/shard_map/ppermute | solution.py:489
  138.1 4.6 %collective-permute-start.13 = (bf16[16,32,128]{2,1,0:T(8,128)(2,1)S(1)}, bf16[16,32,128]{2,1,0:T(8,128)(2,1)S(1)}, u32[]{:S(2)}, u32[]{:S(2)}) collective-permute-start(bf16[16,32,128]{2,1,0:T(8,128)(2,1)S(1)} %pad_maximum_fusion.1.half), channel_id=1, source_target_pairs={{0,1},{1,0},{2,3},{3,2},{4,5},{5,4},{6,7},{7,6},{8,9},{9,8},{10,11... | collective-permute-start | bytes 393224 | tf_op jit(solution)/shard_map/ppermute | solution.py:564
  139.5 3.2 %copy-start.12 = (bf16[2,256,128]{2,1,0:T(8,128)(2,1)}, bf16[2,256,128]{2,1,0:T(8,128)(2,1)S(1)}, u32[]{:S(2)}) copy-start(bf16[2,256,128]{2,1,0:T(8,128)(2,1)S(1)} %collective-permute-done.15.after) | copy-start | bytes 393220
  (6 other events, 9.5 us)
